TPU v7x, 32 devices: a whole 2x2x4 slice. The times are simulated.
32 devices in a mesh: dp: 8 (over z, y), fsdp: 4 (over x, core).
Axes of the slice: x: 2, y: 2, z: 4, core: 2. Of those that a mesh axis runs over, the one named last changes fastest.
Arguments:
- queries: bfloat16 [12288, 2048], P(('dp', 'fsdp')), may hold values from -16 to 16
- passages: bfloat16 [12288, 2048], P(('dp', 'fsdp')), may hold values from -16 to 16
- weight: bfloat16 [2048, 2048], P('fsdp'), may hold values from -0.125 to 0.125
- bank: bfloat16 [256, 128, 2048], P(('dp', 'fsdp')), may hold values from -6 to 6
- neg_ids: int32 [32, 16], P(('dp', 'fsdp')), may hold values from 0 to 255, as said below
- block_home: int32 [256], replicated, may hold values from 0 to 255, as said below
Outputs:
- loss: float32 [], replicated
- grad_weight: float32 [2048, 2048], P(('dp', 'fsdp'))
- grad_queries: bfloat16 [12288, 2048], P(('dp', 'fsdp'))
- grad_passages: bfloat16 [12288, 2048], P(('dp', 'fsdp'))
Inputs may be any that keep to these rules, and one draw needn't show every extreme that they name: `block_home`: A permutation of the slots; block b is held on a device whose fsdp index is b % 4. `neg_ids`: A group's 16 blocks are distinct and all held on devices of the group's own fsdp index; at most 2 of them on one device, and in every group some device holds exactly 2; in each fsdp index one device holds 2 of every group's blocks.
All inputs are finite; a program needn't handle non-finite values.
Results may differ from a plain program's by a relative error of at most 0.012.
The roundings to bfloat16 on the way count: a program that leaves them out, or rounds other values in their place, can miss the bound.
Values may be sent and summed in bfloat16 or wider, within the bound.
No kernel may reach another device: no remote copies, remote signals or barrier semaphores. Data moves between devices by JAX's collectives and lax.ppermute only.
A program may use at most 128 MiB of HBM per device.

v0:
```python
import math

import jax
import jax.numpy as jnp
from jax import lax
from jax.sharding import PartitionSpec as P

CAP = 2


SOFTMAX_TEMPER = 0.25


def body(queries, passages, weight, bank, neg_ids, block_home):
    count_q = queries.shape[0]
    slice_width = weight.shape[1]
    logit_scale = 1.0 / (SOFTMAX_TEMPER * math.sqrt(slice_width))
    full_weight = lax.all_gather(weight, "fsdp", axis=0, tiled=True)
    hidden = jnp.concatenate([queries, passages], axis=0)
    embedded = jnp.dot(hidden, full_weight, preferred_element_type=jnp.float32).astype(jnp.bfloat16)
    emb_q = embedded[:count_q]
    emb_p = embedded[count_q:]
    n_dp = lax.axis_size("dp")
    n_fsdp = lax.axis_size("fsdp")
    per_dev = bank.shape[0]
    block_rows = bank.shape[1]
    named = neg_ids.shape[1]
    slots = block_home[neg_ids[0]]
    owner = slots // per_dev // n_fsdp
    local = slots % per_dev
    order = jnp.arange(named)
    earlier = (owner[None, :] == owner[:, None]) & (order[None, :] < order[:, None])
    rank = jnp.sum(earlier.astype(jnp.int32), axis=1)
    peers = jnp.arange(n_dp)
    places = jnp.arange(CAP)
    hit = (owner[:, None, None] == peers[None, :, None]) & (
        rank[:, None, None] == places[None, None, :]
    )
    request = jnp.sum(jnp.where(hit, local[:, None, None] + 1, 0), axis=0) - 1
    asked = lax.all_to_all(request, "dp", split_axis=0, concat_axis=0, tiled=True)
    valid = asked >= 0
    picked = jnp.take(bank, jnp.clip(asked, 0, per_dev - 1), axis=0)
    picked = jnp.where(valid[:, :, None, None], picked, jnp.zeros_like(picked))
    replies = lax.all_to_all(picked, "dp", split_axis=0, concat_axis=0, tiled=True)
    replies = replies.reshape(n_dp * CAP, block_rows, slice_width)
    negs = jnp.take(replies, owner * CAP + rank, axis=0).reshape(named * block_rows, slice_width)
    inner = jnp.dot(emb_q, emb_p.T, preferred_element_type=jnp.float32) * logit_scale
    outer = jnp.dot(emb_q, negs.T, preferred_element_type=jnp.float32) * logit_scale
    scores = jnp.concatenate([inner, outer], axis=1)
    top = jnp.max(scores, axis=1, keepdims=True)
    expo = jnp.exp(scores - top)
    total = jnp.sum(expo, axis=1, keepdims=True)
    lse = top[:, 0] + jnp.log(total[:, 0])
    loss_local = jnp.sum(lse - jnp.diagonal(inner))
    target = jnp.concatenate(
        [
            jnp.eye(count_q, dtype=jnp.float32),
            jnp.zeros((count_q, named * block_rows), jnp.float32),
        ],
        axis=1,
    )
    grad_s = ((expo / total - target) * logit_scale).astype(jnp.bfloat16)
    grad_in = grad_s[:, :count_q]
    grad_out = grad_s[:, count_q:]
    query_gradient = (
        jnp.dot(grad_in, emb_p, preferred_element_type=jnp.float32)
        + jnp.dot(grad_out, negs, preferred_element_type=jnp.float32)
    ).astype(jnp.bfloat16)
    grad_p = lax.dot_general(
        grad_in, emb_q, (((0,), (0,)), ((), ())), preferred_element_type=jnp.float32
    ).astype(jnp.bfloat16)
    grad_rows = jnp.concatenate([query_gradient, grad_p], axis=0)
    back = lax.dot_general(
        grad_rows, full_weight, (((1,), (1,)), ((), ())), preferred_element_type=jnp.float32
    ).astype(jnp.bfloat16)
    devices_all = n_dp * n_fsdp
    loss = lax.psum(loss_local, ("dp", "fsdp")) / (count_q * devices_all)
    grad_weight = lax.psum_scatter(
        lax.dot_general(
            hidden, grad_rows, (((0,), (0,)), ((), ())), preferred_element_type=jnp.float32
        ),
        ("dp", "fsdp"),
        scatter_dimension=0,
        tiled=True,
    )
    return (loss, grad_weight, back[:count_q], back[count_q:])


def solution(mesh):
    return jax.shard_map(
        body,
        mesh=mesh,
        in_specs=(
            P(("dp", "fsdp"), None),
            P(("dp", "fsdp"), None),
            P("fsdp", None),
            P(("dp", "fsdp"), None, None),
            P(("dp", "fsdp"), None),
            P(),
        ),
        out_specs=(P(), P(("dp", "fsdp"), None), P(("dp", "fsdp"), None), P(("dp", "fsdp"), None)),
        check_vma=False,
    )
```

profile of v0, /device:TPU:0, one launch (start us, length us, event | category | flops | bytes accessed | tf_op | source)
XLA Modules:
  0.0 461.8 jit_solution(14970008667367733022)
XLA Ops:
  7.2 0.0 copy-start
  7.2 0.7 fusion.18
  7.9 0.0 copy-done
  7.9 0.7 gather_fusion
  8.5 0.2 convert_reduce_fusion
  8.8 0.1 select_reduce_fusion
  8.9 0.7 copy.34
  9.6 7.3 %all-to-all-start = ((s32[8,1,2]{2,1,0:T(1,128)}), s32[8,1,2]{2,1,0:T(1,128)S(1)}, u32[]{:S(2)}, u32[]{:S(2)}) async-start(s32[8,1,2]{2,1,0:T(1,128)} %copy.34), calls=%async_computation | async-start | bytes 8192 | tf_op jit(solution)/shard_map/all_to_all | solution.py:40
  16.9 0.0 all-gather.2.cloned.1.call-start
  16.9 0.7 all-gather.2.cloned.1.call-update
  17.6 5.7 %all-to-all-done = s32[8,1,2]{2,1,0:T(1,128)S(1)} async-done(((s32[8,1,2]{2,1,0:T(1,128)}), s32[8,1,2]{2,1,0:T(1,128)S(1)}, u32[]{:S(2)}, u32[]{:S(2)}) %all-to-all-start) | async-done | bytes 96 | tf_op jit(solution)/shard_map/all_to_all | solution.py:40
  23.3 0.1 copy.35
  23.4 0.1 copy.39
  23.5 0.1 reshape.353
  23.5 0.1 copy.36
  23.6 0.1 copy.38
  23.7 7.7 %gather_fusion.1 = bf16[16,128,2048]{2,1,0:T(8,128)(2,1)} fusion(bf16[8,128,2048]{2,1,0:T(8,128)(2,1)} %param.9, s32[1024]{0:T(1024)S(1)} %pad_clamp_fusion.1), kind=kCustom, calls=%fused_computation.1 | custom fusion | bytes 16777280 | tf_op jit(solution)/shard_map/jit(_take)/gather | solution.py:42
  31.5 8.4 %select_select_fusion = bf16[8,2,128,2048]{3,2,1,0:T(8,128)(2,1)} fusion(bf16[8,2,128,2048]{3,2,1,0:T(8,128)(2,1)} %bitcast.42, pred[8,2]{1,0:T(8,128)(4,1)S(1)} %copy.38, pred[8,2]{1,0:T(8,128)(4,1)S(1)} %copy.36), kind=kLoop, calls=%fused_computation.5 | loop fusion | flops 8388608 | bytes 16777248 | tf_op jit(solution)/shard_map/jit(_where)/select_n | solution.py:43
  39.9 0.0 copy-start.3
  39.9 5.1 %all-to-all-start.1 = ((bf16[8,2,128,2048]{3,2,1,0:T(8,128)(2,1)}), bf16[8,2,128,2048]{3,2,1,0:T(8,128)(2,1)}, u32[]{:S(2)}, u32[]{:S(2)}) async-start(bf16[8,2,128,2048]{3,2,1,0:T(8,128)(2,1)} %select_select_fusion), calls=%async_computation.1 | async-start | bytes 16777216 | tf_op jit(solution)/shard_map/all_to_all | solution.py:44
  45.0 0.0 copy-start.4
  45.0 0.2 reduce-scatter.2.cloned.1.call-start
  45.3 0.1 broadcast_bitcast_fusion
  45.4 0.0 copy-done.3
  45.4 1.3 constant_dynamic-update-slice_fusion.1
  46.7 0.0 copy-done.4
  46.7 1.3 constant_dynamic-update-slice_fusion
  47.9 31.0 %all-gather.2.cloned.1.call-done = bf16[2048,2048]{1,0:T(8,128)(2,1)} async-done(((bf16[512,2048]{1,0:T(8,128)(2,1)}), bf16[2048,2048]{1,0:T(8,128)(2,1)}) %all-gather.2.cloned.1.call-update) | async-done | bytes 8388624 | tf_op jit(solution)/shard_map/all_gather | solution.py:18
  79.0 10.0 %convolution_convert_fusion.1 = bf16[768,2048]{1,0:T(8,128)(2,1)S(1)} fusion(bf16[768,2048]{1,0:T(8,128)(2,1)} %constant_dynamic-update-slice_fusion, bf16[2048,2048]{1,0:T(8,128)(2,1)} %all-gather.2.cloned.1.call-done), kind=kOutput, calls=%fused_computation.10 | convolution fusion | flops 6444023808 | bytes 14680064 | tf_op jit(solution)/shard_map/dot_general | solution.py:20
  89.0 0.0 copy-start.5
  89.0 1.0 fusion.23
  90.0 0.7 copy-done.5
  90.8 0.2 copy.40
  91.0 136.4 %all-to-all-done.1 = bf16[8,2,128,2048]{3,2,1,0:T(8,128)(2,1)} async-done(((bf16[8,2,128,2048]{3,2,1,0:T(8,128)(2,1)}), bf16[8,2,128,2048]{3,2,1,0:T(8,128)(2,1)}, u32[]{:S(2)}, u32[]{:S(2)}) %all-to-all-start.1) | async-done | bytes 8388640 | tf_op jit(solution)/shard_map/all_to_all | solution.py:44
  227.4 8.1 %gather_fusion.2 = bf16[16,128,2048]{2,1,0:T(8,128)(2,1)} fusion(bf16[16,128,2048]{2,1,0:T(8,128)(2,1)} %bitcast.8, s32[1024]{0:T(1024)S(1)} %pad_clamp_fusion), kind=kCustom, calls=%fused_computation.2 | custom fusion | bytes 16777280 | tf_op jit(solution)/shard_map/jit(_take)/gather | solution.py:46
  235.5 7.4 %bitcast_select_fusion = bf16[2048,2048]{1,0:T(8,128)(2,1)} fusion(bf16[16,128,2048]{2,1,0:T(8,128)(2,1)} %gather_fusion.2, pred[2048]{0:T(1024)(128)(4,1)S(1)} %broadcast_bitcast_fusion), kind=kLoop, calls=%fused_computation.4 | loop fusion | flops 4194304 | bytes 16779264 | tf_op jit(solution)/shard_map/jit(_take)/select_n | solution.py:46
  242.9 6.5 %fusion.24 = (f32[384]{0:T(512)S(1)}, f32[384,2048]{1,0:T(8,128)S(1)}) fusion(bf16[2048,2048]{1,0:T(8,128)(2,1)} %bitcast_select_fusion, bf16[768,2048]{1,0:T(8,128)(2,1)} %copy-done.5), kind=kOutput, calls=%fused_computation.78 | convolution fusion | flops 3222797824 | bytes 13108736 | tf_op jit(solution)/shard_map/dot_general | solution.py:48
  249.5 0.0 copy-start.2
  249.5 0.6 fusion.1
  250.1 1.1 multiply_convert_fusion
  251.2 1.6 copy-done.2
  252.8 0.0 copy-start.6
  252.8 3.4 fusion.3
  256.2 0.0 copy-done.6
  256.3 1.0 convolution_convert_fusion.2
  257.3 0.0 copy-start.7
  257.3 1.0 add_convert_fusion
  258.3 0.1 copy-done.7
  258.4 12.2 %fusion.2 = f32[2048,2048]{1,0:T(8,128)} fusion(bf16[768,2048]{1,0:T(8,128)(2,1)} %constant_dynamic-update-slice_fusion, bf16[384,2048]{1,0:T(8,128)(2,1)S(1)} %convolution_convert_fusion.2, bf16[384,2048]{1,0:T(8,128)(2,1)S(1)} %add_convert_fusion), kind=kOutput, calls=%fused_computation.16 | convolution fusion | flops 6448742400 | bytes 23068672 | tf_op jit(solution)/shard_map/dot_general | solution.py:79
  270.6 0.0 reduce-scatter.2.cloned.1.call-update
  270.7 3.5 gather_fusion.3
  274.2 0.6 subtract_reduce_fusion
  274.8 45.7 %psum.7 = f32[]{:T(128)} all-reduce(f32[]{:T(128)} %subtract_reduce_fusion), channel_id=1, replica_groups=mesh['dp'=8,'fsdp'=4] {'dp','fsdp'}, use_global_device_ids=true, to_apply=%region_6.7 | all-reduce | flops 1 | bytes 8 | tf_op jit(solution)/shard_map/psum | solution.py:77
  321.1 0.0 copy-start.1
  321.1 9.7 %convolution_convert_fusion = bf16[768,2048]{1,0:T(8,128)(2,1)S(1)} fusion(bf16[2048,2048]{1,0:T(8,128)(2,1)} %all-gather.2.cloned.1.call-done, bf16[384,2048]{1,0:T(8,128)(2,1)} %copy-done.7, bf16[384,2048]{1,0:T(8,128)(2,1)S(1)} %add_convert_fusion), kind=kOutput, calls=%fused_computation.9 | convolution fusion | flops 6450315264 | bytes 14680064 | tf_op jit(solution)/shard_map/dot_general | solution.py:73
  330.8 1.9 fusion.22
  332.7 121.1 %reduce-scatter.2.cloned.1.call-done = f32[64,2048]{1,0:T(8,128)} async-done(((f32[2048,2048]{1,0:T(8,128)}), f32[64,2048]{1,0:T(8,128)}) %reduce-scatter.2.cloned.1.call-update) | async-done | bytes 524304 | tf_op jit(solution)/shard_map/reduce_scatter | solution.py:78
  453.9 0.0 copy-done.1
  (15 shorter events, 0.2 us)
Async XLA Ops:
  7.2 0.7 copy-start
  9.6 13.7 %all-to-all-start = ((s32[8,1,2]{2,1,0:T(1,128)}), s32[8,1,2]{2,1,0:T(1,128)S(1)}, u32[]{:S(2)}, u32[]{:S(2)}) async-start(s32[8,1,2]{2,1,0:T(1,128)} %copy.34), calls=%async_computation | async-start | bytes 8192 | tf_op jit(solution)/shard_map/all_to_all | solution.py:40
  16.9 62.1 %all-gather.2.cloned.1.call-start = ((), (), s32[]{:S(2)}) async-start(), calls=%async_computation.3 | async-start | bytes 10485760 | tf_op jit(solution)/shard_map/all_gather | solution.py:18
  39.9 5.5 %copy-start.3 = (bf16[384,2048]{1,0:T(8,128)(2,1)S(1)}, bf16[384,2048]{1,0:T(8,128)(2,1)}, u32[]{:S(2)}) copy-start(bf16[384,2048]{1,0:T(8,128)(2,1)} %param.6) | copy-start | bytes 4718596
  39.9 187.5 %all-to-all-start.1 = ((bf16[8,2,128,2048]{3,2,1,0:T(8,128)(2,1)}), bf16[8,2,128,2048]{3,2,1,0:T(8,128)(2,1)}, u32[]{:S(2)}, u32[]{:S(2)}) async-start(bf16[8,2,128,2048]{3,2,1,0:T(8,128)(2,1)} %select_select_fusion), calls=%async_computation.1 | async-start | bytes 16777216 | tf_op jit(solution)/shard_map/all_to_all | solution.py:44
  45.0 1.7 copy-start.4
  45.0 408.9 %reduce-scatter.2.cloned.1.call-start = ((), (), s32[]{:S(2)}) async-start(), calls=%async_computation.4 | async-start | bytes 17301504 | tf_op jit(solution)/shard_map/reduce_scatter | solution.py:78
  89.0 1.8 copy-start.5
  249.5 3.4 copy-start.2
  252.8 3.4 copy-start.6
  257.3 1.1 copy-start.7
  321.1 132.8 %copy-start.1 = (s32[256]{0:T(256)S(1)}, s32[256]{0:T(256)}, u32[]{:S(2)}) copy-start(s32[256]{0:T(256)} %param.11) | copy-start | bytes 3076
Sparse Core Ops, SparseCore 0:
  19.3 59.6 all-gather.1
  270.8 183.0 reduce-scatter.1
where the time goes:
time: 463 us; the launch traced here: 462 us
  waiting for transfers between devices  295 us (64%)
  blocking collectives  45.7 us (10%)
  matrix products  44.9 us (10%)
  local copies, waits for them, and re-layouts  28.3 us (6%)
  other arithmetic  19.4 us (4%)
  between operations  16 us (3%)
  starting transfers between devices  12.6 us (3%)
    all_to_all x1, waiting for transfers between devices, body(): lax.all_to_all(picked, 'dp', split_axis=0, concat_axis=0, tiled=True)  136 us
    reduce_scatter x1, waiting for transfers between devices, body(): lax.psum_scatter(lax.dot_general(hidden, grad_rows, (((0,), (0,)), ((), (...  121 us
    psum x1, blocking collectives, body(): loss = lax.psum(loss_local, ('dp', 'fsdp')) / (count_q * devices_all)  45.7 us
    all_gather x1, waiting for transfers between devices, body(): full_weight = lax.all_gather(weight, 'fsdp', axis=0, tiled=True)  31 us
    dot_general x1, matrix products, body(): lax.dot_general(hidden, grad_rows, (((0,), (0,)), ((), ())), preferred_el...  12.2 us
    dot_general x1, matrix products, body(): jnp.dot(hidden, full_weight, preferred_element_type=jnp.float32)  10 us
    dot_general x1, matrix products, body(): lax.dot_general(grad_rows, full_weight, (((1,), (1,)), ((), ())), preferr...  9.7 us
  transfers between devices with their start and end apart: 4, of which 4 were waited for; matrix products, arithmetic and copies ran while one was open for 10% of the time, Pallas kernels for 0%

commit v1 on v0

v1 whole, which is shorter than its diff:
```python
import functools
import math

import jax
import jax.numpy as jnp
from jax import lax
from jax.experimental import pallas as pl
from jax.experimental.pallas import tpu as pltpu
from jax.sharding import PartitionSpec as P

CAP = 2

SOFTMAX_TEMPER = 0.25

NEG_BIG = -1e30

F32 = jnp.float32
BF16 = jnp.bfloat16

VMEM_LIMIT = 32 * 1024 * 1024


def bits_of(size):
    return [1 << i for i in range(size.bit_length() - 1)]


def swap(x, axis, bit):
    return lax.ppermute(x, axis, [(i, i ^ bit) for i in range(lax.axis_size(axis))])


def dot_t(a, b):
    return lax.dot_general(a, b, (((1,), (1,)), ((), ())), preferred_element_type=F32)


def params(**kw):
    return pltpu.CompilerParams(vmem_limit_bytes=VMEM_LIMIT, **kw)


def pick_blocks(bank, ids, block_home, me, n_dp, n_fsdp):
    per_dev, block_rows, width = bank.shape
    named = ids.shape[1]
    span = per_dev * n_fsdp
    half = n_dp // 2

    def kernel(ids_ref, home_ref, me_ref, bank_ref, *refs):
        outs, table, sem = refs[:half], refs[half], refs[half + 1]
        here = me_ref[0]
        copies = []
        for k in range(half):
            for side in range(2):
                group = here ^ k ^ (side * half)
                for p in range(CAP):
                    table[p] = 0
                count = jnp.int32(0)
                for j in range(named):
                    slot = home_ref[ids_ref[group, j]]
                    mine = lax.div(slot, span) == here

                    @pl.when(mine)
                    def _():
                        table[jnp.minimum(count, CAP - 1)] = lax.rem(slot, per_dev)

                    count = count + mine.astype(jnp.int32)
                for p in range(CAP):
                    at = side * CAP + p
                    copy = pltpu.make_async_copy(
                        bank_ref.at[table[p]],
                        outs[k].at[pl.ds(at * block_rows, block_rows)],
                        sem.at[k * 2 * CAP + at],
                    )
                    copy.start()
                    copies.append(copy)
        for copy in copies:
            copy.wait()

    smem = pl.BlockSpec(memory_space=pltpu.SMEM)
    shape = (2 * CAP * block_rows, width)
    return pl.pallas_call(
        kernel,
        in_specs=[smem, smem, smem, pl.BlockSpec(memory_space=pl.ANY)],
        out_specs=[pl.BlockSpec(memory_space=pltpu.VMEM)] * half,
        out_shape=[jax.ShapeDtypeStruct(shape, bank.dtype)] * half,
        scratch_shapes=[
            pltpu.SMEM((CAP,), jnp.int32),
            pltpu.SemaphoreType.DMA((half * 2 * CAP,)),
        ],
        compiler_params=params(),
        cost_estimate=pl.CostEstimate(
            flops=0, bytes_accessed=4 * half * shape[0] * width, transcendentals=0
        ),
        name="pick_blocks",
    )(ids, block_home, me.reshape(1), bank)


def column(x):
    return jnp.max(x, axis=1, keepdims=True)


def part_scores(emb_q, emb_v, block, scale):
    count, width = emb_q.shape
    rows = block.shape[0] // 2

    def kernel(q_ref, v_ref, x_ref, own, guest):
        own[...] = dot_t(q_ref[...], x_ref[:rows]) * scale
        guest[...] = dot_t(v_ref[...], x_ref[rows:]) * scale

    return pl.pallas_call(
        kernel,
        out_shape=[jax.ShapeDtypeStruct((count, rows), F32)] * 2,
        compiler_params=params(),
        cost_estimate=pl.CostEstimate(
            flops=4 * count * rows * width,
            bytes_accessed=4 * (count + rows) * width,
            transcendentals=0,
        ),
        name="part_scores",
    )(emb_q, emb_v, block)


def pack_stats(inner, own, guest):
    count = inner.shape[0]
    n = len(own)

    def kernel(*refs):
        mine = [r[...] for r in refs[: n + 1]]
        other = [r[...] for r in refs[n + 1 : -1]]
        cols = []
        for group in (mine, other):
            top = functools.reduce(jnp.maximum, [column(s) for s in group])
            total = sum(jnp.sum(jnp.exp(s - top), axis=1, keepdims=True) for s in group)
            cols += [top, total]
        row = lax.broadcasted_iota(jnp.int32, (count, count), 0)
        col = lax.broadcasted_iota(jnp.int32, (count, count), 1)
        cols.append(jnp.sum(jnp.where(row == col, mine[0], 0.0), axis=1, keepdims=True))
        lane = lax.broadcasted_iota(jnp.int32, (count, 128), 1)
        wide = jnp.zeros((count, 128), F32)
        for i, c in enumerate(cols):
            wide = jnp.where(lane == i, c, wide)
        refs[-1][...] = wide.T[:8]

    return pl.pallas_call(
        kernel,
        out_shape=jax.ShapeDtypeStruct((8, count), F32),
        compiler_params=params(),
        name="pack_stats",
    )(inner, *own, *guest)


def joined(mine, there, a, b):
    pad = jnp.zeros((120, mine.shape[1]), F32)
    m = jnp.concatenate([mine, pad], axis=0).T
    t = jnp.concatenate([there, pad], axis=0).T
    m_top, m_sum = m[:, a : a + 1], m[:, a + 1 : a + 2]
    t_top, t_sum = t[:, b : b + 1], t[:, b + 1 : b + 2]
    top = jnp.maximum(m_top, t_top)
    return top, m_sum * jnp.exp(m_top - top) + t_sum * jnp.exp(t_top - top)


def guest_rows(scores, blocks, mine, there, scale, tile):
    count = mine.shape[1]
    n = len(scores)
    part, width = scores[0].shape[1], blocks[0].shape[1]

    def kernel(mine_ref, there_ref, *refs):
        s_refs, x_refs, out, probs = refs[:n], refs[n : 2 * n], refs[2 * n], refs[2 * n + 1]

        @pl.when(pl.program_id(0) == 0)
        def _():
            top, total = joined(mine_ref[...], there_ref[...], 2, 0)
            level = scale / total
            for k in range(n):
                probs[:, k * part : (k + 1) * part] = (
                    jnp.exp(s_refs[k][...] - top) * level
                ).astype(BF16)

        acc = jnp.zeros((count, tile), F32)
        for k in range(n):
            acc += jnp.dot(
                probs[:, k * part : (k + 1) * part], x_refs[k][...], preferred_element_type=F32
            )
        out[...] = acc.astype(BF16)

    whole = lambda a: pl.BlockSpec(a.shape, lambda i: (0, 0))
    return pl.pallas_call(
        kernel,
        grid=(width // tile,),
        in_specs=[whole(mine), whole(there)]
        + [whole(s) for s in scores]
        + [pl.BlockSpec((part, tile), lambda i: (1, i))] * n,
        out_specs=pl.BlockSpec((count, tile), lambda i: (0, i)),
        out_shape=jax.ShapeDtypeStruct((count, width), BF16),
        scratch_shapes=[pltpu.VMEM((count, n * part), BF16)],
        compiler_params=params(),
        cost_estimate=pl.CostEstimate(
            flops=2 * count * n * part * width,
            bytes_accessed=2 * n * part * width + 2 * count * width,
            transcendentals=count * n * part,
        ),
        name="guest_rows",
    )(mine, there, *scores, *blocks)


def own_rows(inner, scores, blocks, emb_q, emb_p, mine, there, scale, tile):
    count = inner.shape[0]
    n = len(scores)
    part, width = scores[0].shape[1], blocks[0].shape[1]

    def kernel(mine_ref, there_ref, inner_ref, *refs):
        s_refs, x_refs = refs[:n], refs[n : 2 * n]
        q_ref, p_ref, out, out_q, out_p, loss, probs, near, near_t = refs[2 * n :]

        @pl.when(pl.program_id(0) == 0)
        def _():
            top, total = joined(mine_ref[...], there_ref[...], 0, 2)
            level = scale / total
            for k in range(n):
                probs[:, k * part : (k + 1) * part] = (
                    jnp.exp(s_refs[k][...] - top) * level
                ).astype(BF16)
            s = inner_ref[...]
            row = lax.broadcasted_iota(jnp.int32, s.shape, 0)
            col = lax.broadcasted_iota(jnp.int32, s.shape, 1)
            target = jnp.where(row == col, 1.0, 0.0)
            grad = (jnp.exp(s - top) / total - target) * scale
            near[...] = grad.astype(BF16)
            near_t[...] = grad.T.astype(BF16)
            gtop, gtotal = joined(mine_ref[...], there_ref[...], 2, 0)
            rows = jnp.sum(top + jnp.log(total) + gtop + jnp.log(gtotal), axis=0, keepdims=True)
            lanes = jnp.sum(mine_ref[4:5, :] + there_ref[4:5, :], axis=1, keepdims=True)
            loss[...] = jnp.broadcast_to(rows - lanes, loss.shape)

        acc = jnp.dot(near[...], p_ref[...], preferred_element_type=F32)
        for k in range(n):
            acc += jnp.dot(
                probs[:, k * part : (k + 1) * part], x_refs[k][...], preferred_element_type=F32
            )
        out[...] = acc
        out_q[...] = acc.astype(BF16)
        out_p[...] = jnp.dot(near_t[...], q_ref[...], preferred_element_type=F32).astype(BF16)

    whole = lambda a: pl.BlockSpec(a.shape, lambda i: (0, 0))
    cut = lambda r: pl.BlockSpec((r, tile), lambda i: (0, i))
    return pl.pallas_call(
        kernel,
        grid=(width // tile,),
        in_specs=[whole(mine), whole(there), whole(inner)]
        + [whole(s) for s in scores]
        + [cut(part)] * n
        + [cut(count)] * 2,
        out_specs=[cut(count)] * 3 + [pl.BlockSpec((8, 128), lambda i: (0, 0))],
        out_shape=[
            jax.ShapeDtypeStruct((count, width), F32),
            jax.ShapeDtypeStruct((count, width), BF16),
            jax.ShapeDtypeStruct((count, width), BF16),
            jax.ShapeDtypeStruct((8, 128), F32),
        ],
        scratch_shapes=[
            pltpu.VMEM((count, n * part), BF16),
            pltpu.VMEM((count, count), BF16),
            pltpu.VMEM((count, count), BF16),
        ],
        compiler_params=params(),
        cost_estimate=pl.CostEstimate(
            flops=2 * count * (n * part + 2 * count) * width,
            bytes_accessed=2 * n * part * width + 12 * count * width,
            transcendentals=count * (n * part + count),
        ),
        name="own_rows",
    )(mine, there, inner, *scores, *blocks, emb_q, emb_p)


def weight_part(left, rights, base, rows_at, col_at, cols, dtype):
    quarter = left.shape[0] // 4
    count = rights[0].shape[0]
    n = len(rights)
    first, step = rows_at[0], (rows_at[1] - rows_at[0] if len(rows_at) > 1 else 1)

    def kernel(left_ref, *refs):
        acc = refs[n][...] if base is not None else jnp.zeros((quarter, cols), F32)
        for k in range(n):
            acc += jnp.dot(
                left_ref[:, k * count : (k + 1) * count],
                refs[k][...],
                preferred_element_type=F32,
            )
        refs[-1][...] = acc.astype(dtype)

    in_specs = [pl.BlockSpec((quarter, left.shape[1]), lambda i: (first + step * i, 0))]
    in_specs += [pl.BlockSpec((count, cols), lambda i: (0, col_at))] * n
    args = [left, *rights]
    if base is not None:
        in_specs.append(pl.BlockSpec((quarter, cols), lambda i: (first + step * i, col_at)))
        args.append(base)
    total = len(rows_at) * quarter
    return pl.pallas_call(
        kernel,
        grid=(len(rows_at),),
        in_specs=in_specs,
        out_specs=pl.BlockSpec((quarter, cols), lambda i: (i, 0)),
        out_shape=jax.ShapeDtypeStruct((total, cols), dtype),
        compiler_params=params(),
        cost_estimate=pl.CostEstimate(
            flops=2 * total * n * count * cols,
            bytes_accessed=2 * n * count * (cols + total) + 8 * total * cols,
            transcendentals=0,
        ),
        name="weight_part",
    )(*args)


def tied(x, after):
    return x + jnp.minimum(jnp.abs(after[:1, :1]), 0.0)


def body(queries, passages, weight, bank, neg_ids, block_home):
    count, kin = queries.shape
    width = weight.shape[1]
    scale = 1.0 / (SOFTMAX_TEMPER * math.sqrt(width))
    n_dp = lax.axis_size("dp")
    n_fsdp = lax.axis_size("fsdp")
    devices = n_dp * n_fsdp
    block_rows = bank.shape[1]
    named = neg_ids.shape[1]
    half = n_dp // 2
    me = lax.axis_index("dp")
    linear = me * n_fsdp + lax.axis_index("fsdp")

    ids = lax.all_to_all(
        jnp.broadcast_to(neg_ids, (n_dp, named)), "dp", split_axis=0, concat_axis=0, tiled=True
    )
    visit = swap(jnp.where(ids[0, 0] < 0, jnp.zeros_like(queries), queries), "dp", half)
    picked = pick_blocks(bank, ids, block_home, me, n_dp, n_fsdp)
    parts = [picked[0]] + [swap(picked[k], "dp", k) for k in range(1, half)]

    full_weight = lax.all_gather(weight, "fsdp", axis=0, tiled=True)
    emb_q = jnp.dot(queries, full_weight, preferred_element_type=F32).astype(BF16)
    emb_p = jnp.dot(passages, full_weight, preferred_element_type=F32).astype(BF16)
    emb_v = jnp.dot(visit, full_weight, preferred_element_type=F32).astype(BF16)

    f_bits = [("fsdp", b) for b in bits_of(n_fsdp)]
    d_bits = [("dp", b) for b in bits_of(n_dp)]
    stages = [f_bits[1], d_bits[0]] + f_bits[2:] + d_bits[1:]
    mask = []
    for p in range(devices // 2):
        m = 0
        for s, (axis, bit) in enumerate(stages):
            if not (p >> (len(stages) - 1 - s)) & 1:
                m |= bit if axis == "fsdp" else bit * n_fsdp
        mask.append(m)
    mask = jnp.array(mask, jnp.int32)
    hidden_t = jnp.concatenate([queries, passages, visit], axis=0).T
    hidden_t = hidden_t.reshape(devices, kin // devices, -1)
    left = jnp.take(hidden_t, linear ^ mask, axis=0).reshape(kin // 2, -1)
    left_out = jnp.take(hidden_t, linear ^ 1 ^ mask, axis=0).reshape(kin // 2, -1)
    left_in = swap(left_out, *f_bits[0])

    masked = n_dp * CAP > named
    if masked:
        owner = block_home[ids] // bank.shape[0] // n_fsdp

    inner = dot_t(emb_q, emb_p) * scale
    s_own, s_guest = [], []
    for k, x in enumerate(parts):
        pair = list(part_scores(emb_q, emb_v, x, scale))
        if masked:
            for i, group in enumerate((me, me ^ half)):
                held = jnp.sum((owner[group] == (me ^ k)).astype(jnp.int32))
                there = jnp.arange(CAP * block_rows) // block_rows < held
                pair[i] = jnp.where(there[None, :], pair[i], NEG_BIG)
        s_own.append(pair[0])
        s_guest.append(pair[1])

    mine = pack_stats(inner, s_own, s_guest)
    there = swap(mine, "dp", half)
    tile = 512
    rows_v = guest_rows(s_guest, parts, mine, there, scale, tile)
    home = swap(rows_v, "dp", half)
    rows_own, rows_q, rows_p, loss = own_rows(
        inner, s_own, parts, emb_q, emb_p, mine, there, scale, tile
    )

    rights = [rows_q, rows_p, rows_v]
    far_rights = [swap(r, *f_bits[0]) for r in rights]
    base = weight_part(left, rights, None, (0, 1, 2, 3), 0, width, F32)
    cols = width // 2
    give = ((0, 1), (0, 2))
    hold = ((2, 3), (1, 3))
    sends = [weight_part(left_in, far_rights, base, give[i], i, cols, BF16) for i in range(2)]
    keeps = [weight_part(left_in, far_rights, base, hold[i], i, cols, F32) for i in range(2)]
    orders = [stages, [stages[1], stages[0]] + stages[2:]]

    loss = loss[:1, :1]
    for axis, bit in f_bits + d_bits[:-2]:
        loss = loss + swap(loss, axis, bit)

    mid = kin // 4
    for s in range(len(stages)):
        last = s + 1 == len(stages)
        if last:
            loss = tied(loss, keeps[0])
            loss = loss + swap(loss, *d_bits[-2])
        got = [swap(sends[i], *orders[i][s]) for i in range(2)]
        keeps = [keeps[i] + got[i].astype(F32) for i in range(2)]
        if not last:
            mid = mid // 2
            sends = [k[:mid].astype(BF16) for k in keeps]
            keeps = [k[mid:] for k in keeps]
    grad_weight = jnp.concatenate(keeps, axis=1)
    loss = loss[0, 0] / (count * devices)

    back_p = dot_t(rows_p, full_weight).astype(BF16)
    both = (rows_own + home.astype(F32)).astype(BF16)
    back_q = dot_t(both, full_weight).astype(BF16)
    return (loss, grad_weight, back_q, back_p)


def solution(mesh):
    return jax.shard_map(
        body,
        mesh=mesh,
        in_specs=(
            P(("dp", "fsdp"), None),
            P(("dp", "fsdp"), None),
            P("fsdp", None),
            P(("dp", "fsdp"), None, None),
            P(("dp", "fsdp"), None),
            P(),
        ),
        out_specs=(P(), P(("dp", "fsdp"), None), P(("dp", "fsdp"), None), P(("dp", "fsdp"), None)),
        check_vma=False,
    )
```

time: 463 us -> 314 us (0.68)
  waiting for transfers between devices: 295 us -> 156 us
  Pallas kernels: 0 us -> 54 us
  blocking collectives: 45.7 us -> 0 us
  matrix products: 44.9 us -> 30.7 us
  starting transfers between devices: 12.6 us -> 26.6 us
  local copies, waits for them, and re-layouts: 28.3 us -> 15.1 us
  other arithmetic: 19.4 us -> 10.6 us
    ppermute x0 -> x22, waiting for transfers between devices: none -> 150 us  [swap(): lax.ppermute(x, axis, [(i, i ^ bit) for i in range(lax.axis_size(axis))])]
    all_to_all x2 -> x1, waiting for transfers between devices: 142 us -> 5.51 us  [body(): lax.all_to_all(jnp.broadcast_to(neg_ids, (n_dp, named)), 'dp', split_axis...]
    reduce_scatter x1 -> x0, waiting for transfers between devices: 121 us -> none  [body(): lax.psum_scatter(lax.dot_general(hidden, grad_rows, (((0,), (0,)), ((), (...]
    pallas_call x0 -> x13, Pallas kernels: none -> 54 us  [the longest x5 24.5 us: weight_part(): pl.pallas_call(kernel, grid=(len(rows_at),), in_specs=in_specs, out_specs...]
    psum x1 -> x0, blocking collectives: 45.7 us -> none  [body(): loss = lax.psum(loss_local, ('dp', 'fsdp')) / (count_q * devices_all)]
    all_gather x1, waiting for transfers between devices: 31 us -> 0.01 us  [body(): full_weight = lax.all_gather(weight, 'fsdp', axis=0, tiled=True)]
    ppermute x0 -> x22, starting transfers between devices: none -> 19.2 us  [swap(): lax.ppermute(x, axis, [(i, i ^ bit) for i in range(lax.axis_size(axis))])]
    dot_general x8 -> x6, matrix products: 44.9 us -> 30.7 us  [the longest x3 14.9 us: dot_t(): lax.dot_general(a, b, (((1,), (1,)), ((), ())), preferred_element_type=F32)]
  transfers between devices with their start and end apart: 4 -> 24, of which waited for: 4 -> 12; matrix products, arithmetic and copies ran while one was open for 10% -> 17% of each run, Pallas kernels for 0% -> 16%
where the time goes in v1:
time: 314 us; the launch traced here: 313 us
  waiting for transfers between devices  156 us (50%)
  Pallas kernels  54 us (17%)
  matrix products  30.7 us (10%)
  starting transfers between devices  26.6 us (8%)
  between operations  20 us (6%)
  local copies, waits for them, and re-layouts  15.1 us (5%)
  other arithmetic  10.6 us (3%)
    ppermute x22, waiting for transfers between devices, swap(): lax.ppermute(x, axis, [(i, i ^ bit) for i in range(lax.axis_size(axis))])  150 us
    pallas_call x5, Pallas kernels, weight_part(): pl.pallas_call(kernel, grid=(len(rows_at),), in_specs=in_specs, out_specs...  24.5 us
    ppermute x22, starting transfers between devices, swap(): lax.ppermute(x, axis, [(i, i ^ bit) for i in range(lax.axis_size(axis))])  19.2 us
    dot_general x3, matrix products, dot_t(): lax.dot_general(a, b, (((1,), (1,)), ((), ())), preferred_element_type=F32)  14.9 us
    pallas_call x4, Pallas kernels, part_scores(): pl.pallas_call(kernel, out_shape=[jax.ShapeDtypeStruct((count, rows), F32...  8.91 us
    pallas_call x1, Pallas kernels, own_rows(): pl.pallas_call(kernel, grid=(width // tile,), in_specs=[whole(mine), whol...  8.27 us
    dot_general x1, matrix products, body(): jnp.dot(queries, full_weight, preferred_element_type=F32).astype(BF16)  7.41 us
    all_to_all x1, starting transfers between devices, body(): lax.all_to_all(jnp.broadcast_to(neg_ids, (n_dp, named)), 'dp', split_axis...  7.28 us
  transfers between devices with their start and end apart: 24, of which 12 were waited for; matrix products, arithmetic and copies ran while one was open for 17% of the time, Pallas kernels for 16%

profile of v1, /device:TPU:0, one launch (start us, length us, event | category | flops | bytes accessed | tf_op | source)
XLA Modules:
  0.0 313.3 jit_solution(7951942996110953113)
XLA Ops:
  7.2 0.7 all-gather.2.cloned.1.call-update
  7.9 0.6 broadcast_in_dim.17
  8.5 7.3 %all-to-all-start = ((s32[8,1,16]{2,1,0:T(1,128)}), s32[8,1,16]{2,1,0:T(1,128)S(1)}, u32[]{:S(2)}, u32[]{:S(2)}) async-start(s32[8,1,16]{2,1,0:T(1,128)} %broadcast_in_dim.17), calls=%async_computation | async-start | bytes 8192 | tf_op jit(solution)/shard_map/all_to_all | solution.py:328
  15.8 0.9 copy.14
  16.7 5.5 %all-to-all-done = s32[8,1,16]{2,1,0:T(1,128)S(1)} async-done(((s32[8,1,16]{2,1,0:T(1,128)}), s32[8,1,16]{2,1,0:T(1,128)S(1)}, u32[]{:S(2)}, u32[]{:S(2)}) %all-to-all-start) | async-done | bytes 544 | tf_op jit(solution)/shard_map/all_to_all | solution.py:328
  22.2 0.5 slice.52
  23.4 1.3 broadcast_select_fusion.2
  24.7 0.6 collective-permute-start
  25.2 1.9 copy.16
  27.2 2.2 copy-done.2
  29.4 4.7 %pick_blocks.1 = (bf16[512,2048]{1,0:T(8,128)(2,1)S(1)}, bf16[512,2048]{1,0:T(8,128)(2,1)}, bf16[512,2048]{1,0:T(8,128)(2,1)}, bf16[512,2048]{1,0:T(8,128)(2,1)}) custom-call(s32[8,16]{1,0:T(8,128)S(1)} %bitcast.23, s32[256]{0:T(256)S(1)} %copy-done.3, s32[1]{0:T(128)} %bitcast.3.me_ref, bf16[8,128,2048]{2,1,0:T(8,128)(2,1)S(1)} %copy-done.2), custom_call_target="tpu_custom_call" | custom-call | bytes 16777216 | tf_op jit(solution)/shard_map/pick_blocks/pallas_call | solution.py:78
  34.1 0.7 collective-permute-start.1
  34.8 0.7 collective-permute-start.2
  35.5 2.1 collective-permute-start.3
  37.7 56.7 %collective-permute-done = bf16[384,2048]{0,1:T(8,128)(2,1)} collective-permute-done((bf16[384,2048]{0,1:T(8,128)(2,1)}, bf16[384,2048]{0,1:T(8,128)(2,1)}, u32[]{:S(2)}, u32[]{:S(2)}) %collective-permute-start) | collective-permute-done | bytes 1572896 | tf_op jit(solution)/shard_map/ppermute | solution.py:28
  94.4 3.4 %pad_maximum_fusion = bf16[1152,2048]{0,1:T(8,128)(2,1)} fusion(bf16[384,2048]{0,1:T(8,128)(2,1)} %collective-permute-done, bf16[384,2048]{0,1:T(8,128)(2,1)S(1)} %copy.16, bf16[384,2048]{0,1:T(8,128)(2,1)S(1)} %copy.14), kind=kLoop, calls=%fused_computation.2 | loop fusion | flops 14155776 | bytes 9437184 | tf_op jit(solution)/shard_map/concatenate | solution.py:351
  97.8 3.3 %gather_fusion = bf16[16,64,1152]{2,1,0:T(8,128)(2,1)S(1)} fusion(bf16[32,64,1152]{2,1,0:T(8,128)(2,1)} %bitcast.24, s32[1024]{0:T(1024)S(1)} %pad_clamp_fusion.1), kind=kCustom, calls=%fused_computation.clone | custom fusion | bytes 4718656 | tf_op jit(solution)/shard_map/jit(_take)/gather | solution.py:354
  101.1 1.7 broadcast_select_fusion.1
  102.8 7.4 %convolution_convert_fusion.4.q_ref.refs_8_ = bf16[384,2048]{1,0:T(8,128)(2,1)S(1)} fusion(bf16[384,2048]{1,0:T(8,128)(2,1)} %param.9, bf16[2048,2048]{1,0:T(8,128)(2,1)} %all-gather.2.cloned.1.call-done), kind=kOutput, calls=%fused_computation.8 | convolution fusion | flops 3222011904 | bytes 11534336 | tf_op jit(solution)/shard_map/dot_general | solution.py:336
  110.2 5.0 %convolution_convert_fusion.2.v_ref = bf16[384,2048]{1,0:T(8,128)(2,1)S(1)} fusion(bf16[384,2048]{0,1:T(8,128)(2,1)} %collective-permute-done, bf16[2048,2048]{1,0:T(8,128)(2,1)S(1)} %copy-done.10), kind=kOutput, calls=%fused_computation.6 | convolution fusion | flops 3222011904 | bytes 11534336 | tf_op jit(solution)/shard_map/dot_general | solution.py:338
  115.3 1.0 part_scores.4
  116.3 2.6 part_scores.5
  118.9 2.7 part_scores.6
  121.7 3.4 %convolution_convert_fusion.3.refs_9_ = bf16[384,2048]{1,0:T(8,128)(2,1)S(1)} fusion(bf16[384,2048]{1,0:T(8,128)(2,1)S(1)} %copy-done.7, bf16[2048,2048]{1,0:T(8,128)(2,1)S(1)} %copy-done.10), kind=kOutput, calls=%fused_computation.7 | convolution fusion | flops 3222011904 | bytes 11534336 | tf_op jit(solution)/shard_map/dot_general | solution.py:337
  125.1 35.0 %collective-permute-done.3.x_ref.refs_7_ = bf16[512,2048]{1,0:T(8,128)(2,1)} collective-permute-done((bf16[512,2048]{1,0:T(8,128)(2,1)}, bf16[512,2048]{1,0:T(8,128)(2,1)}, u32[]{:S(2)}, u32[]{:S(2)}) %collective-permute-start.3) | collective-permute-done | bytes 2097184 | tf_op jit(solution)/shard_map/ppermute | solution.py:28
  160.1 2.6 part_scores.7
  162.7 1.2 convolution_multiply_fusion.refs_0_.inner_ref
  163.9 1.2 pack_stats.1.mine_ref
  165.2 4.6 %collective-permute-done.4.there_ref = f32[8,384]{1,0:T(8,128)S(1)} collective-permute-done((f32[8,384]{1,0:T(8,128)S(1)}, f32[8,384]{1,0:T(8,128)S(1)}, u32[]{:S(2)}, u32[]{:S(2)}) %collective-permute-start.4) | collective-permute-done | bytes 12320 | tf_op jit(solution)/shard_map/ppermute | solution.py:28
  169.7 8.3 %own_rows.1 = (f32[384,2048]{1,0:T(8,128)S(1)}, bf16[384,2048]{1,0:T(8,128)(2,1)}, bf16[384,2048]{1,0:T(8,128)(2,1)}, f32[8,128]{1,0:T(8,128)S(1)}) custom-call(f32[8,384]{1,0:T(8,128)S(1)} %pack_stats.1.mine_ref, f32[8,384]{1,0:T(8,128)S(1)} %collective-permute-done.4.there_ref, f32[384,384]{1,0:T(8,128)S(1)} %convolution_multiply_fusion.refs_0_.inner_ref, ...), custom_call_target="tpu_custom_call" | custom-call | flops 2818572288 | bytes 13631488 | tf_op jit(solution)/shard_map/own_rows/pallas_call | solution.py:243
  178.0 0.5 collective-permute-start.10
  178.5 6.4 %guest_rows.1.refs_2_ = bf16[384,2048]{1,0:T(8,128)(2,1)} custom-call(f32[8,384]{1,0:T(8,128)S(1)} %pack_stats.1.mine_ref, f32[8,384]{1,0:T(8,128)S(1)} %collective-permute-done.4.there_ref, f32[384,256]{1,0:T(8,128)S(1)} %get-tuple-element.29.refs_5_.refs_0_, f32[384,256]{1,0:T(8,128)S(1)} %get-tuple-element.30.refs_6_.refs_1_, ...), custom_call_target="tpu_custom_call" | custom-call | flops 1610612736 | bytes 5767168 | tf_op jit(solution)/shard_map/guest_rows/pallas_call | solution.py:184
  184.9 4.5 %gather_fusion.1 = bf16[16,64,1152]{2,1,0:T(8,128)(2,1)} fusion(bf16[32,64,1152]{2,1,0:T(8,128)(2,1)} %bitcast.25, s32[1024]{0:T(1024)S(1)} %pad_clamp_fusion), kind=kCustom, calls=%fused_computation.1.clone | custom fusion | bytes 4718656 | tf_op jit(solution)/shard_map/jit(_take)/gather | solution.py:353
  189.4 2.0 broadcast_select_fusion
  191.4 9.5 %weight_part.5.refs_3_ = f32[1024,2048]{1,0:T(8,128)S(1)} custom-call(bf16[1024,1152]{1,0:T(8,128)(2,1)S(1)} %bitcast.21, bf16[384,2048]{1,0:T(8,128)(2,1)} %get-tuple-element.34.refs_0_, bf16[384,2048]{1,0:T(8,128)(2,1)} %get-tuple-element.35.refs_1_, bf16[384,2048]{1,0:T(8,128)(2,1)} %guest_rows.1.refs_2_), custom_call_target="tpu_custom_call" | custom-call | flops 4831838208 | bytes 23855104 | tf_op jit(solution)/shard_map/weight_part/pallas_call | solution.py:295
  201.0 3.7 %weight_part.7 = bf16[512,1024]{1,0:T(8,128)(2,1)S(1)} custom-call(bf16[1024,1152]{1,0:T(8,128)(2,1)S(1)} %collective-permute-done.8.left_ref, bf16[384,2048]{1,0:T(8,128)(2,1)} %collective-permute-done.9.refs_0_, bf16[384,2048]{1,0:T(8,128)(2,1)} %collective-permute-done.10.refs_1_, bf16[384,2048]{1,0:T(8,128)(2,1)} %collective-permute-done.11.refs_2_, ...), custom_call_target="tpu_custom_call" | custom-call | flops 1207959552 | bytes 7733248 | tf_op jit(solution)/shard_map/weight_part/pallas_call | solution.py:295
  204.7 1.6 collective-permute-start.12
  206.3 3.7 %weight_part.9 = bf16[512,1024]{1,0:T(8,128)(2,1)S(1)} custom-call(bf16[1024,1152]{1,0:T(8,128)(2,1)S(1)} %collective-permute-done.8.left_ref, bf16[384,2048]{1,0:T(8,128)(2,1)} %collective-permute-done.9.refs_0_, bf16[384,2048]{1,0:T(8,128)(2,1)} %collective-permute-done.10.refs_1_, bf16[384,2048]{1,0:T(8,128)(2,1)} %collective-permute-done.11.refs_2_, ...), custom_call_target="tpu_custom_call" | custom-call | flops 1207959552 | bytes 7733248 | tf_op jit(solution)/shard_map/weight_part/pallas_call | solution.py:295
  210.0 0.7 collective-permute-start.17
  210.7 0.5 slice.53
  211.2 3.7 %weight_part.8 = f32[512,1024]{1,0:T(8,128)S(1)} custom-call(bf16[1024,1152]{1,0:T(8,128)(2,1)S(1)} %collective-permute-done.8.left_ref, bf16[384,2048]{1,0:T(8,128)(2,1)} %collective-permute-done.9.refs_0_, bf16[384,2048]{1,0:T(8,128)(2,1)} %collective-permute-done.10.refs_1_, bf16[384,2048]{1,0:T(8,128)(2,1)} %collective-permute-done.11.refs_2_, ...), custom_call_target="tpu_custom_call" | custom-call | flops 1207959552 | bytes 7733248 | tf_op jit(solution)/shard_map/weight_part/pallas_call | solution.py:295
  214.9 4.0 %weight_part.6 = f32[512,1024]{1,0:T(8,128)S(1)} custom-call(bf16[1024,1152]{1,0:T(8,128)(2,1)S(1)} %collective-permute-done.8.left_ref, bf16[384,2048]{1,0:T(8,128)(2,1)} %collective-permute-done.9.refs_0_, bf16[384,2048]{1,0:T(8,128)(2,1)} %collective-permute-done.10.refs_1_, bf16[384,2048]{1,0:T(8,128)(2,1)} %collective-permute-done.11.refs_2_, ...), custom_call_target="tpu_custom_call" | custom-call | flops 1207959552 | bytes 7733248 | tf_op jit(solution)/shard_map/weight_part/pallas_call | solution.py:295
  218.9 11.4 %collective-permute-done.12 = bf16[512,1024]{1,0:T(8,128)(2,1)S(1)} collective-permute-done((bf16[512,1024]{1,0:T(8,128)(2,1)S(1)}, bf16[512,1024]{1,0:T(8,128)(2,1)S(1)}, u32[]{:S(2)}, u32[]{:S(2)}) %collective-permute-start.12) | collective-permute-done | bytes 1048608 | tf_op jit(solution)/shard_map/ppermute | solution.py:28
  230.3 0.4 convert_add_fusion.1
  230.8 4.6 %collective-permute-done.17 = bf16[512,1024]{1,0:T(8,128)(2,1)S(1)} collective-permute-done((bf16[512,1024]{1,0:T(8,128)(2,1)S(1)}, bf16[512,1024]{1,0:T(8,128)(2,1)S(1)}, u32[]{:S(2)}, u32[]{:S(2)}) %collective-permute-start.17) | collective-permute-done | bytes 1048608 | tf_op jit(solution)/shard_map/ppermute | solution.py:28
  235.4 0.4 convert_add_fusion
  236.0 0.7 collective-permute-start.13
  236.7 0.5 collective-permute-start.18
  237.2 9.0 %convolution_convert_fusion = bf16[384,2048]{1,0:T(8,128)(2,1)} fusion(bf16[384,2048]{1,0:T(8,128)(2,1)} %get-tuple-element.35.refs_1_, bf16[2048,2048]{1,0:T(8,128)(2,1)} %all-gather.2.cloned.1.call-done), kind=kOutput, calls=%fused_computation.4 | convolution fusion | flops 3222011904 | bytes 11534336 | tf_op jit(solution)/shard_map/dot_general | solution.py:32
  247.6 2.3 collective-permute-start.6
  249.9 1.5 collective-permute-done.6
  251.9 2.0 collective-permute-start.7
  253.9 1.7 collective-permute-done.7
  256.2 0.1 slice_add_fusion.1
  256.6 2.1 collective-permute-start.19
  258.7 22.3 %collective-permute-done.21 = bf16[384,2048]{1,0:T(8,128)(2,1)S(1)} collective-permute-done((bf16[384,2048]{1,0:T(8,128)(2,1)}, bf16[384,2048]{1,0:T(8,128)(2,1)S(1)}, u32[]{:S(2)}, u32[]{:S(2)}) %collective-permute-start.21) | collective-permute-done | bytes 1572896 | tf_op jit(solution)/shard_map/ppermute | solution.py:28
  281.0 4.6 %convolution_convert_fusion.1 = bf16[384,2048]{1,0:T(8,128)(2,1)} fusion(bf16[2048,2048]{1,0:T(8,128)(2,1)S(1)} %bitcast.28, f32[384,2048]{1,0:T(8,128)S(1)} %copy-done.5, bf16[384,2048]{1,0:T(8,128)(2,1)S(1)} %collective-permute-done.21), kind=kOutput, calls=%fused_computation.5 | convolution fusion | flops 3224371200 | bytes 14680064 | tf_op jit(solution)/shard_map/dot_general | solution.py:32
  285.6 1.0 collective-permute-done.14
  286.6 0.5 slice.75
  287.8 1.4 collective-permute-start.15
  289.2 3.1 collective-permute-start.16
  293.0 9.2 %collective-permute-done.16 = bf16[64,1024]{1,0:T(8,128)(2,1)S(1)} collective-permute-done((bf16[64,1024]{1,0:T(8,128)(2,1)S(1)}, bf16[64,1024]{1,0:T(8,128)(2,1)S(1)}, u32[]{:S(2)}, u32[]{:S(2)}) %collective-permute-start.16) | collective-permute-done | bytes 131104 | tf_op jit(solution)/shard_map/ppermute | solution.py:28
  302.3 2.2 collective-permute-done.20
  304.5 0.8 pad_maximum_fusion.1
  (61 shorter events, 0.9 us)
Async XLA Ops:
  7.2 0.8 copy-start.8
  7.2 8.6 %copy-start.6 = (bf16[384,2048]{1,0:T(8,128)(2,1)S(1)}, bf16[384,2048]{1,0:T(8,128)(2,1)}, u32[]{:S(2)}) copy-start(bf16[384,2048]{1,0:T(8,128)(2,1)} %param.9) | copy-start | bytes 4718596
  7.2 95.6 %all-gather.2.cloned.1.call-start = ((), (), s32[]{:S(2)}) async-start(), calls=%async_computation.1 | async-start | bytes 10485760 | tf_op jit(solution)/shard_map/all_gather | solution.py:335
  8.5 13.7 %all-to-all-start = ((s32[8,1,16]{2,1,0:T(1,128)}), s32[8,1,16]{2,1,0:T(1,128)S(1)}, u32[]{:S(2)}, u32[]{:S(2)}) async-start(s32[8,1,16]{2,1,0:T(1,128)} %broadcast_in_dim.17), calls=%async_computation | async-start | bytes 8192 | tf_op jit(solution)/shard_map/all_to_all | solution.py:328
  24.7 2.4 copy-start.9
  24.7 2.5 copy-start.3
  24.7 69.7 %collective-permute-start = (bf16[384,2048]{0,1:T(8,128)(2,1)}, bf16[384,2048]{0,1:T(8,128)(2,1)}, u32[]{:S(2)}, u32[]{:S(2)}) collective-permute-start(bf16[384,2048]{0,1:T(8,128)(2,1)} %broadcast_select_fusion.2), channel_id=1, source_target_pairs={{0,16},{4,20},{8,24},{12,28},{16,0},{20,4},{24,8},{28,12},{1,17},{... | collective-permute-start | bytes 4718600 | tf_op jit(solution)/shard_map/ppermute | solution.py:28
  27.2 2.2 copy-start.2
  34.1 63.7 %copy-start = (bf16[512,2048]{1,0:T(8,128)(2,1)}, bf16[512,2048]{1,0:T(8,128)(2,1)S(1)}, u32[]{:S(2)}) copy-start(bf16[512,2048]{1,0:T(8,128)(2,1)S(1)} %get-tuple-element.21.x_ref.refs_4_) | copy-start | bytes 6291460
  34.1 82.2 %collective-permute-start.1 = (bf16[512,2048]{1,0:T(8,128)(2,1)}, bf16[512,2048]{1,0:T(8,128)(2,1)}, u32[]{:S(2)}, u32[]{:S(2)}) collective-permute-start(bf16[512,2048]{1,0:T(8,128)(2,1)} %get-tuple-element.23), channel_id=1, source_target_pairs={{0,4},{4,0},{8,12},{12,8},{16,20},{20,16},{24,28},{28,24},{1,5},{5... | collective-permute-start | bytes 6291464 | tf_op jit(solution)/shard_map/ppermute | solution.py:28
  34.8 84.1 %collective-permute-start.2 = (bf16[512,2048]{1,0:T(8,128)(2,1)}, bf16[512,2048]{1,0:T(8,128)(2,1)}, u32[]{:S(2)}, u32[]{:S(2)}) collective-permute-start(bf16[512,2048]{1,0:T(8,128)(2,1)} %get-tuple-element.25), channel_id=1, source_target_pairs={{0,8},{4,12},{8,0},{12,4},{16,24},{20,28},{24,16},{28,20},{1,9},{5... | collective-permute-start | bytes 6291464 | tf_op jit(solution)/shard_map/ppermute | solution.py:28
  35.5 124.6 %collective-permute-start.3 = (bf16[512,2048]{1,0:T(8,128)(2,1)}, bf16[512,2048]{1,0:T(8,128)(2,1)}, u32[]{:S(2)}, u32[]{:S(2)}) collective-permute-start(bf16[512,2048]{1,0:T(8,128)(2,1)} %get-tuple-element.27), channel_id=1, source_target_pairs={{0,12},{4,8},{8,4},{12,0},{16,28},{20,24},{24,20},{28,16},{1,13},{... | collective-permute-start | bytes 6291464 | tf_op jit(solution)/shard_map/ppermute | solution.py:28
  102.8 98.2 %collective-permute-start.8 = (bf16[1024,1152]{1,0:T(8,128)(2,1)}, bf16[1024,1152]{1,0:T(8,128)(2,1)S(1)}, u32[]{:S(2)}, u32[]{:S(2)}) collective-permute-start(bf16[1024,1152]{1,0:T(8,128)(2,1)} %bitcast.6), channel_id=1, source_target_pairs={{0,1},{1,0},{2,3},{3,2},{4,5},{5,4},{6,7},{7,6},{8,9},{9,8},{10,11... | collective-permute-start | bytes 7077896 | tf_op jit(solution)/shard_map/ppermute | solution.py:28
  102.8 7.4 %copy-start.10 = (bf16[2048,2048]{1,0:T(8,128)(2,1)S(1)}, bf16[2048,2048]{1,0:T(8,128)(2,1)}, u32[]{:S(2)}) copy-start(bf16[2048,2048]{1,0:T(8,128)(2,1)} %all-gather.2.cloned.1.call-done) | copy-start | bytes 25165828
  110.2 5.0 %copy-start.1 = (bf16[512,2048]{1,0:T(8,128)(2,1)S(1)}, bf16[512,2048]{1,0:T(8,128)(2,1)}, u32[]{:S(2)}) copy-start(bf16[512,2048]{1,0:T(8,128)(2,1)} %copy-done) | copy-start | bytes 6291460
  118.9 2.7 copy-start.7
  165.1 4.6 %collective-permute-start.4 = (f32[8,384]{1,0:T(8,128)S(1)}, f32[8,384]{1,0:T(8,128)S(1)}, u32[]{:S(2)}, u32[]{:S(2)}) collective-permute-start(f32[8,384]{1,0:T(8,128)S(1)} %pack_stats.1.mine_ref), channel_id=1, source_target_pairs={{0,16},{4,20},{8,24},{12,28},{16,0},{20,4},{24,8},{28,12},{1,17},{... | collective-permute-start | bytes 36872 | tf_op jit(solution)/shard_map/ppermute | solution.py:28
  178.0 6.9 %copy-start.4 = (f32[384,2048]{1,0:T(8,128)}, f32[384,2048]{1,0:T(8,128)S(1)}, u32[]{:S(2)}) copy-start(f32[384,2048]{1,0:T(8,128)S(1)} %get-tuple-element.36) | copy-start | bytes 9437188
  178.0 23.0 %collective-permute-start.9 = (bf16[384,2048]{1,0:T(8,128)(2,1)}, bf16[384,2048]{1,0:T(8,128)(2,1)}, u32[]{:S(2)}, u32[]{:S(2)}) collective-permute-start(bf16[384,2048]{1,0:T(8,128)(2,1)} %get-tuple-element.34.refs_0_), channel_id=1, source_target_pairs={{0,1},{1,0},{2,3},{3,2},{4,5},{5,4},{6,7},{7,6},{8,9},{9,8},{10,11... | collective-permute-start | bytes 4718600 | tf_op jit(solution)/shard_map/ppermute | solution.py:28
  178.0 23.0 %collective-permute-start.10 = (bf16[384,2048]{1,0:T(8,128)(2,1)}, bf16[384,2048]{1,0:T(8,128)(2,1)}, u32[]{:S(2)}, u32[]{:S(2)}) collective-permute-start(bf16[384,2048]{1,0:T(8,128)(2,1)} %get-tuple-element.35.refs_1_), channel_id=1, source_target_pairs={{0,1},{1,0},{2,3},{3,2},{4,5},{5,4},{6,7},{7,6},{8,9},{9,8},{10,11... | collective-permute-start | bytes 4718600 | tf_op jit(solution)/shard_map/ppermute | solution.py:28
  184.9 16.1 %collective-permute-start.11 = (bf16[384,2048]{1,0:T(8,128)(2,1)}, bf16[384,2048]{1,0:T(8,128)(2,1)}, u32[]{:S(2)}, u32[]{:S(2)}) collective-permute-start(bf16[384,2048]{1,0:T(8,128)(2,1)} %guest_rows.1.refs_2_), channel_id=1, source_target_pairs={{0,1},{1,0},{2,3},{3,2},{4,5},{5,4},{6,7},{7,6},{8,9},{9,8},{10,11... | collective-permute-start | bytes 4718600 | tf_op jit(solution)/shard_map/ppermute | solution.py:28
  204.7 25.6 %collective-permute-start.12 = (bf16[512,1024]{1,0:T(8,128)(2,1)S(1)}, bf16[512,1024]{1,0:T(8,128)(2,1)S(1)}, u32[]{:S(2)}, u32[]{:S(2)}) collective-permute-start(bf16[512,1024]{1,0:T(8,128)(2,1)S(1)} %weight_part.7), channel_id=1, source_target_pairs={{0,2},{1,3},{2,0},{3,1},{4,6},{5,7},{6,4},{7,5},{8,10},{9,11},{10,... | collective-permute-start | bytes 3145736 | tf_op jit(solution)/shard_map/ppermute | solution.py:28
  210.0 25.4 %collective-permute-start.17 = (bf16[512,1024]{1,0:T(8,128)(2,1)S(1)}, bf16[512,1024]{1,0:T(8,128)(2,1)S(1)}, u32[]{:S(2)}, u32[]{:S(2)}) collective-permute-start(bf16[512,1024]{1,0:T(8,128)(2,1)S(1)} %weight_part.9), channel_id=1, source_target_pairs={{0,4},{4,0},{8,12},{12,8},{16,20},{20,16},{24,28},{28,24},{1,5},{5... | collective-permute-start | bytes 3145736 | tf_op jit(solution)/shard_map/ppermute | solution.py:28
  210.7 70.3 %collective-permute-start.21 = (bf16[384,2048]{1,0:T(8,128)(2,1)}, bf16[384,2048]{1,0:T(8,128)(2,1)S(1)}, u32[]{:S(2)}, u32[]{:S(2)}) collective-permute-start(bf16[384,2048]{1,0:T(8,128)(2,1)} %guest_rows.1.refs_2_), channel_id=1, source_target_pairs={{0,16},{4,20},{8,24},{12,28},{16,0},{20,4},{24,8},{28,12},{1,17},{... | collective-permute-start | bytes 4718600 | tf_op jit(solution)/shard_map/ppermute | solution.py:28
  211.2 35.0 %collective-permute-start.5 = (f32[1,1]{1,0:T(1,128)}, f32[1,1]{1,0:T(1,128)}, u32[]{:S(2)}, u32[]{:S(2)}) collective-permute-start(f32[1,1]{1,0:T(1,128)} %slice.53), channel_id=1, source_target_pairs={{0,1},{1,0},{2,3},{3,2},{4,5},{5,4},{6,7},{7,6},{8,9},{9,8},{10,11... | collective-permute-start | bytes 20 | tf_op jit(solution)/shard_map/ppermute | solution.py:28
  235.4 45.6 %slice-start = ((s8[8388608]{0:T(1024)(128)(4,1)}), s8[4194304]{0:T(1024)(128)(4,1)S(1)}, s32[]{:S(2)}) async-start(s8[8388608]{0:T(1024)(128)(4,1)} %bitcast.27), calls=%async_computation.2 | async-start | bytes 8388608
  236.0 45.0 %slice-start.1 = ((s8[8388608]{0:T(1024)(128)(4,1)}), s8[4194304]{0:T(1024)(128)(4,1)S(1)}, s32[]{:S(2)}) async-start(s8[8388608]{0:T(1024)(128)(4,1)} %bitcast.27), calls=%async_computation.3 | async-start | bytes 8388608
  236.0 20.2 %collective-permute-start.13 = (bf16[256,1024]{1,0:T(8,128)(2,1)S(1)}, bf16[256,1024]{1,0:T(8,128)(2,1)S(1)}, u32[]{:S(2)}, u32[]{:S(2)}) collective-permute-start(bf16[256,1024]{1,0:T(8,128)(2,1)S(1)} %slice.97), channel_id=1, source_target_pairs={{0,4},{4,0},{8,12},{12,8},{16,20},{20,16},{24,28},{28,24},{1,5},{5... | collective-permute-start | bytes 1572872 | tf_op jit(solution)/shard_map/ppermute | solution.py:28
  236.7 19.7 %collective-permute-start.18 = (bf16[256,1024]{1,0:T(8,128)(2,1)S(1)}, bf16[256,1024]{1,0:T(8,128)(2,1)S(1)}, u32[]{:S(2)}, u32[]{:S(2)}) collective-permute-start(bf16[256,1024]{1,0:T(8,128)(2,1)S(1)} %slice.96), channel_id=1, source_target_pairs={{0,2},{1,3},{2,0},{3,1},{4,6},{5,7},{6,4},{7,5},{8,10},{9,11},{10,... | collective-permute-start | bytes 1572872 | tf_op jit(solution)/shard_map/ppermute | solution.py:28
  247.6 3.7 %collective-permute-start.6 = (f32[1,1]{1,0:T(1,128)}, f32[1,1]{1,0:T(1,128)}, u32[]{:S(2)}, u32[]{:S(2)}) collective-permute-start(f32[1,1]{1,0:T(1,128)} %add.48), channel_id=1, source_target_pairs={{0,2},{1,3},{2,0},{3,1},{4,6},{5,7},{6,4},{7,5},{8,10},{9,11},{10,... | collective-permute-start | bytes 20 | tf_op jit(solution)/shard_map/ppermute | solution.py:28
  251.9 3.7 %collective-permute-start.7 = (f32[1,1]{1,0:T(1,128)}, f32[1,1]{1,0:T(1,128)}, u32[]{:S(2)}, u32[]{:S(2)}) collective-permute-start(f32[1,1]{1,0:T(1,128)} %add.49), channel_id=1, source_target_pairs={{0,4},{4,0},{8,12},{12,8},{16,20},{20,16},{24,28},{28,24},{1,5},{5... | collective-permute-start | bytes 20 | tf_op jit(solution)/shard_map/ppermute | solution.py:28
  256.3 24.7 %copy-start.5 = (f32[384,2048]{1,0:T(8,128)S(1)}, f32[384,2048]{1,0:T(8,128)}, u32[]{:S(2)}) copy-start(f32[384,2048]{1,0:T(8,128)} %copy-done.4) | copy-start | bytes 9437188
  256.4 30.2 %collective-permute-start.14 = (bf16[128,1024]{1,0:T(8,128)(2,1)S(1)}, bf16[128,1024]{1,0:T(8,128)(2,1)S(1)}, u32[]{:S(2)}, u32[]{:S(2)}) collective-permute-start(bf16[128,1024]{1,0:T(8,128)(2,1)S(1)} %slice.99), channel_id=1, source_target_pairs={{0,8},{4,12},{8,0},{12,4},{16,24},{20,28},{24,16},{28,20},{1,9},{5... | collective-permute-start | bytes 786440 | tf_op jit(solution)/shard_map/ppermute | solution.py:28
  256.6 35.7 %collective-permute-start.19 = (bf16[128,1024]{1,0:T(8,128)(2,1)S(1)}, bf16[128,1024]{1,0:T(8,128)(2,1)S(1)}, u32[]{:S(2)}, u32[]{:S(2)}) collective-permute-start(bf16[128,1024]{1,0:T(8,128)(2,1)S(1)} %slice.98), channel_id=1, source_target_pairs={{0,8},{4,12},{8,0},{12,4},{16,24},{20,28},{24,16},{28,20},{1,9},{5... | collective-permute-start | bytes 786440 | tf_op jit(solution)/shard_map/ppermute | solution.py:28
  287.8 4.7 %collective-permute-start.15 = (f32[1,1]{1,0:T(1,128)}, f32[1,1]{1,0:T(1,128)}, u32[]{:S(2)}, u32[]{:S(2)}) collective-permute-start(f32[1,1]{1,0:T(1,128)} %add.55), channel_id=1, source_target_pairs={{0,8},{4,12},{8,0},{12,4},{16,24},{20,28},{24,16},{28,20},{1,9},{5... | collective-permute-start | bytes 20 | tf_op jit(solution)/shard_map/ppermute | solution.py:28
  289.2 13.0 %collective-permute-start.16 = (bf16[64,1024]{1,0:T(8,128)(2,1)S(1)}, bf16[64,1024]{1,0:T(8,128)(2,1)S(1)}, u32[]{:S(2)}, u32[]{:S(2)}) collective-permute-start(bf16[64,1024]{1,0:T(8,128)(2,1)S(1)} %slice.101), channel_id=1, source_target_pairs={{0,16},{4,20},{8,24},{12,28},{16,0},{20,4},{24,8},{28,12},{1,17},{... | collective-permute-start | bytes 393224 | tf_op jit(solution)/shard_map/ppermute | solution.py:28
  292.4 12.0 %collective-permute-start.20 = (bf16[64,1024]{1,0:T(8,128)(2,1)S(1)}, bf16[64,1024]{1,0:T(8,128)(2,1)S(1)}, u32[]{:S(2)}, u32[]{:S(2)}) collective-permute-start(bf16[64,1024]{1,0:T(8,128)(2,1)S(1)} %slice.100), channel_id=1, source_target_pairs={{0,16},{4,20},{8,24},{12,28},{16,0},{20,4},{24,8},{28,12},{1,17},{... | collective-permute-start | bytes 393224 | tf_op jit(solution)/shard_map/ppermute | solution.py:28
Sparse Core Ops, SparseCore 0:
  9.6 60.9 all-gather.1

commit v2 on v0

v2 whole, which is shorter than its diff:
```python
import functools
import math

import jax
import jax.numpy as jnp
from jax import lax
from jax.experimental import pallas as pl
from jax.experimental.pallas import tpu as pltpu
from jax.sharding import PartitionSpec as P

CAP = 2

SOFTMAX_TEMPER = 0.25

NEG_BIG = -1e30

TAIL = 16

F32 = jnp.float32
BF16 = jnp.bfloat16

VMEM_LIMIT = 24 * 1024 * 1024


def bits_of(size):
    return [1 << i for i in range(size.bit_length() - 1)]


def swap(x, axis, bit):
    return lax.ppermute(x, axis, [(i, i ^ bit) for i in range(lax.axis_size(axis))])


def move(x, bit_of):
    n_dp, n_fsdp = lax.axis_size("dp"), lax.axis_size("fsdp")
    pairs = [
        (i * n_fsdp + f, (i ^ bit_of(f)) * n_fsdp + f) for i in range(n_dp) for f in range(n_fsdp)
    ]
    return lax.ppermute(x, ("dp", "fsdp"), pairs)


def dot_t(a, b):
    return lax.dot_general(a, b, (((1,), (1,)), ((), ())), preferred_element_type=F32)


ANY = pl.BlockSpec(memory_space=pl.ANY)


def params(**kw):
    return pltpu.CompilerParams(vmem_limit_bytes=VMEM_LIMIT, **kw)


def pick_blocks(bank, ids, block_home, me, n_dp, n_fsdp):
    per_dev, block_rows, width = bank.shape
    named = ids.shape[1]
    span = per_dev * n_fsdp
    half = n_dp // 2
    rows = CAP * block_rows

    def kernel(ids_ref, home_ref, me_ref, bank_ref, own, *refs):
        guests, none, table, held, sem, whole_sem = refs[:half], *refs[half:]
        load = pltpu.make_async_copy(bank_ref, held, whole_sem)
        load.start()
        here = me_ref[0]
        none[...] = jnp.zeros(none.shape, none.dtype)
        base = here & half
        targets = [(here ^ k ^ half, guests[k], 0) for k in range(half)]
        targets += [(base + k, own, k * rows) for k in range(half)]
        for t, (group, _, _) in enumerate(targets):
            for p in range(CAP):
                table[t * CAP + p] = 0
            count = jnp.int32(0)
            for j in range(named):
                slot = home_ref[ids_ref[group, j]]
                mine = lax.div(slot, span) == here

                @pl.when(mine)
                def _():
                    table[t * CAP + jnp.minimum(count, CAP - 1)] = lax.rem(slot, per_dev)

                count = count + mine.astype(jnp.int32)
        load.wait()
        copies = []
        for t, (_, out, at) in enumerate(targets):
            for p in range(CAP):
                copy = pltpu.make_async_copy(
                    held.at[table[t * CAP + p]],
                    out.at[pl.ds(at + p * block_rows, block_rows)],
                    sem.at[len(copies)],
                )
                copy.start()
                copies.append(copy)
        for copy in copies:
            copy.wait()

    smem = pl.BlockSpec(memory_space=pltpu.SMEM)
    return pl.pallas_call(
        kernel,
        in_specs=[smem, smem, smem, ANY],
        out_specs=[ANY] * (half + 1) + [pl.BlockSpec(memory_space=pltpu.VMEM)],
        out_shape=[jax.ShapeDtypeStruct((half * rows, width), bank.dtype)]
        + [jax.ShapeDtypeStruct((rows, width), bank.dtype)] * half
        + [jax.ShapeDtypeStruct((8, 128), jnp.int32)],
        scratch_shapes=[
            pltpu.SMEM((n_dp * CAP,), jnp.int32),
            pltpu.VMEM(bank.shape, bank.dtype),
            pltpu.SemaphoreType.DMA((n_dp * CAP,)),
            pltpu.SemaphoreType.DMA,
        ],
        compiler_params=params(),
        cost_estimate=pl.CostEstimate(
            flops=0, bytes_accessed=4 * n_dp * rows * width, transcendentals=0
        ),
        name="pick_blocks",
    )(ids, block_home, me.reshape(1), bank)


def part_scores(emb, x, rows, held, scale, emb_p=None, before=None, pack=False, after=()):
    count, width = emb.shape
    sets = x.shape[0] // rows

    def kernel(*refs):
        refs = list(refs)
        held_ref = refs.pop(0) if held is not None else None
        emb_ref, x_ref = refs.pop(0), refs.pop(0)
        p_ref = refs.pop(0) if emb_p is not None else None
        before_ref = refs.pop(0) if before is not None else None
        del refs[: len(after)]
        out, stats, state = refs[0], refs[1], refs[-1]
        step = pl.program_id(0)

        def fold(s):
            groups = [s[:, i : i + 128] for i in range(0, s.shape[1], 128)]
            old = state[:, :128]
            top = functools.reduce(jnp.maximum, groups, old)
            total = state[:, 128:] * jnp.exp(old - top)
            state[:, :128] = top
            state[:, 128:] = total + sum(jnp.exp(g - top) for g in groups)

        @pl.when(step == 0)
        def _():
            if before is not None:
                state[...] = before_ref[...]
            else:
                state[:, :128] = jnp.full((count, 128), NEG_BIG, F32)
                state[:, 128:] = jnp.zeros((count, 128), F32)
            if emb_p is not None:
                inner = dot_t(emb_ref[...], p_ref[...]) * scale
                refs[2][...] = inner
                fold(inner)

        s = dot_t(emb_ref[...], x_ref[...]) * scale
        if held is not None:
            col = lax.broadcasted_iota(jnp.int32, s.shape, 1)
            s = jnp.where(col < held_ref[step], s, NEG_BIG)
        out[...] = s
        fold(s)

        @pl.when(step == sets - 1)
        def _():
            if pack:
                tops = state[:, :128].T
                top = jnp.max(tops, axis=0, keepdims=True)
                total = jnp.sum(state[:, 128:].T * jnp.exp(tops - top), axis=0, keepdims=True)
                row = lax.broadcasted_iota(jnp.int32, (8, count), 0)
                stats[...] = jnp.where(row == 0, top, total)
            else:
                stats[...] = state[...]

    whole = lambda a: pl.BlockSpec(a.shape, lambda i: (0, 0))
    args, in_specs = [emb, x], [whole(emb), pl.BlockSpec((rows, width), lambda i: (i, 0))]
    for a in (emb_p, before):
        if a is not None:
            args.append(a)
            in_specs.append(whole(a))
    args += after
    in_specs += [ANY] * len(after)
    if held is not None:
        args.insert(0, held)
        in_specs.insert(0, pl.BlockSpec(memory_space=pltpu.SMEM))
    stats_shape = (8, count) if pack else (count, 256)
    out_shape = [
        jax.ShapeDtypeStruct((count, x.shape[0]), F32),
        jax.ShapeDtypeStruct(stats_shape, F32),
    ]
    out_specs = [
        pl.BlockSpec((count, rows), lambda i: (0, i)),
        pl.BlockSpec(stats_shape, lambda i: (0, 0)),
    ]
    if emb_p is not None:
        out_shape.append(jax.ShapeDtypeStruct((count, count), F32))
        out_specs.append(pl.BlockSpec((count, count), lambda i: (0, 0)))
    return pl.pallas_call(
        kernel,
        grid=(sets,),
        in_specs=in_specs,
        out_specs=out_specs,
        out_shape=out_shape,
        scratch_shapes=[pltpu.VMEM((count, 256), F32)],
        compiler_params=params(),
        cost_estimate=pl.CostEstimate(
            flops=2 * count * x.shape[0] * width,
            bytes_accessed=2 * (count + x.shape[0]) * width,
            transcendentals=2 * count * x.shape[0],
        ),
        name="part_scores",
    )(*args)


def joined(mine, there):
    pad = jnp.zeros((120, mine.shape[1]), F32)
    m = jnp.concatenate([mine, pad], axis=0).T
    t = jnp.concatenate([there, pad], axis=0).T
    top = jnp.maximum(m[:, 0:1], t[:, 0:1])
    return top, m[:, 1:2] * jnp.exp(m[:, 0:1] - top) + t[:, 1:2] * jnp.exp(t[:, 0:1] - top)


def split_rows(x, cols):
    hi = x.astype(BF16).astype(F32)
    mid = (x - hi).astype(BF16).astype(F32)
    low = (x - hi - mid).astype(BF16).astype(F32)
    row = lax.broadcasted_iota(jnp.int32, (TAIL, cols), 0)
    wide = jnp.where(row == 0, hi, jnp.where(row == 1, mid, jnp.where(row == 2, low, 0.0)))
    return wide.astype(BF16)


def joined_rows(x):
    return jnp.sum(x[:, :128].astype(F32), axis=0, keepdims=True)[:, :1]


def guest_rows(mine, there, scores, guests, stays, scale, tile, after):
    count = mine.shape[1]
    n = len(guests)
    part, width = guests[0].shape
    tiles = width // tile

    def kernel(stays_ref, mine_ref, there_ref, *refs):
        s_refs, x_refs = refs[:n], refs[n : 2 * n]
        full, backs, probs = refs[2 * n + 1], refs[2 * n + 2 : -1], refs[-1]

        @pl.when(pl.program_id(0) == 0)
        def _():
            top, total = joined(mine_ref[...], there_ref[...])
            level = scale / total
            for k in range(n):
                probs[:, k * part : (k + 1) * part] = (
                    jnp.exp(s_refs[k][...] - top) * level
                ).astype(BF16)

        far = jnp.zeros((count, tile), F32)
        for k in range(n):
            far += jnp.dot(
                probs[:, k * part : (k + 1) * part], x_refs[k][...], preferred_element_type=F32
            )
        full[...] = far
        far = jnp.where(stays_ref[0] > 0, 0.0, far).astype(BF16)
        for i in range(tiles):

            @pl.when(pl.program_id(0) == i)
            def _():
                backs[i][...] = far

    whole = lambda a: pl.BlockSpec(a.shape, lambda i: (0, 0))
    return pl.pallas_call(
        kernel,
        grid=(tiles,),
        in_specs=[pl.BlockSpec(memory_space=pltpu.SMEM), whole(mine), whole(there)]
        + [whole(s) for s in scores]
        + [pl.BlockSpec((part, tile), lambda i: (0, i))] * n
        + [ANY],
        out_specs=[pl.BlockSpec((count, tile), lambda i: (0, i))]
        + [pl.BlockSpec((count, tile), lambda i: (0, 0))] * tiles,
        out_shape=[jax.ShapeDtypeStruct((count, width), F32)]
        + [jax.ShapeDtypeStruct((count, tile), BF16)] * tiles,
        scratch_shapes=[pltpu.VMEM((count, n * part), BF16)],
        compiler_params=params(),
        cost_estimate=pl.CostEstimate(
            flops=2 * count * n * part * width,
            bytes_accessed=2 * n * part * width + 6 * count * width,
            transcendentals=count * n * part,
        ),
        name="guest_rows",
    )(stays, mine, there, *scores, *guests, after)


def own_grads(mine, there, inner, own, scale):
    count = inner.shape[0]

    def kernel(mine_ref, there_ref, inner_ref, own_ref, out, near, near_t, loss):
        top, total = joined(mine_ref[...], there_ref[...])
        out[...] = (jnp.exp(own_ref[...] - top) * (scale / total)).astype(BF16)
        s = inner_ref[...]
        row = lax.broadcasted_iota(jnp.int32, s.shape, 0)
        col = lax.broadcasted_iota(jnp.int32, s.shape, 1)
        target = jnp.where(row == col, 1.0, 0.0)
        grad = (jnp.exp(s - top) / total - target) * scale
        near[...] = grad.astype(BF16)
        near_t[...] = grad.T.astype(BF16)
        rows = top + jnp.log(total) - jnp.sum(s * target, axis=1, keepdims=True)
        loss[...] = jnp.broadcast_to(jnp.sum(rows, axis=0, keepdims=True), loss.shape)

    wide = jax.ShapeDtypeStruct(own.shape, BF16)
    square = jax.ShapeDtypeStruct((count, count), BF16)
    return pl.pallas_call(
        kernel,
        out_shape=[wide, square, square, jax.ShapeDtypeStruct((8, 128), F32)],
        compiler_params=params(),
        cost_estimate=pl.CostEstimate(
            flops=8 * count * (own.shape[1] + count),
            bytes_accessed=6 * count * (own.shape[1] + count),
            transcendentals=count * (own.shape[1] + count),
        ),
        name="own_grads",
    )(mine, there, inner, own)


def grad_rows(p_own, near, near_t, own, emb_q, emb_p, far, backs, loss, stays, tile, start, before):
    count = near.shape[0]
    tiles = len(backs)
    total, width = own.shape

    def kernel(stays_ref, own_ref, near_ref, near_t_ref, x_ref, q_ref, p_ref, far_ref, *refs):
        back_refs, loss_ref = refs[:tiles], refs[tiles]
        outs, full = refs[-tiles - 1 : -1], refs[-1]
        acc = jnp.dot(near_ref[...], p_ref[...], preferred_element_type=F32)
        acc += jnp.dot(own_ref[...], x_ref[...], preferred_element_type=F32)
        acc += jnp.where(stays_ref[0] > 0, far_ref[...], 0.0)
        full[...] = acc
        pos = jnp.dot(near_t_ref[...], q_ref[...], preferred_element_type=F32).astype(BF16)
        acc = acc.astype(BF16)
        tail = split_rows(loss_ref[0:1, 0:1], tile)
        for i in range(tiles):

            @pl.when(pl.program_id(0) == i)
            def _():
                outs[i][:count] = acc
                outs[i][count : 2 * count] = pos
                outs[i][2 * count : 3 * count] = back_refs[i][...]
                outs[i][3 * count :] = tail

    whole = lambda a: pl.BlockSpec(a.shape, lambda i: (0, 0))
    cut = lambda r: pl.BlockSpec((r, tile), lambda i: (0, start + i))
    args = [stays, p_own, near, near_t, own, emb_q, emb_p, far, *backs, loss, *before]
    return pl.pallas_call(
        kernel,
        grid=(tiles,),
        in_specs=[pl.BlockSpec(memory_space=pltpu.SMEM)]
        + [whole(p_own), whole(near), whole(near_t), cut(total)]
        + [cut(count)] * 3
        + [whole(b) for b in backs]
        + [whole(loss)]
        + [ANY] * len(before),
        out_specs=[pl.BlockSpec((3 * count + TAIL, tile), lambda i: (0, 0))] * tiles
        + [cut(count)],
        out_shape=[jax.ShapeDtypeStruct((3 * count + TAIL, tile), BF16)] * tiles
        + [jax.ShapeDtypeStruct((count, width), F32)],
        input_output_aliases={len(args) - len(before) + i: tiles + i for i in range(len(before))},
        compiler_params=params(),
        cost_estimate=pl.CostEstimate(
            flops=2 * count * (total + 2 * count) * tile * tiles,
            bytes_accessed=(2 * total + 20 * count) * tile * tiles,
            transcendentals=0,
        ),
        name="grad_rows",
    )(*args)


def last_product(pieces, at, count, weight, tile, full=None, after=()):
    kin, width = weight.shape
    n = len(pieces)
    cols = pieces[0].shape[1]

    def kernel(w_ref, *refs):
        out, rows = refs[-2], refs[-1]

        @pl.when(pl.program_id(0) == 0)
        def _():
            for k in range(n):
                piece = refs[k][...]
                if full is not None:
                    piece = refs[n][:, k * cols : (k + 1) * cols] + piece.astype(F32)
                rows[:, k * cols : (k + 1) * cols] = piece.astype(BF16)

        out[...] = dot_t(rows[...], w_ref[...]).astype(BF16)

    args = [weight, *pieces]
    in_specs = [pl.BlockSpec((tile, width), lambda i: (i, 0))]
    in_specs += [pl.BlockSpec((count, cols), lambda i: (at, 0))] * n
    if full is not None:
        args.append(full)
        in_specs.append(pl.BlockSpec((count, width), lambda i: (0, 0)))
    return pl.pallas_call(
        kernel,
        grid=(kin // tile,),
        in_specs=in_specs + [ANY] * len(after),
        out_specs=pl.BlockSpec((count, tile), lambda i: (0, i)),
        out_shape=jax.ShapeDtypeStruct((count, kin), BF16),
        scratch_shapes=[pltpu.VMEM((count, width), BF16)],
        compiler_params=params(),
        cost_estimate=pl.CostEstimate(
            flops=2 * count * width * kin,
            bytes_accessed=2 * width * kin + 4 * count * (width + kin),
            transcendentals=0,
        ),
        name="last_product",
    )(*args, *after)


def weight_part(left, at, rights, base, rows_at, dtype, tails=(), after=()):
    depth, tile = left.shape[1], rights[0].shape[1]
    n, m = len(rights), len(rows_at)
    quarter = left.shape[0] // (8 if at is not None else 4)
    at = at or 0
    first, step = rows_at[0], rows_at[1] - rows_at[0]
    total = m * quarter

    def kernel(left_ref, *refs):
        out = refs[-2] if tails else refs[-1]
        if tails:
            rows = pl.ds(pl.multiple_of(pl.program_id(0) * quarter, quarter), quarter)
        else:
            rows = slice(None)
        for k in range(n):
            cols = slice(k * tile, (k + 1) * tile)
            acc = jnp.dot(left_ref[...], refs[k][...], preferred_element_type=F32)
            if base is not None:
                acc += refs[n][:, cols]
            out[rows, cols] = acc.astype(dtype)
        if tails:
            loss = sum(joined_rows(r[...]) for r in refs[n + 1 : n + 1 + len(tails)])
            out[total:, :] = split_rows(loss, n * tile)
            refs[-1][...] = jnp.broadcast_to(loss, refs[-1].shape)

    in_specs = [pl.BlockSpec((quarter, depth), lambda i: (at + first + step * i, 0))]
    in_specs += [pl.BlockSpec((depth, tile), lambda i: (0, 0))] * n
    args = [left, *rights]
    if base is not None:
        in_specs.append(pl.BlockSpec((quarter, n * tile), lambda i: (first + step * i, 0)))
        args.append(base)
    for t in tails:
        in_specs.append(pl.BlockSpec((TAIL, tile), lambda i: (depth // TAIL, 0)))
        args.append(t)
    in_specs += [ANY] * len(after)
    args += after
    if tails:
        shape = (total + TAIL, n * tile)
        out_shape = [jax.ShapeDtypeStruct(shape, dtype), jax.ShapeDtypeStruct((8, 128), F32)]
        out_specs = [pl.BlockSpec(s.shape, lambda i: (0, 0)) for s in out_shape]
    else:
        out_shape = jax.ShapeDtypeStruct((total, n * tile), dtype)
        out_specs = pl.BlockSpec((quarter, n * tile), lambda i: (i, 0))
    return pl.pallas_call(
        kernel,
        grid=(m,),
        in_specs=in_specs,
        out_specs=out_specs,
        out_shape=out_shape,
        compiler_params=params(),
        cost_estimate=pl.CostEstimate(
            flops=2 * total * n * depth * tile,
            bytes_accessed=2 * depth * (n * tile + total) + 8 * total * n * tile,
            transcendentals=0,
        ),
        name="weight_part",
    )(*args)


def fold_stage(keep, got, loss=None, after=()):
    rows, cols = keep.shape
    mid = rows // 2

    def kernel(keep_ref, got_ref, *refs):
        if loss is None:
            send, rest = refs[-2:]
        else:
            send, rest, state = refs[-3:]
            value = refs[0][0:1, 0:1] + joined_rows(got_ref[rows:])
            state[...] = jnp.broadcast_to(value, state.shape)
            send[mid:] = split_rows(value, cols)
        send[:mid] = (keep_ref[:mid] + got_ref[:mid].astype(F32)).astype(BF16)
        rest[...] = keep_ref[mid:] + got_ref[mid:rows].astype(F32)

    args = [keep, got] + ([loss] if loss is not None else [])
    in_specs = [pl.BlockSpec(memory_space=pltpu.VMEM)] * len(args)
    args += after
    in_specs += [ANY] * len(after)
    out_shape = [
        jax.ShapeDtypeStruct((mid + (TAIL if loss is not None else 0), cols), BF16),
        jax.ShapeDtypeStruct((rows - mid, cols), F32),
    ]
    if loss is not None:
        out_shape.append(jax.ShapeDtypeStruct((8, 128), F32))
    return pl.pallas_call(
        kernel,
        in_specs=in_specs,
        out_shape=out_shape,
        compiler_params=params(),
        cost_estimate=pl.CostEstimate(
            flops=rows * cols, bytes_accessed=9 * rows * cols, transcendentals=0
        ),
        name="fold_stage",
    )(*args)


def last_stage(keeps, gots, loss):
    rows, cols = keeps[0].shape

    def kernel(keep0, got0, keep1, got1, loss_ref, out, state):
        out[:, :cols] = keep0[...] + got0[:rows].astype(F32)
        out[:, cols:] = keep1[...] + got1[:rows].astype(F32)
        state[...] = loss_ref[...] + joined_rows(got0[rows:])

    return pl.pallas_call(
        kernel,
        out_shape=[
            jax.ShapeDtypeStruct((rows, 2 * cols), F32),
            jax.ShapeDtypeStruct((8, 128), F32),
        ],
        compiler_params=params(),
        name="last_stage",
    )(keeps[0], gots[0], keeps[1], gots[1], loss)


def body(queries, passages, weight, bank, neg_ids, block_home):
    count, kin = queries.shape
    width = weight.shape[1]
    scale = 1.0 / (SOFTMAX_TEMPER * math.sqrt(width))
    n_dp = lax.axis_size("dp")
    n_fsdp = lax.axis_size("fsdp")
    devices = n_dp * n_fsdp
    block_rows = bank.shape[1]
    named = neg_ids.shape[1]
    half = n_dp // 2
    me = lax.axis_index("dp")
    core = lax.axis_index("fsdp") % 2
    linear = me * n_fsdp + lax.axis_index("fsdp")

    trip = lambda f: half if f % 2 == 0 else 0

    ids = lax.all_to_all(
        jnp.broadcast_to(neg_ids, (n_dp, named)), "dp", split_axis=0, concat_axis=0, tiled=True
    )
    leaving = jnp.where(ids[0, 0] < 0, jnp.zeros_like(queries), queries)
    visit = move(leaving, trip)
    own, *guests, zero = pick_blocks(bank, ids, block_home, me, n_dp, n_fsdp)
    guests = [
        move(g, lambda f, k=k: k if f % 2 == 0 else k ^ half) for k, g in enumerate(guests)
    ]
    sides = [list(range(half)), list(range(half, n_dp))]
    own = lax.all_to_all(
        own, "dp", split_axis=0, concat_axis=0, tiled=True, axis_index_groups=sides
    )
    late = jnp.where(zero[0, 0] < 0, jnp.zeros_like(passages), passages)

    full_weight = lax.all_gather(weight, "fsdp", axis=0, tiled=True)
    emb_q = jnp.dot(queries, full_weight, preferred_element_type=F32).astype(BF16)
    emb_p = jnp.dot(passages, full_weight, preferred_element_type=F32).astype(BF16)
    emb_v = jnp.dot(visit, full_weight, preferred_element_type=F32).astype(BF16)

    f_bits = [("fsdp", b) for b in bits_of(n_fsdp)]
    d_bits = [("dp", b) for b in bits_of(n_dp)]
    stages = [f_bits[1], d_bits[0]] + f_bits[2:] + d_bits[1:]
    mask = []
    for p in range(devices // 2):
        m = 0
        for s, (axis, bit) in enumerate(stages):
            if not (p >> (len(stages) - 1 - s)) & 1:
                m |= bit if axis == "fsdp" else bit * n_fsdp
        mask.append(m)
    mask = jnp.array(mask, jnp.int32)
    hidden_t = jnp.concatenate([queries, late, visit], axis=0).T
    hidden_t = hidden_t.reshape(devices, kin // devices, -1)
    order = linear ^ jnp.concatenate([mask ^ 1, mask])
    left = jnp.take(hidden_t, order, axis=0).reshape(kin, -1)
    left_in = swap(left[: kin // 2], *f_bits[0])

    masked = n_dp * CAP > named
    own_held, guest_held = None, [None] * half
    if masked:
        owner = block_home[ids] // bank.shape[0] // n_fsdp
        held = lambda g, by: (jnp.sum(owner[g] == by) * block_rows).astype(jnp.int32)
        far = jnp.where(core == 0, 0, half)
        own_held = jnp.stack([held(me, (me & half) + k) for k in range(half)])
        guest_held = [held(me ^ half ^ far, me ^ k ^ far).reshape(1) for k in range(half)]
    rows = CAP * block_rows
    s_own, own_stats, inner = part_scores(
        emb_q, own, rows, own_held, scale, emb_p=emb_p, pack=True
    )
    their_stats = move(own_stats, trip)
    s_guest, stats = [], None
    for k, x in enumerate(guests):
        after = (inner,) if k == half // 2 else ()
        s, stats = part_scores(
            emb_v, x, rows, guest_held[k], scale, before=stats, pack=k == half - 1, after=after
        )
        s_guest.append(s)

    far_stats = move(stats, trip)
    tile = width // 4
    stays = core.astype(jnp.int32).reshape(1)
    far, *backs = guest_rows(
        stats, their_stats, s_guest, guests, stays, scale, tile, left_in
    )
    home = [move(r, trip) for r in backs]
    p_own, near, near_t, loss = own_grads(own_stats, far_stats, inner, s_own, scale)
    rows, kept = [], ()
    for i in range(2):
        *g, full = grad_rows(
            p_own,
            near,
            near_t,
            own,
            emb_q,
            emb_p,
            far,
            backs[2 * i : 2 * i + 2],
            loss,
            stays,
            tile,
            2 * i,
            kept,
        )
        rows += g
        kept = (full,)
    far_rows = [swap(r, *f_bits[0]) for r in rows]

    orders = [stages, [stages[1], stages[0]] + stages[2:]]
    give = ((0, 1), (0, 2))
    hold = ((2, 3), (1, 3))
    every = (0, 1, 2, 3)
    bases = [
        weight_part(left, 4, rows[:2], None, every, F32),
        weight_part(left, 4, rows[2:], None, every, F32, after=(home[0],)),
    ]
    got = [far_rows[:2], far_rows[2:]]
    send, loss = weight_part(
        left_in, None, got[0], bases[0], give[0], BF16, tails=(rows[0], far_rows[0])
    )
    sends = [send, weight_part(left_in, None, got[1], bases[1], give[1], BF16, after=(home[1],))]
    back_p = last_product(rows, 1, count, full_weight, tile, after=(sends[1],))
    keeps = [
        weight_part(left_in, None, got[0], bases[0], hold[0], F32),
        weight_part(left_in, None, got[1], bases[1], hold[1], F32),
    ]
    waits = {(0, 0): (back_p, keeps[1]), (0, 1): (home[2], home[3])}
    for s in range(len(stages)):
        gots = [swap(sends[i], *orders[i][s]) for i in range(2)]
        if s + 1 < len(stages):
            send0, keep0, loss = fold_stage(keeps[0], gots[0], loss, waits.get((s, 0), ()))
            send1, keep1 = fold_stage(keeps[1], gots[1], after=waits.get((s, 1), ()))
            sends, keeps = [send0, send1], [keep0, keep1]
    back_q = last_product(home, 0, count, full_weight, tile, full=full, after=tuple(sends))
    grad_weight, loss = last_stage(keeps, gots, loss)
    loss = loss[0, 0] / (count * devices)
    return (loss, grad_weight, back_q, back_p)


def solution(mesh):
    return jax.shard_map(
        body,
        mesh=mesh,
        in_specs=(
            P(("dp", "fsdp"), None),
            P(("dp", "fsdp"), None),
            P("fsdp", None),
            P(("dp", "fsdp"), None, None),
            P(("dp", "fsdp"), None),
            P(),
        ),
        out_specs=(P(), P(("dp", "fsdp"), None), P(("dp", "fsdp"), None), P(("dp", "fsdp"), None)),
        check_vma=False,
    )
```

time: 463 us -> 279 us (0.60)
  waiting for transfers between devices: 295 us -> 92.4 us
  Pallas kernels: 0 us -> 55.3 us
  starting transfers between devices: 12.6 us -> 60.2 us
  blocking collectives: 45.7 us -> 0 us
  matrix products: 44.9 us -> 20.4 us
  other arithmetic: 19.4 us -> 10.8 us
  local copies, waits for them, and re-layouts: 28.3 us -> 20.5 us
    all_to_all x2, waiting for transfers between devices: 142 us -> 6.39 us  [the longest x1 6.39 us: body(): lax.all_to_all(jnp.broadcast_to(neg_ids, (n_dp, named)), 'dp', split_axis...]
    reduce_scatter x1 -> x0, waiting for transfers between devices: 121 us -> none  [body(): lax.psum_scatter(lax.dot_general(hidden, grad_rows, (((0,), (0,)), ((), (...]
    ppermute x0 -> x24, waiting for transfers between devices: none -> 85.4 us  [the longest x11 59.6 us: move(): return lax.ppermute(x, ('dp', 'fsdp'), pairs)]
    pallas_call x0 -> x25, Pallas kernels: none -> 55.3 us  [the longest x6 13.7 us: weight_part(): pl.pallas_call(kernel, grid=(m,), in_specs=in_specs, out_specs=out_specs,...]
    ppermute x0 -> x24, starting transfers between devices: none -> 47.8 us  [the longest x11 36.2 us: move(): return lax.ppermute(x, ('dp', 'fsdp'), pairs)]
    psum x1 -> x0, blocking collectives: 45.7 us -> none  [body(): loss = lax.psum(loss_local, ('dp', 'fsdp')) / (count_q * devices_all)]
    all_gather x1, waiting for transfers between devices: 31 us -> 0.01 us  [body(): full_weight = lax.all_gather(weight, 'fsdp', axis=0, tiled=True)]
    dot_general x8 -> x3, matrix products: 44.9 us -> 20.4 us  [the longest x1 8.56 us: body(): jnp.dot(passages, full_weight, preferred_element_type=F32).astype(BF16)]
  transfers between devices with their start and end apart: 4 -> 27, of which waited for: 4 -> 10; matrix products, arithmetic and copies ran while one was open for 10% -> 15% of each run, Pallas kernels for 0% -> 20%
where the time goes in v2:
time: 279 us; the launch traced here: 277 us
  waiting for transfers between devices  92.4 us (33%)
  starting transfers between devices  60.2 us (22%)
  Pallas kernels  55.3 us (20%)
  local copies, waits for them, and re-layouts  20.5 us (7%)
  matrix products  20.4 us (7%)
  between operations  17.6 us (6%)
  other arithmetic  10.8 us (4%)
    ppermute x11, waiting for transfers between devices, move(): return lax.ppermute(x, ('dp', 'fsdp'), pairs)  59.6 us
    ppermute x11, starting transfers between devices, move(): return lax.ppermute(x, ('dp', 'fsdp'), pairs)  36.2 us
    ppermute x13, waiting for transfers between devices, swap(): lax.ppermute(x, axis, [(i, i ^ bit) for i in range(lax.axis_size(axis))])  25.7 us
    pallas_call x6, Pallas kernels, weight_part(): pl.pallas_call(kernel, grid=(m,), in_specs=in_specs, out_specs=out_specs,...  13.7 us
    unnamed x40, local copies, waits for them, and re-layouts  12.6 us
    pallas_call x5, Pallas kernels, part_scores(): pl.pallas_call(kernel, grid=(sets,), in_specs=in_specs, out_specs=out_spe...  12.1 us
    ppermute x13, starting transfers between devices, swap(): lax.ppermute(x, axis, [(i, i ^ bit) for i in range(lax.axis_size(axis))])  11.7 us
    pallas_call x2, Pallas kernels, last_product(): pl.pallas_call(kernel, grid=(kin // tile,), in_specs=in_specs + [ANY] * l...  10 us
  transfers between devices with their start and end apart: 27, of which 10 were waited for; matrix products, arithmetic and copies ran while one was open for 15% of the time, Pallas kernels for 20%

profile of v2, /device:TPU:0, one launch (start us, length us, event | category | flops | bytes accessed | tf_op | source)
XLA Modules:
  0.0 277.2 jit_solution(16098215340893420870)
XLA Ops:
  7.2 0.7 all-gather.2.cloned.1.call-update
  8.5 7.3 %all-to-all-start = ((s32[8,1,16]{2,1,0:T(1,128)}), s32[8,1,16]{2,1,0:T(1,128)S(1)}, u32[]{:S(2)}, u32[]{:S(2)}) async-start(s32[8,1,16]{2,1,0:T(1,128)} %broadcast_in_dim.24), calls=%async_computation | async-start | bytes 8192 | tf_op jit(solution)/shard_map/all_to_all | solution.py:539
  15.8 6.4 %all-to-all-done = s32[8,1,16]{2,1,0:T(1,128)S(1)} async-done(((s32[8,1,16]{2,1,0:T(1,128)}), s32[8,1,16]{2,1,0:T(1,128)S(1)}, u32[]{:S(2)}, u32[]{:S(2)}) %all-to-all-start) | async-done | bytes 544 | tf_op jit(solution)/shard_map/all_to_all | solution.py:539
  22.2 3.3 %copy-done.6 = bf16[8,128,2048]{2,1,0:T(8,128)(2,1)S(1)} copy-done((bf16[8,128,2048]{2,1,0:T(8,128)(2,1)S(1)}, bf16[8,128,2048]{2,1,0:T(8,128)(2,1)}, u32[]{:S(2)}) %copy-start.6) | copy-done | bytes 4194328
  25.5 3.7 %pick_blocks.1 = (bf16[1024,2048]{1,0:T(8,128)(2,1)S(1)}, bf16[256,2048]{1,0:T(8,128)(2,1)}, bf16[256,2048]{1,0:T(8,128)(2,1)}, bf16[256,2048]{1,0:T(8,128)(2,1)...) custom-call(s32[8,16]{1,0:T(8,128)S(1)} %bitcast.27, s32[256]{0:T(256)S(1)} %copy-done.8, s32[1]{0:T(128)} %bitcast.2.me_ref, ...), custom_call_target="tpu_custom_call" | custom-call | bytes 16777216 | tf_op jit(solution)/shard_map/pick_blocks/pallas_call | solution.py:96
  29.3 2.0 copy-done.7
  31.3 5.0 %all-to-all-start.1 = ((bf16[4,256,2048]{2,1,0:T(8,128)(2,1)}), bf16[4,256,2048]{2,1,0:T(8,128)(2,1)}, u32[]{:S(2)}, u32[]{:S(2)}) async-start(bf16[4,256,2048]{2,1,0:T(8,128)(2,1)} %bitcast.26), calls=%async_computation.1 | async-start | bytes 8388608 | tf_op jit(solution)/shard_map/all_to_all | solution.py:549
  36.3 0.9 copy.17
  38.4 1.3 broadcast_select_fusion
  39.7 2.1 collective-permute-start
  41.9 1.6 copy.15
  43.6 9.4 %collective-permute-start.5 = (bf16[256,2048]{1,0:T(8,128)(2,1)}, bf16[256,2048]{1,0:T(8,128)(2,1)}, u32[]{:S(2)}, u32[]{:S(2)}) collective-permute-start(bf16[256,2048]{1,0:T(8,128)(2,1)} %get-tuple-element.61), channel_id=1, source_target_pairs={{0,0},{1,17},{2,2},{3,19},{4,4},{5,21},{6,6},{7,23},{8,8},{9,25},{... | collective-permute-start | bytes 3145736 | tf_op jit(solution)/shard_map/ppermute | solution.py:38
  53.1 2.0 collective-permute-start.4
  55.1 1.4 collective-permute-start.3
  57.7 1.6 broadcast_select_fusion.1
  59.3 57.1 %collective-permute-done = bf16[384,2048]{0,1:T(8,128)(2,1)} collective-permute-done((bf16[384,2048]{0,1:T(8,128)(2,1)}, bf16[384,2048]{0,1:T(8,128)(2,1)}, u32[]{:S(2)}, u32[]{:S(2)}) %collective-permute-start) | collective-permute-done | bytes 1572896 | tf_op jit(solution)/shard_map/ppermute | solution.py:38
  116.4 3.5 %pad_maximum_fusion = bf16[1152,2048]{0,1:T(8,128)(2,1)} fusion(bf16[384,2048]{0,1:T(8,128)(2,1)} %collective-permute-done, bf16[384,2048]{0,1:T(8,128)(2,1)S(1)} %broadcast_select_fusion.1, bf16[384,2048]{0,1:T(8,128)(2,1)S(1)} %copy.17), kind=kLoop, calls=%fused_computation.1 | loop fusion | flops 14155776 | bytes 9437184 | tf_op jit(solution)/shard_map/concatenate | solution.py:570
  119.9 5.6 %gather_fusion = bf16[32,64,1152]{2,1,0:T(8,128)(2,1)} fusion(bf16[32,64,1152]{2,1,0:T(8,128)(2,1)} %bitcast.31, s32[1024]{0:T(1024)S(1)} %pad_clamp_fusion), kind=kCustom, calls=%fused_computation | custom fusion | bytes 9437312 | tf_op jit(solution)/shard_map/jit(_take)/gather | solution.py:573
  125.5 3.4 %slice_select_fusion = bf16[16,64,1152]{2,1,0:T(8,128)(2,1)} fusion(bf16[32,64,1152]{2,1,0:T(8,128)(2,1)} %gather_fusion, pred[16]{0:T(512)(128)(4,1)S(1)} %bitcast.32), kind=kLoop, calls=%fused_computation.6 | loop fusion | flops 1179648 | bytes 4718608 | tf_op jit(solution)/shard_map/jit(_take)/select_n | solution.py:573
  128.9 8.6 %convolution_convert_fusion.1.refs_2_.p_ref = bf16[384,2048]{1,0:T(8,128)(2,1)} fusion(bf16[384,2048]{1,0:T(8,128)(2,1)} %param.8, bf16[2048,2048]{1,0:T(8,128)(2,1)} %all-gather.2.cloned.1.call-done.w_ref), kind=kOutput, calls=%fused_computation.4 | convolution fusion | flops 3222011904 | bytes 11534336 | tf_op jit(solution)/shard_map/dot_general | solution.py:556
  137.5 4.5 %convolution_convert_fusion.2.refs_0_.q_ref = bf16[384,2048]{1,0:T(8,128)(2,1)} fusion(bf16[384,2048]{1,0:T(8,128)(2,1)S(1)} %copy-done.11, bf16[2048,2048]{1,0:T(8,128)(2,1)S(1)} %copy-done), kind=kOutput, calls=%fused_computation.5 | convolution fusion | flops 3222011904 | bytes 11534336 | tf_op jit(solution)/shard_map/dot_general | solution.py:555
  142.0 1.4 copy-done.1
  143.4 1.4 copy-done.3
  144.8 5.8 %part_scores.5 = (f32[384,1024]{1,0:T(8,128)S(1)}, f32[8,384]{1,0:T(8,128)S(1)}, f32[384,384]{1,0:T(8,128)S(1)}) custom-call(bf16[384,2048]{1,0:T(8,128)(2,1)S(1)} %copy-done.3, bf16[1024,2048]{1,0:T(8,128)(2,1)} %bitcast.11.refs_1_.x_ref, bf16[384,2048]{1,0:T(8,128)(2,1)S(1)} %copy-done.1), custom_call_target="tpu_custom_call" | custom-call | flops 1610612736 | bytes 5767168 | tf_op jit(solution)/shard_map/part_scores/pallas_call | solution.py:192
  150.5 7.3 %convolution_convert_fusion.refs_0_ = bf16[384,2048]{1,0:T(8,128)(2,1)S(1)} fusion(bf16[384,2048]{0,1:T(8,128)(2,1)} %collective-permute-done, bf16[2048,2048]{1,0:T(8,128)(2,1)} %all-gather.2.cloned.1.call-done.w_ref), kind=kOutput, calls=%fused_computation.3 | convolution fusion | flops 3222011904 | bytes 11534336 | tf_op jit(solution)/shard_map/dot_general | solution.py:557
  157.9 5.3 %collective-permute-start.7 = (f32[8,384]{1,0:T(8,128)S(1)}, f32[8,384]{1,0:T(8,128)S(1)}, u32[]{:S(2)}, u32[]{:S(2)}) collective-permute-start(f32[8,384]{1,0:T(8,128)S(1)} %get-tuple-element.57.mine_ref), channel_id=1, source_target_pairs={{0,16},{1,1},{2,18},{3,3},{4,20},{5,5},{6,22},{7,7},{8,24},{9,9},{... | collective-permute-start | bytes 36872 | tf_op jit(solution)/shard_map/ppermute | solution.py:38
  163.3 1.9 part_scores.6
  165.1 0.6 part_scores.7
  165.8 1.9 part_scores.8
  167.7 2.0 part_scores.9
  169.6 2.1 collective-permute-start.6
  171.8 5.1 %guest_rows.1 = (f32[384,2048]{1,0:T(8,128)S(1)}, bf16[384,512]{1,0:T(8,128)(2,1)S(1)}, bf16[384,512]{1,0:T(8,128)(2,1)S(1)}, bf16[384,512]{1,0:T(8,128)(2,1)S(1)}, bf16[384,512]{1,0:T(8,128)(2,1)S(1)}) custom-call(s32[1]{0:T(128)} %bitcast.9.stays_ref, f32[8,384]{1,0:T(8,128)S(1)} %get-tuple-element.66.mine_ref, ...), custom_call_target="tpu_custom_call" | custom-call | flops 1610612736 | bytes 8912896 | tf_op jit(solution)/shard_map/guest_rows/pallas_call | solution.py:263
  176.9 5.0 %collective-permute-start.13 = (bf16[384,512]{1,0:T(8,128)(2,1)S(1)}, bf16[384,512]{1,0:T(8,128)(2,1)S(1)}, u32[]{:S(2)}, u32[]{:S(2)}) collective-permute-start(bf16[384,512]{1,0:T(8,128)(2,1)S(1)} %get-tuple-element.76.refs_0_), channel_id=1, source_target_pairs={{0,16},{1,1},{2,18},{3,3},{4,20},{5,5},{6,22},{7,7},{8,24},{9,9},{... | collective-permute-start | bytes 1179656 | tf_op jit(solution)/shard_map/ppermute | solution.py:38
  181.9 1.5 own_grads.1
  183.4 3.6 %grad_rows.2 = (bf16[1168,512]{1,0:T(8,128)(2,1)S(1)}, bf16[1168,512]{1,0:T(8,128)(2,1)S(1)}, f32[384,2048]{1,0:T(8,128)S(1)}) custom-call(s32[1]{0:T(128)} %bitcast.9.stays_ref, bf16[384,1024]{1,0:T(8,128)(2,1)S(1)} %get-tuple-element.68.own_ref, bf16[384,384]{1,0:T(8,128)(2,1)S(1)} %get-tuple-element.69.near_ref, ...), custom_call_target="tpu_custom_call" | custom-call | flops 1409286144 | bytes 9961472 | tf_op jit(solution)/shard_map/grad_rows/pallas_call | solution.py:343
  187.1 3.8 %grad_rows.3 = (bf16[1168,512]{1,0:T(8,128)(2,1)S(1)}, bf16[1168,512]{1,0:T(8,128)(2,1)S(1)}, f32[384,2048]{1,0:T(8,128)S(1)}) custom-call(s32[1]{0:T(128)} %bitcast.9.stays_ref, bf16[384,1024]{1,0:T(8,128)(2,1)S(1)} %get-tuple-element.68.own_ref, bf16[384,384]{1,0:T(8,128)(2,1)S(1)} %get-tuple-element.69.near_ref, ...), custom_call_target="tpu_custom_call", output_to_operand_aliasing={{2}: (11, {})} | custom-call | flops 1409286144 | bytes 9961472 | tf_op jit(solution)/shard_map/grad_rows/pallas_call | solution.py:343
  191.9 1.1 bitcast_select_fusion.left_ref
  193.0 1.9 collective-permute-start.14
  194.9 3.4 %weight_part.6.refs_2_ = f32[1024,1024]{1,0:T(8,128)S(1)} custom-call(bf16[2048,1152]{1,0:T(8,128)(2,1)S(1)} %bitcast_select_fusion.left_ref, bf16[1168,512]{1,0:T(8,128)(2,1)S(1)} %get-tuple-element.79.refs_0_.refs_3_, bf16[1168,512]{1,0:T(8,128)(2,1)S(1)} %get-tuple-element.80.refs_1_), custom_call_target="tpu_custom_call" | custom-call | flops 2415919104 | bytes 13107200 | tf_op jit(solution)/shard_map/weight_part/pallas_call | solution.py:451
  198.3 3.4 %weight_part.9.refs_2_ = f32[1024,1024]{1,0:T(8,128)S(1)} custom-call(bf16[2048,1152]{1,0:T(8,128)(2,1)S(1)} %bitcast_select_fusion.left_ref, bf16[1168,512]{1,0:T(8,128)(2,1)S(1)} %get-tuple-element.86.refs_0_.refs_2_, bf16[1168,512]{1,0:T(8,128)(2,1)S(1)} %get-tuple-element.87.refs_1_.refs_3_, bf16[384,512]{1,0:T(8,128)(2,1)S(1)} %collective-permute-done.13.refs_2_.refs_0_), custom_call_target="tpu_custom_call" | custom-call | flops 2415919104 | bytes 13107200 | tf_op jit(solution)/shard_map/weight_part/pallas_call | solution.py:451
  201.8 1.7 weight_part.8
  203.5 1.3 collective-permute-start.10
  204.8 1.6 collective-permute-done.14.refs_3_.refs_1_
  206.4 1.7 weight_part.10.refs_4_
  208.1 1.5 collective-permute-start.18
  209.7 3.8 %collective-permute-start.19 = (bf16[384,512]{1,0:T(8,128)(2,1)S(1)}, bf16[384,512]{1,0:T(8,128)(2,1)S(1)}, u32[]{:S(2)}, u32[]{:S(2)}) collective-permute-start(bf16[384,512]{1,0:T(8,128)(2,1)S(1)} %get-tuple-element.83.refs_0_), channel_id=1, source_target_pairs={{0,16},{1,1},{2,18},{3,3},{4,20},{5,5},{6,22},{7,7},{8,24},{9,9},{... | collective-permute-start | bytes 1179656 | tf_op jit(solution)/shard_map/ppermute | solution.py:38
  213.5 2.9 %collective-permute-start.20 = (bf16[384,512]{1,0:T(8,128)(2,1)S(1)}, bf16[384,512]{1,0:T(8,128)(2,1)S(1)}, u32[]{:S(2)}, u32[]{:S(2)}) collective-permute-start(bf16[384,512]{1,0:T(8,128)(2,1)S(1)} %get-tuple-element.84.refs_1_), channel_id=1, source_target_pairs={{0,16},{1,1},{2,18},{3,3},{4,20},{5,5},{6,22},{7,7},{8,24},{9,9},{... | collective-permute-start | bytes 1179656 | tf_op jit(solution)/shard_map/ppermute | solution.py:38
  216.4 1.7 weight_part.11.refs_2_.keep_ref
  218.2 1.7 weight_part.7.keep_ref
  220.5 4.9 %last_product.2.refs_1_ = bf16[384,2048]{1,0:T(8,128)(2,1)} custom-call(bf16[2048,2048]{1,0:T(8,128)(2,1)S(1)} %bitcast.25, bf16[1168,512]{1,0:T(8,128)(2,1)S(1)} %get-tuple-element.79.refs_0_.refs_3_, bf16[1168,512]{1,0:T(8,128)(2,1)S(1)} %get-tuple-element.80.refs_1_, bf16[1168,512]{1,0:T(8,128)(2,1)S(1)} %get-tuple-element.86.refs_0_.refs_2_, ...), custom_call_target="tpu_custom_call" | custom-call | flops 3221225472 | bytes 14680064 | tf_op jit(solution)/shard_map/last_product/pallas_call | solution.py:391
  225.4 2.7 collective-permute-done.10.got_ref
  228.2 1.4 copy-done.5
  229.9 2.0 collective-permute-start.15
  232.0 0.9 collective-permute-done.20.refs_1_.refs_3_
  233.1 1.2 collective-permute-start.21
  234.3 8.4 %collective-permute-done.15.got_ref = bf16[272,1024]{1,0:T(8,128)(2,1)S(1)} collective-permute-done((bf16[272,1024]{1,0:T(8,128)(2,1)S(1)}, bf16[272,1024]{1,0:T(8,128)(2,1)S(1)}, u32[]{:S(2)}, u32[]{:S(2)}) %collective-permute-start.15) | collective-permute-done | bytes 557088 | tf_op jit(solution)/shard_map/ppermute | solution.py:30
  242.9 0.8 collective-permute-done.21.got_ref
  243.8 1.3 collective-permute-start.22
  245.1 9.6 %collective-permute-done.22.got_ref = bf16[128,1024]{1,0:T(8,128)(2,1)S(1)} collective-permute-done((bf16[128,1024]{1,0:T(8,128)(2,1)S(1)}, bf16[128,1024]{1,0:T(8,128)(2,1)S(1)}, u32[]{:S(2)}, u32[]{:S(2)}) %collective-permute-start.22) | collective-permute-done | bytes 262176 | tf_op jit(solution)/shard_map/ppermute | solution.py:30
  254.9 3.0 %collective-permute-start.17 = (bf16[80,1024]{1,0:T(8,128)(2,1)S(1)}, bf16[80,1024]{1,0:T(8,128)(2,1)S(1)}, u32[]{:S(2)}, u32[]{:S(2)}) collective-permute-start(bf16[80,1024]{1,0:T(8,128)(2,1)S(1)} %get-tuple-element.95.refs_5_), channel_id=1, source_target_pairs={{0,16},{4,20},{8,24},{12,28},{16,0},{20,4},{24,8},{28,12},{1,17},{... | collective-permute-start | bytes 491528 | tf_op jit(solution)/shard_map/ppermute | solution.py:30
  257.9 5.1 %last_product.3 = bf16[384,2048]{1,0:T(8,128)(2,1)} custom-call(bf16[2048,2048]{1,0:T(8,128)(2,1)S(1)} %bitcast.25, bf16[384,512]{1,0:T(8,128)(2,1)S(1)} %collective-permute-done.13.refs_2_.refs_0_, bf16[384,512]{1,0:T(8,128)(2,1)S(1)} %collective-permute-done.14.refs_3_.refs_1_, bf16[384,512]{1,0:T(8,128)(2,1)S(1)} %collective-permute-done.19.refs_0_.refs_2_, ...), custom_call_target="tpu_custom_call" | custom-call | flops 3221225472 | bytes 14680064 | tf_op jit(solution)/shard_map/last_product/pallas_call | solution.py:391
  263.0 2.3 collective-permute-done.23.got1
  265.3 1.9 collective-permute-done.17.got0
  267.2 0.8 last_stage.1
  (76 shorter events, 5.1 us)
Async XLA Ops:
  7.2 0.8 copy-start.12
  7.2 15.0 %copy-start.8 = (s32[256]{0:T(256)S(1)}, s32[256]{0:T(256)}, u32[]{:S(2)}) copy-start(s32[256]{0:T(256)} %home_ref.1) | copy-start | bytes 3076
  7.2 121.7 %all-gather.2.cloned.1.call-start = ((), (), s32[]{:S(2)}) async-start(), calls=%async_computation.2 | async-start | bytes 10485760 | tf_op jit(solution)/shard_map/all_gather | solution.py:554
  8.5 13.7 %all-to-all-start = ((s32[8,1,16]{2,1,0:T(1,128)}), s32[8,1,16]{2,1,0:T(1,128)S(1)}, u32[]{:S(2)}, u32[]{:S(2)}) async-start(s32[8,1,16]{2,1,0:T(1,128)} %broadcast_in_dim.24), calls=%async_computation | async-start | bytes 8192 | tf_op jit(solution)/shard_map/all_to_all | solution.py:539
  22.2 3.3 %copy-start.6 = (bf16[8,128,2048]{2,1,0:T(8,128)(2,1)S(1)}, bf16[8,128,2048]{2,1,0:T(8,128)(2,1)}, u32[]{:S(2)}) copy-start(bf16[8,128,2048]{2,1,0:T(8,128)(2,1)} %bank_ref.1) | copy-start | bytes 12582916
  29.3 2.0 copy-start.7
  31.3 5.0 %copy-start.10 = (bf16[384,2048]{1,0:T(8,128)(2,1)S(1)}, bf16[384,2048]{1,0:T(8,128)(2,1)}, u32[]{:S(2)}) copy-start(bf16[384,2048]{1,0:T(8,128)(2,1)} %param.7) | copy-start | bytes 4718596
  31.3 110.7 %all-to-all-start.1 = ((bf16[4,256,2048]{2,1,0:T(8,128)(2,1)}), bf16[4,256,2048]{2,1,0:T(8,128)(2,1)}, u32[]{:S(2)}, u32[]{:S(2)}) async-start(bf16[4,256,2048]{2,1,0:T(8,128)(2,1)} %bitcast.26), calls=%async_computation.1 | async-start | bytes 8388608 | tf_op jit(solution)/shard_map/all_to_all | solution.py:549
  37.2 4.6 %copy-start.9 = (bf16[384,2048]{1,0:T(8,128)(2,1)S(1)}, bf16[384,2048]{1,0:T(8,128)(2,1)}, u32[]{:S(2)}) copy-start(bf16[384,2048]{1,0:T(8,128)(2,1)} %param.8) | copy-start | bytes 4718596
  39.7 3.7 %copy-start.14 = (s32[32]{0:T(128)S(1)}, s32[32]{0:T(128)}, u32[]{:S(2)}) copy-start(s32[32]{0:T(128)} %constant.56) | copy-start | bytes 388
  39.7 3.9 %copy-start.13 = (s32[32,1]{0,1:T(1,128)S(1)}, s32[32,1]{0,1:T(1,128)}, u32[]{:S(2)}) copy-start(s32[32,1]{0,1:T(1,128)} %constant.59) | copy-start | bytes 388
  39.7 76.8 %collective-permute-start = (bf16[384,2048]{0,1:T(8,128)(2,1)}, bf16[384,2048]{0,1:T(8,128)(2,1)}, u32[]{:S(2)}, u32[]{:S(2)}) collective-permute-start(bf16[384,2048]{0,1:T(8,128)(2,1)} %broadcast_select_fusion), channel_id=1, source_target_pairs={{0,16},{1,1},{2,18},{3,3},{4,20},{5,5},{6,22},{7,7},{8,24},{9,9},{... | collective-permute-start | bytes 4718600 | tf_op jit(solution)/shard_map/ppermute | solution.py:38
  43.6 114.3 %collective-permute-start.5 = (bf16[256,2048]{1,0:T(8,128)(2,1)}, bf16[256,2048]{1,0:T(8,128)(2,1)}, u32[]{:S(2)}, u32[]{:S(2)}) collective-permute-start(bf16[256,2048]{1,0:T(8,128)(2,1)} %get-tuple-element.61), channel_id=1, source_target_pairs={{0,0},{1,17},{2,2},{3,19},{4,4},{5,21},{6,6},{7,23},{8,8},{9,25},{... | collective-permute-start | bytes 3145736 | tf_op jit(solution)/shard_map/ppermute | solution.py:38
  53.1 112.1 %collective-permute-start.4 = (bf16[256,2048]{1,0:T(8,128)(2,1)}, bf16[256,2048]{1,0:T(8,128)(2,1)S(1)}, u32[]{:S(2)}, u32[]{:S(2)}) collective-permute-start(bf16[256,2048]{1,0:T(8,128)(2,1)} %get-tuple-element.60), channel_id=1, source_target_pairs={{0,4},{1,21},{2,6},{3,23},{4,0},{5,17},{6,2},{7,19},{8,12},{9,29},... | collective-permute-start | bytes 3145736 | tf_op jit(solution)/shard_map/ppermute | solution.py:38
  55.1 110.7 %collective-permute-start.3 = (bf16[256,2048]{1,0:T(8,128)(2,1)}, bf16[256,2048]{1,0:T(8,128)(2,1)}, u32[]{:S(2)}, u32[]{:S(2)}) collective-permute-start(bf16[256,2048]{1,0:T(8,128)(2,1)} %get-tuple-element.59), channel_id=1, source_target_pairs={{0,8},{1,25},{2,10},{3,27},{4,12},{5,29},{6,14},{7,31},{8,0},{9,17... | collective-permute-start | bytes 3145736 | tf_op jit(solution)/shard_map/ppermute | solution.py:38
  56.5 111.1 %collective-permute-start.2 = (bf16[256,2048]{1,0:T(8,128)(2,1)}, bf16[256,2048]{1,0:T(8,128)(2,1)}, u32[]{:S(2)}, u32[]{:S(2)}) collective-permute-start(bf16[256,2048]{1,0:T(8,128)(2,1)} %get-tuple-element.58), channel_id=1, source_target_pairs={{0,12},{1,29},{2,14},{3,31},{4,8},{5,25},{6,10},{7,27},{8,4},{9,21... | collective-permute-start | bytes 3145736 | tf_op jit(solution)/shard_map/ppermute | solution.py:38
  128.9 42.9 %collective-permute-start.1 = (bf16[1024,1152]{1,0:T(8,128)(2,1)}, bf16[1024,1152]{1,0:T(8,128)(2,1)S(1)}, u32[]{:S(2)}, u32[]{:S(2)}) collective-permute-start(bf16[1024,1152]{1,0:T(8,128)(2,1)} %bitcast.8), channel_id=1, source_target_pairs={{0,1},{1,0},{2,3},{3,2},{4,5},{5,4},{6,7},{7,6},{8,9},{9,8},{10,11... | collective-permute-start | bytes 7077896 | tf_op jit(solution)/shard_map/ppermute | solution.py:30
  128.9 8.6 %copy-start = (bf16[2048,2048]{1,0:T(8,128)(2,1)S(1)}, bf16[2048,2048]{1,0:T(8,128)(2,1)}, u32[]{:S(2)}) copy-start(bf16[2048,2048]{1,0:T(8,128)(2,1)} %all-gather.2.cloned.1.call-done.w_ref) | copy-start | bytes 25165828
  128.9 8.6 %copy-start.11 = (bf16[384,2048]{1,0:T(8,128)(2,1)S(1)}, bf16[384,2048]{1,0:T(8,128)(2,1)}, u32[]{:S(2)}) copy-start(bf16[384,2048]{1,0:T(8,128)(2,1)} %param.7) | copy-start | bytes 4718596
  142.0 1.4 copy-start.1
  143.4 1.4 copy-start.3
  157.9 13.9 %collective-permute-start.7 = (f32[8,384]{1,0:T(8,128)S(1)}, f32[8,384]{1,0:T(8,128)S(1)}, u32[]{:S(2)}, u32[]{:S(2)}) collective-permute-start(f32[8,384]{1,0:T(8,128)S(1)} %get-tuple-element.57.mine_ref), channel_id=1, source_target_pairs={{0,16},{1,1},{2,18},{3,3},{4,20},{5,5},{6,22},{7,7},{8,24},{9,9},{... | collective-permute-start | bytes 36872 | tf_op jit(solution)/shard_map/ppermute | solution.py:38
  169.6 12.3 %collective-permute-start.6 = (f32[8,384]{1,0:T(8,128)S(1)}, f32[8,384]{1,0:T(8,128)S(1)}, u32[]{:S(2)}, u32[]{:S(2)}) collective-permute-start(f32[8,384]{1,0:T(8,128)S(1)} %get-tuple-element.66.mine_ref), channel_id=1, source_target_pairs={{0,16},{1,1},{2,18},{3,3},{4,20},{5,5},{6,22},{7,7},{8,24},{9,9},{... | collective-permute-start | bytes 36872 | tf_op jit(solution)/shard_map/ppermute | solution.py:38
  171.8 11.6 %copy-start.4 = (bf16[384,2048]{1,0:T(8,128)(2,1)S(1)}, bf16[384,2048]{1,0:T(8,128)(2,1)}, u32[]{:S(2)}) copy-start(bf16[384,2048]{1,0:T(8,128)(2,1)} %convolution_convert_fusion.2.refs_0_.q_ref) | copy-start | bytes 4718596
  176.9 6.5 %copy-start.2 = (bf16[384,2048]{1,0:T(8,128)(2,1)S(1)}, bf16[384,2048]{1,0:T(8,128)(2,1)}, u32[]{:S(2)}) copy-start(bf16[384,2048]{1,0:T(8,128)(2,1)} %convolution_convert_fusion.1.refs_2_.p_ref) | copy-start | bytes 4718596
  176.9 16.1 %collective-permute-start.13 = (bf16[384,512]{1,0:T(8,128)(2,1)S(1)}, bf16[384,512]{1,0:T(8,128)(2,1)S(1)}, u32[]{:S(2)}, u32[]{:S(2)}) collective-permute-start(bf16[384,512]{1,0:T(8,128)(2,1)S(1)} %get-tuple-element.76.refs_0_), channel_id=1, source_target_pairs={{0,16},{1,1},{2,18},{3,3},{4,20},{5,5},{6,22},{7,7},{8,24},{9,9},{... | collective-permute-start | bytes 1179656 | tf_op jit(solution)/shard_map/ppermute | solution.py:38
  187.0 4.9 %slice-start.2 = ((s8[4718592]{0:T(1024)(128)(4,1)}), s8[4194304]{0:T(1024)(128)(4,1)S(1)}, s32[]{:S(2)}) async-start(s8[4718592]{0:T(1024)(128)(4,1)} %bitcast.29), calls=%async_computation.5 | async-start | bytes 8388608
  187.0 4.9 %slice-start.3 = ((s8[4718592]{0:T(1024)(128)(4,1)}), s8[524288]{0:T(1024)(128)(4,1)S(1)}, s32[]{:S(2)}) async-start(s8[4718592]{0:T(1024)(128)(4,1)} %bitcast.29), calls=%async_computation.6 | async-start | bytes 1048576
  190.8 15.6 %collective-permute-start.11 = (bf16[1168,512]{1,0:T(8,128)(2,1)S(1)}, bf16[1168,512]{1,0:T(8,128)(2,1)S(1)}, u32[]{:S(2)}, u32[]{:S(2)}) collective-permute-start(bf16[1168,512]{1,0:T(8,128)(2,1)S(1)} %get-tuple-element.86.refs_0_.refs_2_), channel_id=1, source_target_pairs={{0,1},{1,0},{2,3},{3,2},{4,5},{5,4},{6,7},{7,6},{8,9},{9,8},{10,11... | collective-permute-start | bytes 3588104 | tf_op jit(solution)/shard_map/ppermute | solution.py:30
  190.9 15.5 %collective-permute-start.12 = (bf16[1168,512]{1,0:T(8,128)(2,1)S(1)}, bf16[1168,512]{1,0:T(8,128)(2,1)S(1)}, u32[]{:S(2)}, u32[]{:S(2)}) collective-permute-start(bf16[1168,512]{1,0:T(8,128)(2,1)S(1)} %get-tuple-element.87.refs_1_.refs_3_), channel_id=1, source_target_pairs={{0,1},{1,0},{2,3},{3,2},{4,5},{5,4},{6,7},{7,6},{8,9},{9,8},{10,11... | collective-permute-start | bytes 3588104 | tf_op jit(solution)/shard_map/ppermute | solution.py:30
  191.4 10.3 %collective-permute-start.8 = (bf16[1168,512]{1,0:T(8,128)(2,1)S(1)}, bf16[1168,512]{1,0:T(8,128)(2,1)S(1)}, u32[]{:S(2)}, u32[]{:S(2)}) collective-permute-start(bf16[1168,512]{1,0:T(8,128)(2,1)S(1)} %get-tuple-element.79.refs_0_.refs_3_), channel_id=1, source_target_pairs={{0,1},{1,0},{2,3},{3,2},{4,5},{5,4},{6,7},{7,6},{8,9},{9,8},{10,11... | collective-permute-start | bytes 3588104 | tf_op jit(solution)/shard_map/ppermute | solution.py:30
  191.5 10.3 %collective-permute-start.9 = (bf16[1168,512]{1,0:T(8,128)(2,1)S(1)}, bf16[1168,512]{1,0:T(8,128)(2,1)S(1)}, u32[]{:S(2)}, u32[]{:S(2)}) collective-permute-start(bf16[1168,512]{1,0:T(8,128)(2,1)S(1)} %get-tuple-element.80.refs_1_), channel_id=1, source_target_pairs={{0,1},{1,0},{2,3},{3,2},{4,5},{5,4},{6,7},{7,6},{8,9},{9,8},{10,11... | collective-permute-start | bytes 3588104 | tf_op jit(solution)/shard_map/ppermute | solution.py:30
  193.0 13.4 %collective-permute-start.14 = (bf16[384,512]{1,0:T(8,128)(2,1)S(1)}, bf16[384,512]{1,0:T(8,128)(2,1)S(1)}, u32[]{:S(2)}, u32[]{:S(2)}) collective-permute-start(bf16[384,512]{1,0:T(8,128)(2,1)S(1)} %get-tuple-element.77.refs_1_), channel_id=1, source_target_pairs={{0,16},{1,1},{2,18},{3,3},{4,20},{5,5},{6,22},{7,7},{8,24},{9,9},{... | collective-permute-start | bytes 1179656 | tf_op jit(solution)/shard_map/ppermute | solution.py:38
  203.5 24.7 %collective-permute-start.10 = (bf16[528,1024]{1,0:T(8,128)(2,1)S(1)}, bf16[528,1024]{1,0:T(8,128)(2,1)S(1)}, u32[]{:S(2)}, u32[]{:S(2)}) collective-permute-start(bf16[528,1024]{1,0:T(8,128)(2,1)S(1)} %get-tuple-element.81), channel_id=1, source_target_pairs={{0,2},{1,3},{2,0},{3,1},{4,6},{5,7},{6,4},{7,5},{8,10},{9,11},{10,... | collective-permute-start | bytes 3244040 | tf_op jit(solution)/shard_map/ppermute | solution.py:30
  208.1 24.7 %collective-permute-start.18 = (bf16[512,1024]{1,0:T(8,128)(2,1)S(1)}, bf16[512,1024]{1,0:T(8,128)(2,1)S(1)}, u32[]{:S(2)}, u32[]{:S(2)}) collective-permute-start(bf16[512,1024]{1,0:T(8,128)(2,1)S(1)} %weight_part.10.refs_4_), channel_id=1, source_target_pairs={{0,4},{4,0},{8,12},{12,8},{16,20},{20,16},{24,28},{28,24},{1,5},{5... | collective-permute-start | bytes 3145736 | tf_op jit(solution)/shard_map/ppermute | solution.py:30
  209.7 22.3 %collective-permute-start.19 = (bf16[384,512]{1,0:T(8,128)(2,1)S(1)}, bf16[384,512]{1,0:T(8,128)(2,1)S(1)}, u32[]{:S(2)}, u32[]{:S(2)}) collective-permute-start(bf16[384,512]{1,0:T(8,128)(2,1)S(1)} %get-tuple-element.83.refs_0_), channel_id=1, source_target_pairs={{0,16},{1,1},{2,18},{3,3},{4,20},{5,5},{6,22},{7,7},{8,24},{9,9},{... | collective-permute-start | bytes 1179656 | tf_op jit(solution)/shard_map/ppermute | solution.py:38
  213.5 19.4 %collective-permute-start.20 = (bf16[384,512]{1,0:T(8,128)(2,1)S(1)}, bf16[384,512]{1,0:T(8,128)(2,1)S(1)}, u32[]{:S(2)}, u32[]{:S(2)}) collective-permute-start(bf16[384,512]{1,0:T(8,128)(2,1)S(1)} %get-tuple-element.84.refs_1_), channel_id=1, source_target_pairs={{0,16},{1,1},{2,18},{3,3},{4,20},{5,5},{6,22},{7,7},{8,24},{9,9},{... | collective-permute-start | bytes 1179656 | tf_op jit(solution)/shard_map/ppermute | solution.py:38
  216.4 3.5 %slice-start = ((s8[8388608]{0:T(1024)(128)(4,1)}), s8[4194304]{0:T(1024)(128)(4,1)S(1)}, s32[]{:S(2)}) async-start(s8[8388608]{0:T(1024)(128)(4,1)} %bitcast.24), calls=%async_computation.3 | async-start | bytes 8388608
  218.2 2.3 slice-start.1
  228.2 1.4 copy-start.5
  229.9 12.7 %collective-permute-start.15 = (bf16[272,1024]{1,0:T(8,128)(2,1)S(1)}, bf16[272,1024]{1,0:T(8,128)(2,1)S(1)}, u32[]{:S(2)}, u32[]{:S(2)}) collective-permute-start(bf16[272,1024]{1,0:T(8,128)(2,1)S(1)} %get-tuple-element.89), channel_id=1, source_target_pairs={{0,4},{4,0},{8,12},{12,8},{16,20},{20,16},{24,28},{28,24},{1,5},{5... | collective-permute-start | bytes 1671176 | tf_op jit(solution)/shard_map/ppermute | solution.py:30
  233.1 10.6 %collective-permute-start.21 = (bf16[256,1024]{1,0:T(8,128)(2,1)S(1)}, bf16[256,1024]{1,0:T(8,128)(2,1)S(1)}, u32[]{:S(2)}, u32[]{:S(2)}) collective-permute-start(bf16[256,1024]{1,0:T(8,128)(2,1)S(1)} %get-tuple-element.97), channel_id=1, source_target_pairs={{0,2},{1,3},{2,0},{3,1},{4,6},{5,7},{6,4},{7,5},{8,10},{9,11},{10,... | collective-permute-start | bytes 1572872 | tf_op jit(solution)/shard_map/ppermute | solution.py:30
  242.8 12.0 %collective-permute-start.16 = (bf16[144,1024]{1,0:T(8,128)(2,1)S(1)}, bf16[144,1024]{1,0:T(8,128)(2,1)S(1)}, u32[]{:S(2)}, u32[]{:S(2)}) collective-permute-start(bf16[144,1024]{1,0:T(8,128)(2,1)S(1)} %get-tuple-element.92), channel_id=1, source_target_pairs={{0,8},{4,12},{8,0},{12,4},{16,24},{20,28},{24,16},{28,20},{1,9},{5... | collective-permute-start | bytes 884744 | tf_op jit(solution)/shard_map/ppermute | solution.py:30
  243.8 10.9 %collective-permute-start.22 = (bf16[128,1024]{1,0:T(8,128)(2,1)S(1)}, bf16[128,1024]{1,0:T(8,128)(2,1)S(1)}, u32[]{:S(2)}, u32[]{:S(2)}) collective-permute-start(bf16[128,1024]{1,0:T(8,128)(2,1)S(1)} %get-tuple-element.99), channel_id=1, source_target_pairs={{0,8},{4,12},{8,0},{12,4},{16,24},{20,28},{24,16},{28,20},{1,9},{5... | collective-permute-start | bytes 786440 | tf_op jit(solution)/shard_map/ppermute | solution.py:30
  254.7 10.6 %collective-permute-start.23 = (bf16[64,1024]{1,0:T(8,128)(2,1)S(1)}, bf16[64,1024]{1,0:T(8,128)(2,1)S(1)}, u32[]{:S(2)}, u32[]{:S(2)}) collective-permute-start(bf16[64,1024]{1,0:T(8,128)(2,1)S(1)} %get-tuple-element.101.refs_6_), channel_id=1, source_target_pairs={{0,16},{4,20},{8,24},{12,28},{16,0},{20,4},{24,8},{28,12},{1,17},{... | collective-permute-start | bytes 393224 | tf_op jit(solution)/shard_map/ppermute | solution.py:30
  254.9 12.3 %collective-permute-start.17 = (bf16[80,1024]{1,0:T(8,128)(2,1)S(1)}, bf16[80,1024]{1,0:T(8,128)(2,1)S(1)}, u32[]{:S(2)}, u32[]{:S(2)}) collective-permute-start(bf16[80,1024]{1,0:T(8,128)(2,1)S(1)} %get-tuple-element.95.refs_5_), channel_id=1, source_target_pairs={{0,16},{4,20},{8,24},{12,28},{16,0},{20,4},{24,8},{28,12},{1,17},{... | collective-permute-start | bytes 491528 | tf_op jit(solution)/shard_map/ppermute | solution.py:30
Sparse Core Ops, SparseCore 0:
  9.6 60.9 all-gather.1

commit v3 on v2

--- a/solution.py
+++ b/solution.py
@@ -464,7 +464,7 @@
     )(*args)
 
 
-def fold_stage(keep, got, loss=None, after=()):
+def fold_stage(keep, got, loss=None, after=(), outer=1):
     rows, cols = keep.shape
     mid = rows // 2
 
@@ -476,8 +476,13 @@
             value = refs[0][0:1, 0:1] + joined_rows(got_ref[rows:])
             state[...] = jnp.broadcast_to(value, state.shape)
             send[mid:] = split_rows(value, cols)
-        send[:mid] = (keep_ref[:mid] + got_ref[:mid].astype(F32)).astype(BF16)
-        rest[...] = keep_ref[mid:] + got_ref[mid:rows].astype(F32)
+        part = mid // outer
+        for o in range(outer):
+            to = slice(o * part, (o + 1) * part)
+            one = slice(2 * o * part, (2 * o + 1) * part)
+            two = slice((2 * o + 1) * part, (2 * o + 2) * part)
+            send[to] = (keep_ref[one] + got_ref[one].astype(F32)).astype(BF16)
+            rest[to] = keep_ref[two] + got_ref[two].astype(F32)
 
     args = [keep, got] + ([loss] if loss is not None else [])
     in_specs = [pl.BlockSpec(memory_space=pltpu.VMEM)] * len(args)
@@ -623,7 +628,8 @@
         kept = (full,)
     far_rows = [swap(r, *f_bits[0]) for r in rows]
 
-    orders = [stages, [stages[1], stages[0]] + stages[2:]]
+    orders = [stages, [stages[1]] + d_bits[1:] + [stages[0]] + f_bits[2:]]
+    lie = [stages[0]] + stages[2:]
     give = ((0, 1), (0, 2))
     hold = ((2, 3), (1, 3))
     every = (0, 1, 2, 3)
@@ -646,7 +652,9 @@
         gots = [swap(sends[i], *orders[i][s]) for i in range(2)]
         if s + 1 < len(stages):
             send0, keep0, loss = fold_stage(keeps[0], gots[0], loss, waits.get((s, 0), ()))
-            send1, keep1 = fold_stage(keeps[1], gots[1], after=waits.get((s, 1), ()))
+            outer = 1 << lie.index(orders[1][s + 1])
+            lie.remove(orders[1][s + 1])
+            send1, keep1 = fold_stage(keeps[1], gots[1], after=waits.get((s, 1), ()), outer=outer)
             sends, keeps = [send0, send1], [keep0, keep1]
     back_q = last_product(home, 0, count, full_weight, tile, full=full, after=tuple(sends))
     grad_weight, loss = last_stage(keeps, gots, loss)

time: 279 us -> 282 us (1.011)
  waiting for transfers between devices: 92.4 us -> 97.2 us
    ppermute x13, waiting for transfers between devices: 25.7 us -> 30.4 us  [swap(): lax.ppermute(x, axis, [(i, i ^ bit) for i in range(lax.axis_size(axis))])]
  transfers between devices with their start and end apart: 27 -> 27, of which waited for: 10 -> 9; matrix products, arithmetic and copies ran while one was open for 15% -> 15% of each run, Pallas kernels for 20% -> 19%
where the time goes in v3:
time: 282 us; the launch traced here: 281 us
  waiting for transfers between devices  97.2 us (34%)
  starting transfers between devices  59 us (21%)
  Pallas kernels  55.3 us (20%)
  local copies, waits for them, and re-layouts  20.5 us (7%)
  matrix products  20.4 us (7%)
  between operations  17.6 us (6%)
  other arithmetic  10.8 us (4%)
    ppermute x11, waiting for transfers between devices, move(): return lax.ppermute(x, ('dp', 'fsdp'), pairs)  59.7 us
    ppermute x11, starting transfers between devices, move(): return lax.ppermute(x, ('dp', 'fsdp'), pairs)  36.2 us
    ppermute x13, waiting for transfers between devices, swap(): lax.ppermute(x, axis, [(i, i ^ bit) for i in range(lax.axis_size(axis))])  30.4 us
    pallas_call x6, Pallas kernels, weight_part(): pl.pallas_call(kernel, grid=(m,), in_specs=in_specs, out_specs=out_specs,...  13.7 us
    unnamed x40, local copies, waits for them, and re-layouts  12.6 us
    pallas_call x5, Pallas kernels, part_scores(): pl.pallas_call(kernel, grid=(sets,), in_specs=in_specs, out_specs=out_spe...  12.1 us
    ppermute x13, starting transfers between devices, swap(): lax.ppermute(x, axis, [(i, i ^ bit) for i in range(lax.axis_size(axis))])  10.5 us
    pallas_call x2, Pallas kernels, last_product(): pl.pallas_call(kernel, grid=(kin // tile,), in_specs=in_specs + [ANY] * l...  10.1 us
  transfers between devices with their start and end apart: 27, of which 9 were waited for; matrix products, arithmetic and copies ran while one was open for 15% of the time, Pallas kernels for 19%

profile of v3, /device:TPU:0, one launch (start us, length us, event | category | flops | bytes accessed | tf_op | source)
XLA Modules:
  0.0 280.8 jit_solution(3909304141801017401)
XLA Ops:
  7.2 0.7 all-gather.2.cloned.1.call-update
  7.9 0.6 broadcast_in_dim.24
  8.5 7.3 %all-to-all-start = ((s32[8,1,16]{2,1,0:T(1,128)}), s32[8,1,16]{2,1,0:T(1,128)S(1)}, u32[]{:S(2)}, u32[]{:S(2)}) async-start(s32[8,1,16]{2,1,0:T(1,128)} %broadcast_in_dim.24), calls=%async_computation | async-start | bytes 8192 | tf_op jit(solution)/shard_map/all_to_all | solution.py:544
  15.8 6.4 %all-to-all-done = s32[8,1,16]{2,1,0:T(1,128)S(1)} async-done(((s32[8,1,16]{2,1,0:T(1,128)}), s32[8,1,16]{2,1,0:T(1,128)S(1)}, u32[]{:S(2)}, u32[]{:S(2)}) %all-to-all-start) | async-done | bytes 544 | tf_op jit(solution)/shard_map/all_to_all | solution.py:544
  22.2 3.3 %copy-done.6 = bf16[8,128,2048]{2,1,0:T(8,128)(2,1)S(1)} copy-done((bf16[8,128,2048]{2,1,0:T(8,128)(2,1)S(1)}, bf16[8,128,2048]{2,1,0:T(8,128)(2,1)}, u32[]{:S(2)}) %copy-start.6) | copy-done | bytes 4194328
  25.5 3.7 %pick_blocks.1 = (bf16[1024,2048]{1,0:T(8,128)(2,1)S(1)}, bf16[256,2048]{1,0:T(8,128)(2,1)}, bf16[256,2048]{1,0:T(8,128)(2,1)}, bf16[256,2048]{1,0:T(8,128)(2,1)...) custom-call(s32[8,16]{1,0:T(8,128)S(1)} %bitcast.27, s32[256]{0:T(256)S(1)} %copy-done.8, s32[1]{0:T(128)} %bitcast.2.me_ref, ...), custom_call_target="tpu_custom_call" | custom-call | bytes 16777216 | tf_op jit(solution)/shard_map/pick_blocks/pallas_call | solution.py:96
  29.3 2.0 copy-done.7
  31.3 5.0 %all-to-all-start.1 = ((bf16[4,256,2048]{2,1,0:T(8,128)(2,1)}), bf16[4,256,2048]{2,1,0:T(8,128)(2,1)}, u32[]{:S(2)}, u32[]{:S(2)}) async-start(bf16[4,256,2048]{2,1,0:T(8,128)(2,1)} %bitcast.26), calls=%async_computation.1 | async-start | bytes 8388608 | tf_op jit(solution)/shard_map/all_to_all | solution.py:554
  36.3 0.9 copy.17
  38.4 1.3 broadcast_select_fusion
  39.7 2.1 collective-permute-start
  41.9 1.6 copy.15
  43.6 9.4 %collective-permute-start.5 = (bf16[256,2048]{1,0:T(8,128)(2,1)}, bf16[256,2048]{1,0:T(8,128)(2,1)}, u32[]{:S(2)}, u32[]{:S(2)}) collective-permute-start(bf16[256,2048]{1,0:T(8,128)(2,1)} %get-tuple-element.61), channel_id=1, source_target_pairs={{0,0},{1,17},{2,2},{3,19},{4,4},{5,21},{6,6},{7,23},{8,8},{9,25},{... | collective-permute-start | bytes 3145736 | tf_op jit(solution)/shard_map/ppermute | solution.py:38
  53.1 2.0 collective-permute-start.4
  55.1 1.4 collective-permute-start.3
  57.7 1.6 broadcast_select_fusion.1
  59.3 57.1 %collective-permute-done = bf16[384,2048]{0,1:T(8,128)(2,1)} collective-permute-done((bf16[384,2048]{0,1:T(8,128)(2,1)}, bf16[384,2048]{0,1:T(8,128)(2,1)}, u32[]{:S(2)}, u32[]{:S(2)}) %collective-permute-start) | collective-permute-done | bytes 1572896 | tf_op jit(solution)/shard_map/ppermute | solution.py:38
  116.4 3.5 %pad_maximum_fusion = bf16[1152,2048]{0,1:T(8,128)(2,1)} fusion(bf16[384,2048]{0,1:T(8,128)(2,1)} %collective-permute-done, bf16[384,2048]{0,1:T(8,128)(2,1)S(1)} %broadcast_select_fusion.1, bf16[384,2048]{0,1:T(8,128)(2,1)S(1)} %copy.17), kind=kLoop, calls=%fused_computation.1 | loop fusion | flops 14155776 | bytes 9437184 | tf_op jit(solution)/shard_map/concatenate | solution.py:575
  119.9 5.6 %gather_fusion = bf16[32,64,1152]{2,1,0:T(8,128)(2,1)} fusion(bf16[32,64,1152]{2,1,0:T(8,128)(2,1)} %bitcast.31, s32[1024]{0:T(1024)S(1)} %pad_clamp_fusion), kind=kCustom, calls=%fused_computation | custom fusion | bytes 9437312 | tf_op jit(solution)/shard_map/jit(_take)/gather | solution.py:578
  125.5 3.4 %slice_select_fusion = bf16[16,64,1152]{2,1,0:T(8,128)(2,1)} fusion(bf16[32,64,1152]{2,1,0:T(8,128)(2,1)} %gather_fusion, pred[16]{0:T(512)(128)(4,1)S(1)} %bitcast.32), kind=kLoop, calls=%fused_computation.6 | loop fusion | flops 1179648 | bytes 4718608 | tf_op jit(solution)/shard_map/jit(_take)/select_n | solution.py:578
  128.9 8.6 %convolution_convert_fusion.1.refs_2_.p_ref = bf16[384,2048]{1,0:T(8,128)(2,1)} fusion(bf16[384,2048]{1,0:T(8,128)(2,1)} %param.8, bf16[2048,2048]{1,0:T(8,128)(2,1)} %all-gather.2.cloned.1.call-done.w_ref), kind=kOutput, calls=%fused_computation.4 | convolution fusion | flops 3222011904 | bytes 11534336 | tf_op jit(solution)/shard_map/dot_general | solution.py:561
  137.5 4.5 %convolution_convert_fusion.2.refs_0_.q_ref = bf16[384,2048]{1,0:T(8,128)(2,1)} fusion(bf16[384,2048]{1,0:T(8,128)(2,1)S(1)} %copy-done.11, bf16[2048,2048]{1,0:T(8,128)(2,1)S(1)} %copy-done), kind=kOutput, calls=%fused_computation.5 | convolution fusion | flops 3222011904 | bytes 11534336 | tf_op jit(solution)/shard_map/dot_general | solution.py:560
  142.0 1.4 copy-done.1
  143.4 1.4 copy-done.3
  144.8 5.8 %part_scores.5 = (f32[384,1024]{1,0:T(8,128)S(1)}, f32[8,384]{1,0:T(8,128)S(1)}, f32[384,384]{1,0:T(8,128)S(1)}) custom-call(bf16[384,2048]{1,0:T(8,128)(2,1)S(1)} %copy-done.3, bf16[1024,2048]{1,0:T(8,128)(2,1)} %bitcast.11.refs_1_.x_ref, bf16[384,2048]{1,0:T(8,128)(2,1)S(1)} %copy-done.1), custom_call_target="tpu_custom_call" | custom-call | flops 1610612736 | bytes 5767168 | tf_op jit(solution)/shard_map/part_scores/pallas_call | solution.py:192
  150.5 7.3 %convolution_convert_fusion.refs_0_ = bf16[384,2048]{1,0:T(8,128)(2,1)S(1)} fusion(bf16[384,2048]{0,1:T(8,128)(2,1)} %collective-permute-done, bf16[2048,2048]{1,0:T(8,128)(2,1)} %all-gather.2.cloned.1.call-done.w_ref), kind=kOutput, calls=%fused_computation.3 | convolution fusion | flops 3222011904 | bytes 11534336 | tf_op jit(solution)/shard_map/dot_general | solution.py:562
  157.9 5.3 %collective-permute-start.7 = (f32[8,384]{1,0:T(8,128)S(1)}, f32[8,384]{1,0:T(8,128)S(1)}, u32[]{:S(2)}, u32[]{:S(2)}) collective-permute-start(f32[8,384]{1,0:T(8,128)S(1)} %get-tuple-element.57.mine_ref), channel_id=1, source_target_pairs={{0,16},{1,1},{2,18},{3,3},{4,20},{5,5},{6,22},{7,7},{8,24},{9,9},{... | collective-permute-start | bytes 36872 | tf_op jit(solution)/shard_map/ppermute | solution.py:38
  163.3 1.9 part_scores.6
  165.1 0.6 part_scores.7
  165.8 1.9 part_scores.8
  167.7 2.0 part_scores.9
  169.6 2.1 collective-permute-start.6
  171.8 5.1 %guest_rows.1 = (f32[384,2048]{1,0:T(8,128)S(1)}, bf16[384,512]{1,0:T(8,128)(2,1)S(1)}, bf16[384,512]{1,0:T(8,128)(2,1)S(1)}, bf16[384,512]{1,0:T(8,128)(2,1)S(1)}, bf16[384,512]{1,0:T(8,128)(2,1)S(1)}) custom-call(s32[1]{0:T(128)} %bitcast.9.stays_ref, f32[8,384]{1,0:T(8,128)S(1)} %get-tuple-element.66.mine_ref, ...), custom_call_target="tpu_custom_call" | custom-call | flops 1610612736 | bytes 8912896 | tf_op jit(solution)/shard_map/guest_rows/pallas_call | solution.py:263
  176.9 5.0 %collective-permute-start.13 = (bf16[384,512]{1,0:T(8,128)(2,1)S(1)}, bf16[384,512]{1,0:T(8,128)(2,1)S(1)}, u32[]{:S(2)}, u32[]{:S(2)}) collective-permute-start(bf16[384,512]{1,0:T(8,128)(2,1)S(1)} %get-tuple-element.76.refs_0_), channel_id=1, source_target_pairs={{0,16},{1,1},{2,18},{3,3},{4,20},{5,5},{6,22},{7,7},{8,24},{9,9},{... | collective-permute-start | bytes 1179656 | tf_op jit(solution)/shard_map/ppermute | solution.py:38
  181.9 1.5 own_grads.1
  183.4 3.6 %grad_rows.2 = (bf16[1168,512]{1,0:T(8,128)(2,1)S(1)}, bf16[1168,512]{1,0:T(8,128)(2,1)S(1)}, f32[384,2048]{1,0:T(8,128)S(1)}) custom-call(s32[1]{0:T(128)} %bitcast.9.stays_ref, bf16[384,1024]{1,0:T(8,128)(2,1)S(1)} %get-tuple-element.68.own_ref, bf16[384,384]{1,0:T(8,128)(2,1)S(1)} %get-tuple-element.69.near_ref, ...), custom_call_target="tpu_custom_call" | custom-call | flops 1409286144 | bytes 9961472 | tf_op jit(solution)/shard_map/grad_rows/pallas_call | solution.py:343
  187.1 3.8 %grad_rows.3 = (bf16[1168,512]{1,0:T(8,128)(2,1)S(1)}, bf16[1168,512]{1,0:T(8,128)(2,1)S(1)}, f32[384,2048]{1,0:T(8,128)S(1)}) custom-call(s32[1]{0:T(128)} %bitcast.9.stays_ref, bf16[384,1024]{1,0:T(8,128)(2,1)S(1)} %get-tuple-element.68.own_ref, bf16[384,384]{1,0:T(8,128)(2,1)S(1)} %get-tuple-element.69.near_ref, ...), custom_call_target="tpu_custom_call", output_to_operand_aliasing={{2}: (11, {})} | custom-call | flops 1409286144 | bytes 9961472 | tf_op jit(solution)/shard_map/grad_rows/pallas_call | solution.py:343
  191.9 1.1 bitcast_select_fusion.left_ref
  193.0 1.9 collective-permute-start.14
  194.9 3.4 %weight_part.6.refs_2_ = f32[1024,1024]{1,0:T(8,128)S(1)} custom-call(bf16[2048,1152]{1,0:T(8,128)(2,1)S(1)} %bitcast_select_fusion.left_ref, bf16[1168,512]{1,0:T(8,128)(2,1)S(1)} %get-tuple-element.79.refs_0_.refs_3_, bf16[1168,512]{1,0:T(8,128)(2,1)S(1)} %get-tuple-element.80.refs_1_), custom_call_target="tpu_custom_call" | custom-call | flops 2415919104 | bytes 13107200 | tf_op jit(solution)/shard_map/weight_part/pallas_call | solution.py:451
  198.3 3.4 %weight_part.9.refs_2_ = f32[1024,1024]{1,0:T(8,128)S(1)} custom-call(bf16[2048,1152]{1,0:T(8,128)(2,1)S(1)} %bitcast_select_fusion.left_ref, bf16[1168,512]{1,0:T(8,128)(2,1)S(1)} %get-tuple-element.86.refs_0_.refs_2_, bf16[1168,512]{1,0:T(8,128)(2,1)S(1)} %get-tuple-element.87.refs_1_.refs_3_, bf16[384,512]{1,0:T(8,128)(2,1)S(1)} %collective-permute-done.13.refs_2_.refs_0_), custom_call_target="tpu_custom_call" | custom-call | flops 2415919104 | bytes 13107200 | tf_op jit(solution)/shard_map/weight_part/pallas_call | solution.py:451
  201.8 1.7 weight_part.8
  203.5 1.3 collective-permute-start.10
  204.8 1.6 collective-permute-done.14.refs_3_.refs_1_
  206.4 1.7 weight_part.10.refs_4_
  208.1 1.5 collective-permute-start.18
  209.7 3.8 %collective-permute-start.19 = (bf16[384,512]{1,0:T(8,128)(2,1)S(1)}, bf16[384,512]{1,0:T(8,128)(2,1)S(1)}, u32[]{:S(2)}, u32[]{:S(2)}) collective-permute-start(bf16[384,512]{1,0:T(8,128)(2,1)S(1)} %get-tuple-element.83.refs_0_), channel_id=1, source_target_pairs={{0,16},{1,1},{2,18},{3,3},{4,20},{5,5},{6,22},{7,7},{8,24},{9,9},{... | collective-permute-start | bytes 1179656 | tf_op jit(solution)/shard_map/ppermute | solution.py:38
  213.5 2.9 %collective-permute-start.20 = (bf16[384,512]{1,0:T(8,128)(2,1)S(1)}, bf16[384,512]{1,0:T(8,128)(2,1)S(1)}, u32[]{:S(2)}, u32[]{:S(2)}) collective-permute-start(bf16[384,512]{1,0:T(8,128)(2,1)S(1)} %get-tuple-element.84.refs_1_), channel_id=1, source_target_pairs={{0,16},{1,1},{2,18},{3,3},{4,20},{5,5},{6,22},{7,7},{8,24},{9,9},{... | collective-permute-start | bytes 1179656 | tf_op jit(solution)/shard_map/ppermute | solution.py:38
  216.4 1.7 weight_part.11.refs_2_.keep_ref
  218.2 1.7 weight_part.7.keep_ref
  220.0 0.5 slice-done.1
  220.5 4.9 %last_product.2.refs_1_ = bf16[384,2048]{1,0:T(8,128)(2,1)} custom-call(bf16[2048,2048]{1,0:T(8,128)(2,1)S(1)} %bitcast.25, bf16[1168,512]{1,0:T(8,128)(2,1)S(1)} %get-tuple-element.79.refs_0_.refs_3_, bf16[1168,512]{1,0:T(8,128)(2,1)S(1)} %get-tuple-element.80.refs_1_, bf16[1168,512]{1,0:T(8,128)(2,1)S(1)} %get-tuple-element.86.refs_0_.refs_2_, ...), custom_call_target="tpu_custom_call" | custom-call | flops 3221225472 | bytes 14680064 | tf_op jit(solution)/shard_map/last_product/pallas_call | solution.py:391
  225.4 2.7 collective-permute-done.10.got_ref
  228.2 1.4 copy-done.5
  229.9 2.0 collective-permute-start.15
  232.0 1.0 collective-permute-done.20.refs_1_.refs_3_
  233.2 9.5 %collective-permute-done.15.got_ref = bf16[272,1024]{1,0:T(8,128)(2,1)S(1)} collective-permute-done((bf16[272,1024]{1,0:T(8,128)(2,1)S(1)}, bf16[272,1024]{1,0:T(8,128)(2,1)S(1)}, u32[]{:S(2)}, u32[]{:S(2)}) %collective-permute-start.15) | collective-permute-done | bytes 557088 | tf_op jit(solution)/shard_map/ppermute | solution.py:30
  242.9 5.3 %collective-permute-done.21.got_ref = bf16[256,1024]{1,0:T(8,128)(2,1)S(1)} collective-permute-done((bf16[256,1024]{1,0:T(8,128)(2,1)S(1)}, bf16[256,1024]{1,0:T(8,128)(2,1)S(1)}, u32[]{:S(2)}, u32[]{:S(2)}) %collective-permute-start.21) | collective-permute-done | bytes 524320 | tf_op jit(solution)/shard_map/ppermute | solution.py:30
  248.3 2.6 collective-permute-start.22
  250.9 10.5 %collective-permute-done.22.got_ref = bf16[128,1024]{1,0:T(8,128)(2,1)S(1)} collective-permute-done((bf16[128,1024]{1,0:T(8,128)(2,1)S(1)}, bf16[128,1024]{1,0:T(8,128)(2,1)S(1)}, u32[]{:S(2)}, u32[]{:S(2)}) %collective-permute-start.22) | collective-permute-done | bytes 262176 | tf_op jit(solution)/shard_map/ppermute | solution.py:30
  261.5 1.7 collective-permute-start.23
  263.3 5.1 %last_product.3 = bf16[384,2048]{1,0:T(8,128)(2,1)} custom-call(bf16[2048,2048]{1,0:T(8,128)(2,1)S(1)} %bitcast.25, bf16[384,512]{1,0:T(8,128)(2,1)S(1)} %collective-permute-done.13.refs_2_.refs_0_, bf16[384,512]{1,0:T(8,128)(2,1)S(1)} %collective-permute-done.14.refs_3_.refs_1_, bf16[384,512]{1,0:T(8,128)(2,1)S(1)} %collective-permute-done.19.refs_0_.refs_2_, ...), custom_call_target="tpu_custom_call" | custom-call | flops 3221225472 | bytes 14680064 | tf_op jit(solution)/shard_map/last_product/pallas_call | solution.py:391
  268.4 2.4 collective-permute-done.17.got0
  270.8 0.8 last_stage.1
  (76 shorter events, 4.1 us)
Async XLA Ops:
  7.2 0.8 copy-start.12
  7.2 15.0 %copy-start.8 = (s32[256]{0:T(256)S(1)}, s32[256]{0:T(256)}, u32[]{:S(2)}) copy-start(s32[256]{0:T(256)} %home_ref.1) | copy-start | bytes 3076
  7.2 121.7 %all-gather.2.cloned.1.call-start = ((), (), s32[]{:S(2)}) async-start(), calls=%async_computation.2 | async-start | bytes 10485760 | tf_op jit(solution)/shard_map/all_gather | solution.py:559
  8.5 13.7 %all-to-all-start = ((s32[8,1,16]{2,1,0:T(1,128)}), s32[8,1,16]{2,1,0:T(1,128)S(1)}, u32[]{:S(2)}, u32[]{:S(2)}) async-start(s32[8,1,16]{2,1,0:T(1,128)} %broadcast_in_dim.24), calls=%async_computation | async-start | bytes 8192 | tf_op jit(solution)/shard_map/all_to_all | solution.py:544
  22.2 3.3 %copy-start.6 = (bf16[8,128,2048]{2,1,0:T(8,128)(2,1)S(1)}, bf16[8,128,2048]{2,1,0:T(8,128)(2,1)}, u32[]{:S(2)}) copy-start(bf16[8,128,2048]{2,1,0:T(8,128)(2,1)} %bank_ref.1) | copy-start | bytes 12582916
  29.3 2.0 copy-start.7
  31.3 5.0 %copy-start.10 = (bf16[384,2048]{1,0:T(8,128)(2,1)S(1)}, bf16[384,2048]{1,0:T(8,128)(2,1)}, u32[]{:S(2)}) copy-start(bf16[384,2048]{1,0:T(8,128)(2,1)} %param.7) | copy-start | bytes 4718596
  31.3 110.7 %all-to-all-start.1 = ((bf16[4,256,2048]{2,1,0:T(8,128)(2,1)}), bf16[4,256,2048]{2,1,0:T(8,128)(2,1)}, u32[]{:S(2)}, u32[]{:S(2)}) async-start(bf16[4,256,2048]{2,1,0:T(8,128)(2,1)} %bitcast.26), calls=%async_computation.1 | async-start | bytes 8388608 | tf_op jit(solution)/shard_map/all_to_all | solution.py:554
  37.2 4.6 %copy-start.9 = (bf16[384,2048]{1,0:T(8,128)(2,1)S(1)}, bf16[384,2048]{1,0:T(8,128)(2,1)}, u32[]{:S(2)}) copy-start(bf16[384,2048]{1,0:T(8,128)(2,1)} %param.8) | copy-start | bytes 4718596
  39.7 3.7 %copy-start.14 = (s32[32]{0:T(128)S(1)}, s32[32]{0:T(128)}, u32[]{:S(2)}) copy-start(s32[32]{0:T(128)} %constant.56) | copy-start | bytes 388
  39.7 3.9 %copy-start.13 = (s32[32,1]{0,1:T(1,128)S(1)}, s32[32,1]{0,1:T(1,128)}, u32[]{:S(2)}) copy-start(s32[32,1]{0,1:T(1,128)} %constant.59) | copy-start | bytes 388
  39.7 76.8 %collective-permute-start = (bf16[384,2048]{0,1:T(8,128)(2,1)}, bf16[384,2048]{0,1:T(8,128)(2,1)}, u32[]{:S(2)}, u32[]{:S(2)}) collective-permute-start(bf16[384,2048]{0,1:T(8,128)(2,1)} %broadcast_select_fusion), channel_id=1, source_target_pairs={{0,16},{1,1},{2,18},{3,3},{4,20},{5,5},{6,22},{7,7},{8,24},{9,9},{... | collective-permute-start | bytes 4718600 | tf_op jit(solution)/shard_map/ppermute | solution.py:38
  43.6 114.3 %collective-permute-start.5 = (bf16[256,2048]{1,0:T(8,128)(2,1)}, bf16[256,2048]{1,0:T(8,128)(2,1)}, u32[]{:S(2)}, u32[]{:S(2)}) collective-permute-start(bf16[256,2048]{1,0:T(8,128)(2,1)} %get-tuple-element.61), channel_id=1, source_target_pairs={{0,0},{1,17},{2,2},{3,19},{4,4},{5,21},{6,6},{7,23},{8,8},{9,25},{... | collective-permute-start | bytes 3145736 | tf_op jit(solution)/shard_map/ppermute | solution.py:38
  53.1 112.1 %collective-permute-start.4 = (bf16[256,2048]{1,0:T(8,128)(2,1)}, bf16[256,2048]{1,0:T(8,128)(2,1)S(1)}, u32[]{:S(2)}, u32[]{:S(2)}) collective-permute-start(bf16[256,2048]{1,0:T(8,128)(2,1)} %get-tuple-element.60), channel_id=1, source_target_pairs={{0,4},{1,21},{2,6},{3,23},{4,0},{5,17},{6,2},{7,19},{8,12},{9,29},... | collective-permute-start | bytes 3145736 | tf_op jit(solution)/shard_map/ppermute | solution.py:38
  55.1 110.7 %collective-permute-start.3 = (bf16[256,2048]{1,0:T(8,128)(2,1)}, bf16[256,2048]{1,0:T(8,128)(2,1)}, u32[]{:S(2)}, u32[]{:S(2)}) collective-permute-start(bf16[256,2048]{1,0:T(8,128)(2,1)} %get-tuple-element.59), channel_id=1, source_target_pairs={{0,8},{1,25},{2,10},{3,27},{4,12},{5,29},{6,14},{7,31},{8,0},{9,17... | collective-permute-start | bytes 3145736 | tf_op jit(solution)/shard_map/ppermute | solution.py:38
  56.5 111.1 %collective-permute-start.2 = (bf16[256,2048]{1,0:T(8,128)(2,1)}, bf16[256,2048]{1,0:T(8,128)(2,1)}, u32[]{:S(2)}, u32[]{:S(2)}) collective-permute-start(bf16[256,2048]{1,0:T(8,128)(2,1)} %get-tuple-element.58), channel_id=1, source_target_pairs={{0,12},{1,29},{2,14},{3,31},{4,8},{5,25},{6,10},{7,27},{8,4},{9,21... | collective-permute-start | bytes 3145736 | tf_op jit(solution)/shard_map/ppermute | solution.py:38
  128.9 42.9 %collective-permute-start.1 = (bf16[1024,1152]{1,0:T(8,128)(2,1)}, bf16[1024,1152]{1,0:T(8,128)(2,1)S(1)}, u32[]{:S(2)}, u32[]{:S(2)}) collective-permute-start(bf16[1024,1152]{1,0:T(8,128)(2,1)} %bitcast.8), channel_id=1, source_target_pairs={{0,1},{1,0},{2,3},{3,2},{4,5},{5,4},{6,7},{7,6},{8,9},{9,8},{10,11... | collective-permute-start | bytes 7077896 | tf_op jit(solution)/shard_map/ppermute | solution.py:30
  128.9 8.6 %copy-start = (bf16[2048,2048]{1,0:T(8,128)(2,1)S(1)}, bf16[2048,2048]{1,0:T(8,128)(2,1)}, u32[]{:S(2)}) copy-start(bf16[2048,2048]{1,0:T(8,128)(2,1)} %all-gather.2.cloned.1.call-done.w_ref) | copy-start | bytes 25165828
  128.9 8.6 %copy-start.11 = (bf16[384,2048]{1,0:T(8,128)(2,1)S(1)}, bf16[384,2048]{1,0:T(8,128)(2,1)}, u32[]{:S(2)}) copy-start(bf16[384,2048]{1,0:T(8,128)(2,1)} %param.7) | copy-start | bytes 4718596
  142.0 1.4 copy-start.1
  143.4 1.4 copy-start.3
  157.9 13.9 %collective-permute-start.7 = (f32[8,384]{1,0:T(8,128)S(1)}, f32[8,384]{1,0:T(8,128)S(1)}, u32[]{:S(2)}, u32[]{:S(2)}) collective-permute-start(f32[8,384]{1,0:T(8,128)S(1)} %get-tuple-element.57.mine_ref), channel_id=1, source_target_pairs={{0,16},{1,1},{2,18},{3,3},{4,20},{5,5},{6,22},{7,7},{8,24},{9,9},{... | collective-permute-start | bytes 36872 | tf_op jit(solution)/shard_map/ppermute | solution.py:38
  169.6 12.3 %collective-permute-start.6 = (f32[8,384]{1,0:T(8,128)S(1)}, f32[8,384]{1,0:T(8,128)S(1)}, u32[]{:S(2)}, u32[]{:S(2)}) collective-permute-start(f32[8,384]{1,0:T(8,128)S(1)} %get-tuple-element.66.mine_ref), channel_id=1, source_target_pairs={{0,16},{1,1},{2,18},{3,3},{4,20},{5,5},{6,22},{7,7},{8,24},{9,9},{... | collective-permute-start | bytes 36872 | tf_op jit(solution)/shard_map/ppermute | solution.py:38
  171.8 11.6 %copy-start.4 = (bf16[384,2048]{1,0:T(8,128)(2,1)S(1)}, bf16[384,2048]{1,0:T(8,128)(2,1)}, u32[]{:S(2)}) copy-start(bf16[384,2048]{1,0:T(8,128)(2,1)} %convolution_convert_fusion.2.refs_0_.q_ref) | copy-start | bytes 4718596
  176.9 6.5 %copy-start.2 = (bf16[384,2048]{1,0:T(8,128)(2,1)S(1)}, bf16[384,2048]{1,0:T(8,128)(2,1)}, u32[]{:S(2)}) copy-start(bf16[384,2048]{1,0:T(8,128)(2,1)} %convolution_convert_fusion.1.refs_2_.p_ref) | copy-start | bytes 4718596
  176.9 16.1 %collective-permute-start.13 = (bf16[384,512]{1,0:T(8,128)(2,1)S(1)}, bf16[384,512]{1,0:T(8,128)(2,1)S(1)}, u32[]{:S(2)}, u32[]{:S(2)}) collective-permute-start(bf16[384,512]{1,0:T(8,128)(2,1)S(1)} %get-tuple-element.76.refs_0_), channel_id=1, source_target_pairs={{0,16},{1,1},{2,18},{3,3},{4,20},{5,5},{6,22},{7,7},{8,24},{9,9},{... | collective-permute-start | bytes 1179656 | tf_op jit(solution)/shard_map/ppermute | solution.py:38
  187.0 4.9 %slice-start.2 = ((s8[4718592]{0:T(1024)(128)(4,1)}), s8[4194304]{0:T(1024)(128)(4,1)S(1)}, s32[]{:S(2)}) async-start(s8[4718592]{0:T(1024)(128)(4,1)} %bitcast.29), calls=%async_computation.5 | async-start | bytes 8388608
  187.0 4.9 %slice-start.3 = ((s8[4718592]{0:T(1024)(128)(4,1)}), s8[524288]{0:T(1024)(128)(4,1)S(1)}, s32[]{:S(2)}) async-start(s8[4718592]{0:T(1024)(128)(4,1)} %bitcast.29), calls=%async_computation.6 | async-start | bytes 1048576
  190.8 15.6 %collective-permute-start.11 = (bf16[1168,512]{1,0:T(8,128)(2,1)S(1)}, bf16[1168,512]{1,0:T(8,128)(2,1)S(1)}, u32[]{:S(2)}, u32[]{:S(2)}) collective-permute-start(bf16[1168,512]{1,0:T(8,128)(2,1)S(1)} %get-tuple-element.86.refs_0_.refs_2_), channel_id=1, source_target_pairs={{0,1},{1,0},{2,3},{3,2},{4,5},{5,4},{6,7},{7,6},{8,9},{9,8},{10,11... | collective-permute-start | bytes 3588104 | tf_op jit(solution)/shard_map/ppermute | solution.py:30
  190.9 15.5 %collective-permute-start.12 = (bf16[1168,512]{1,0:T(8,128)(2,1)S(1)}, bf16[1168,512]{1,0:T(8,128)(2,1)S(1)}, u32[]{:S(2)}, u32[]{:S(2)}) collective-permute-start(bf16[1168,512]{1,0:T(8,128)(2,1)S(1)} %get-tuple-element.87.refs_1_.refs_3_), channel_id=1, source_target_pairs={{0,1},{1,0},{2,3},{3,2},{4,5},{5,4},{6,7},{7,6},{8,9},{9,8},{10,11... | collective-permute-start | bytes 3588104 | tf_op jit(solution)/shard_map/ppermute | solution.py:30
  191.4 10.3 %collective-permute-start.8 = (bf16[1168,512]{1,0:T(8,128)(2,1)S(1)}, bf16[1168,512]{1,0:T(8,128)(2,1)S(1)}, u32[]{:S(2)}, u32[]{:S(2)}) collective-permute-start(bf16[1168,512]{1,0:T(8,128)(2,1)S(1)} %get-tuple-element.79.refs_0_.refs_3_), channel_id=1, source_target_pairs={{0,1},{1,0},{2,3},{3,2},{4,5},{5,4},{6,7},{7,6},{8,9},{9,8},{10,11... | collective-permute-start | bytes 3588104 | tf_op jit(solution)/shard_map/ppermute | solution.py:30
  191.5 10.3 %collective-permute-start.9 = (bf16[1168,512]{1,0:T(8,128)(2,1)S(1)}, bf16[1168,512]{1,0:T(8,128)(2,1)S(1)}, u32[]{:S(2)}, u32[]{:S(2)}) collective-permute-start(bf16[1168,512]{1,0:T(8,128)(2,1)S(1)} %get-tuple-element.80.refs_1_), channel_id=1, source_target_pairs={{0,1},{1,0},{2,3},{3,2},{4,5},{5,4},{6,7},{7,6},{8,9},{9,8},{10,11... | collective-permute-start | bytes 3588104 | tf_op jit(solution)/shard_map/ppermute | solution.py:30
  193.0 13.4 %collective-permute-start.14 = (bf16[384,512]{1,0:T(8,128)(2,1)S(1)}, bf16[384,512]{1,0:T(8,128)(2,1)S(1)}, u32[]{:S(2)}, u32[]{:S(2)}) collective-permute-start(bf16[384,512]{1,0:T(8,128)(2,1)S(1)} %get-tuple-element.77.refs_1_), channel_id=1, source_target_pairs={{0,16},{1,1},{2,18},{3,3},{4,20},{5,5},{6,22},{7,7},{8,24},{9,9},{... | collective-permute-start | bytes 1179656 | tf_op jit(solution)/shard_map/ppermute | solution.py:38
  203.5 24.7 %collective-permute-start.10 = (bf16[528,1024]{1,0:T(8,128)(2,1)S(1)}, bf16[528,1024]{1,0:T(8,128)(2,1)S(1)}, u32[]{:S(2)}, u32[]{:S(2)}) collective-permute-start(bf16[528,1024]{1,0:T(8,128)(2,1)S(1)} %get-tuple-element.81), channel_id=1, source_target_pairs={{0,2},{1,3},{2,0},{3,1},{4,6},{5,7},{6,4},{7,5},{8,10},{9,11},{10,... | collective-permute-start | bytes 3244040 | tf_op jit(solution)/shard_map/ppermute | solution.py:30
  208.1 24.8 %collective-permute-start.18 = (bf16[512,1024]{1,0:T(8,128)(2,1)S(1)}, bf16[512,1024]{1,0:T(8,128)(2,1)S(1)}, u32[]{:S(2)}, u32[]{:S(2)}) collective-permute-start(bf16[512,1024]{1,0:T(8,128)(2,1)S(1)} %weight_part.10.refs_4_), channel_id=1, source_target_pairs={{0,4},{4,0},{8,12},{12,8},{16,20},{20,16},{24,28},{28,24},{1,5},{5... | collective-permute-start | bytes 3145736 | tf_op jit(solution)/shard_map/ppermute | solution.py:30
  209.7 22.3 %collective-permute-start.19 = (bf16[384,512]{1,0:T(8,128)(2,1)S(1)}, bf16[384,512]{1,0:T(8,128)(2,1)S(1)}, u32[]{:S(2)}, u32[]{:S(2)}) collective-permute-start(bf16[384,512]{1,0:T(8,128)(2,1)S(1)} %get-tuple-element.83.refs_0_), channel_id=1, source_target_pairs={{0,16},{1,1},{2,18},{3,3},{4,20},{5,5},{6,22},{7,7},{8,24},{9,9},{... | collective-permute-start | bytes 1179656 | tf_op jit(solution)/shard_map/ppermute | solution.py:38
  213.5 19.4 %collective-permute-start.20 = (bf16[384,512]{1,0:T(8,128)(2,1)S(1)}, bf16[384,512]{1,0:T(8,128)(2,1)S(1)}, u32[]{:S(2)}, u32[]{:S(2)}) collective-permute-start(bf16[384,512]{1,0:T(8,128)(2,1)S(1)} %get-tuple-element.84.refs_1_), channel_id=1, source_target_pairs={{0,16},{1,1},{2,18},{3,3},{4,20},{5,5},{6,22},{7,7},{8,24},{9,9},{... | collective-permute-start | bytes 1179656 | tf_op jit(solution)/shard_map/ppermute | solution.py:38
  216.4 3.5 %slice-start = ((s8[8388608]{0:T(1024)(128)(4,1)}), s8[4194304]{0:T(1024)(128)(4,1)S(1)}, s32[]{:S(2)}) async-start(s8[8388608]{0:T(1024)(128)(4,1)} %bitcast.24), calls=%async_computation.3 | async-start | bytes 8388608
  218.2 2.3 slice-start.1
  228.2 1.4 copy-start.5
  229.9 12.7 %collective-permute-start.15 = (bf16[272,1024]{1,0:T(8,128)(2,1)S(1)}, bf16[272,1024]{1,0:T(8,128)(2,1)S(1)}, u32[]{:S(2)}, u32[]{:S(2)}) collective-permute-start(bf16[272,1024]{1,0:T(8,128)(2,1)S(1)} %get-tuple-element.89), channel_id=1, source_target_pairs={{0,4},{4,0},{8,12},{12,8},{16,20},{20,16},{24,28},{28,24},{1,5},{5... | collective-permute-start | bytes 1671176 | tf_op jit(solution)/shard_map/ppermute | solution.py:30
  233.1 15.1 %collective-permute-start.21 = (bf16[256,1024]{1,0:T(8,128)(2,1)S(1)}, bf16[256,1024]{1,0:T(8,128)(2,1)S(1)}, u32[]{:S(2)}, u32[]{:S(2)}) collective-permute-start(bf16[256,1024]{1,0:T(8,128)(2,1)S(1)} %get-tuple-element.97), channel_id=1, source_target_pairs={{0,8},{4,12},{8,0},{12,4},{16,24},{20,28},{24,16},{28,20},{1,9},{5... | collective-permute-start | bytes 1572872 | tf_op jit(solution)/shard_map/ppermute | solution.py:30
  242.8 20.3 %collective-permute-start.16 = (bf16[144,1024]{1,0:T(8,128)(2,1)S(1)}, bf16[144,1024]{1,0:T(8,128)(2,1)S(1)}, u32[]{:S(2)}, u32[]{:S(2)}) collective-permute-start(bf16[144,1024]{1,0:T(8,128)(2,1)S(1)} %get-tuple-element.92), channel_id=1, source_target_pairs={{0,8},{4,12},{8,0},{12,4},{16,24},{20,28},{24,16},{28,20},{1,9},{5... | collective-permute-start | bytes 884744 | tf_op jit(solution)/shard_map/ppermute | solution.py:30
  248.3 13.1 %collective-permute-start.22 = (bf16[128,1024]{1,0:T(8,128)(2,1)S(1)}, bf16[128,1024]{1,0:T(8,128)(2,1)S(1)}, u32[]{:S(2)}, u32[]{:S(2)}) collective-permute-start(bf16[128,1024]{1,0:T(8,128)(2,1)S(1)} %get-tuple-element.99), channel_id=1, source_target_pairs={{0,16},{4,20},{8,24},{12,28},{16,0},{20,4},{24,8},{28,12},{1,17},{... | collective-permute-start | bytes 786440 | tf_op jit(solution)/shard_map/ppermute | solution.py:30
  261.5 7.0 %collective-permute-start.23 = (bf16[64,1024]{1,0:T(8,128)(2,1)S(1)}, bf16[64,1024]{1,0:T(8,128)(2,1)S(1)}, u32[]{:S(2)}, u32[]{:S(2)}) collective-permute-start(bf16[64,1024]{1,0:T(8,128)(2,1)S(1)} %get-tuple-element.101.refs_6_), channel_id=1, source_target_pairs={{0,2},{1,3},{2,0},{3,1},{4,6},{5,7},{6,4},{7,5},{8,10},{9,11},{10,... | collective-permute-start | bytes 393224 | tf_op jit(solution)/shard_map/ppermute | solution.py:30
  263.2 7.6 %collective-permute-start.17 = (bf16[80,1024]{1,0:T(8,128)(2,1)S(1)}, bf16[80,1024]{1,0:T(8,128)(2,1)S(1)}, u32[]{:S(2)}, u32[]{:S(2)}) collective-permute-start(bf16[80,1024]{1,0:T(8,128)(2,1)S(1)} %get-tuple-element.95.refs_5_), channel_id=1, source_target_pairs={{0,16},{4,20},{8,24},{12,28},{16,0},{20,4},{24,8},{28,12},{1,17},{... | collective-permute-start | bytes 491528 | tf_op jit(solution)/shard_map/ppermute | solution.py:30
Sparse Core Ops, SparseCore 0:
  9.6 60.9 all-gather.1

commit v4 on v2

--- a/solution.py
+++ b/solution.py
@@ -19,7 +19,7 @@
 F32 = jnp.float32
 BF16 = jnp.bfloat16
 
-VMEM_LIMIT = 24 * 1024 * 1024
+VMEM_LIMIT = 20 * 1024 * 1024
 
 
 def bits_of(size):
@@ -30,10 +30,13 @@
     return lax.ppermute(x, axis, [(i, i ^ bit) for i in range(lax.axis_size(axis))])
 
 
-def move(x, bit_of):
+def move(x, bit_of, stay=True):
     n_dp, n_fsdp = lax.axis_size("dp"), lax.axis_size("fsdp")
     pairs = [
-        (i * n_fsdp + f, (i ^ bit_of(f)) * n_fsdp + f) for i in range(n_dp) for f in range(n_fsdp)
+        (i * n_fsdp + f, (i ^ bit_of(f)) * n_fsdp + f)
+        for i in range(n_dp)
+        for f in range(n_fsdp)
+        if stay or bit_of(f)
     ]
     return lax.ppermute(x, ("dp", "fsdp"), pairs)
 
@@ -114,16 +117,19 @@
     )(ids, block_home, me.reshape(1), bank)
 
 
-def part_scores(emb, x, rows, held, scale, emb_p=None, before=None, pack=False, after=()):
-    count, width = emb.shape
+def part_scores(
+    emb, count, x, rows, held, scale, near=False, before=None, pack=False, after=(), other=()
+):
+    width = emb.shape[1]
     sets = x.shape[0] // rows
 
     def kernel(*refs):
         refs = list(refs)
         held_ref = refs.pop(0) if held is not None else None
         emb_ref, x_ref = refs.pop(0), refs.pop(0)
-        p_ref = refs.pop(0) if emb_p is not None else None
+        p_ref = refs.pop(0) if near else None
         before_ref = refs.pop(0) if before is not None else None
+        other_refs = [refs.pop(0) for _ in other]
         del refs[: len(after)]
         out, stats, state = refs[0], refs[1], refs[-1]
         step = pl.program_id(0)
@@ -143,12 +149,15 @@
             else:
                 state[:, :128] = jnp.full((count, 128), NEG_BIG, F32)
                 state[:, 128:] = jnp.zeros((count, 128), F32)
-            if emb_p is not None:
+            if near:
                 inner = dot_t(emb_ref[...], p_ref[...]) * scale
                 refs[2][...] = inner
                 fold(inner)
 
-        s = dot_t(emb_ref[...], x_ref[...]) * scale
+        cand = x_ref[...]
+        if other:
+            cand = lax.select(other_refs[0][0] > 0, cand, other_refs[1][...])
+        s = dot_t(emb_ref[...], cand) * scale
         if held is not None:
             col = lax.broadcasted_iota(jnp.int32, s.shape, 1)
             s = jnp.where(col < held_ref[step], s, NEG_BIG)
@@ -167,11 +176,19 @@
                 stats[...] = state[...]
 
     whole = lambda a: pl.BlockSpec(a.shape, lambda i: (0, 0))
-    args, in_specs = [emb, x], [whole(emb), pl.BlockSpec((rows, width), lambda i: (i, 0))]
-    for a in (emb_p, before):
-        if a is not None:
-            args.append(a)
-            in_specs.append(whole(a))
+    args = [emb, x]
+    in_specs = [pl.BlockSpec((count, width), lambda i: (0, 0))]
+    in_specs.append(pl.BlockSpec((rows, width), lambda i: (i, 0)))
+    if near:
+        args.append(emb)
+        in_specs.append(pl.BlockSpec((count, width), lambda i: (1, 0)))
+    if before is not None:
+        args.append(before)
+        in_specs.append(whole(before))
+    if other:
+        args += other
+        in_specs.append(pl.BlockSpec(memory_space=pltpu.SMEM))
+        in_specs.append(pl.BlockSpec((rows, width), lambda i: (i, 0)))
     args += after
     in_specs += [ANY] * len(after)
     if held is not None:
@@ -186,7 +203,7 @@
         pl.BlockSpec((count, rows), lambda i: (0, i)),
         pl.BlockSpec(stats_shape, lambda i: (0, 0)),
     ]
-    if emb_p is not None:
+    if near:
         out_shape.append(jax.ShapeDtypeStruct((count, count), F32))
         out_specs.append(pl.BlockSpec((count, count), lambda i: (0, 0)))
     return pl.pallas_call(
@@ -227,7 +244,7 @@
     return jnp.sum(x[:, :128].astype(F32), axis=0, keepdims=True)[:, :1]
 
 
-def guest_rows(mine, there, scores, guests, stays, scale, tile, after):
+def guest_rows(mine, there, scores, guests, stay, stays, scale, tile, after):
     count = mine.shape[1]
     n = len(guests)
     part, width = guests[0].shape
@@ -235,7 +252,7 @@
 
     def kernel(stays_ref, mine_ref, there_ref, *refs):
         s_refs, x_refs = refs[:n], refs[n : 2 * n]
-        full, backs, probs = refs[2 * n + 1], refs[2 * n + 2 : -1], refs[-1]
+        stay_ref, full, backs, probs = refs[2 * n], refs[2 * n + 2], refs[2 * n + 3 : -1], refs[-1]
 
         @pl.when(pl.program_id(0) == 0)
         def _():
@@ -248,8 +265,11 @@
 
         far = jnp.zeros((count, tile), F32)
         for k in range(n):
+            x = x_refs[k][...]
+            if k == 0:
+                x = lax.select(stays_ref[0] > 0, x, stay_ref[...])
             far += jnp.dot(
-                probs[:, k * part : (k + 1) * part], x_refs[k][...], preferred_element_type=F32
+                probs[:, k * part : (k + 1) * part], x, preferred_element_type=F32
             )
         full[...] = far
         far = jnp.where(stays_ref[0] > 0, 0.0, far).astype(BF16)
@@ -265,7 +285,7 @@
         grid=(tiles,),
         in_specs=[pl.BlockSpec(memory_space=pltpu.SMEM), whole(mine), whole(there)]
         + [whole(s) for s in scores]
-        + [pl.BlockSpec((part, tile), lambda i: (0, i))] * n
+        + [pl.BlockSpec((part, tile), lambda i: (0, i))] * (n + 1)
         + [ANY],
         out_specs=[pl.BlockSpec((count, tile), lambda i: (0, i))]
         + [pl.BlockSpec((count, tile), lambda i: (0, 0))] * tiles,
@@ -279,7 +299,7 @@
             transcendentals=count * n * part,
         ),
         name="guest_rows",
-    )(stays, mine, there, *scores, *guests, after)
+    )(stays, mine, there, *scores, *guests, stay, after)
 
 
 def own_grads(mine, there, inner, own, scale):
@@ -313,7 +333,7 @@
     )(mine, there, inner, own)
 
 
-def grad_rows(p_own, near, near_t, own, emb_q, emb_p, far, backs, loss, stays, tile, start, before):
+def grad_rows(p_own, near, near_t, own, emb, far, backs, loss, stays, tile, start, before):
     count = near.shape[0]
     tiles = len(backs)
     total, width = own.shape
@@ -338,14 +358,14 @@
                 outs[i][3 * count :] = tail
 
     whole = lambda a: pl.BlockSpec(a.shape, lambda i: (0, 0))
-    cut = lambda r: pl.BlockSpec((r, tile), lambda i: (0, start + i))
-    args = [stays, p_own, near, near_t, own, emb_q, emb_p, far, *backs, loss, *before]
+    cut = lambda r, at=0: pl.BlockSpec((r, tile), lambda i: (at, start + i))
+    args = [stays, p_own, near, near_t, own, emb, emb, far, *backs, loss, *before]
     return pl.pallas_call(
         kernel,
         grid=(tiles,),
         in_specs=[pl.BlockSpec(memory_space=pltpu.SMEM)]
         + [whole(p_own), whole(near), whole(near_t), cut(total)]
-        + [cut(count)] * 3
+        + [cut(count), cut(count, 1), cut(count)]
         + [whole(b) for b in backs]
         + [whole(loss)]
         + [ANY] * len(before),
@@ -540,11 +560,14 @@
         jnp.broadcast_to(neg_ids, (n_dp, named)), "dp", split_axis=0, concat_axis=0, tiled=True
     )
     leaving = jnp.where(ids[0, 0] < 0, jnp.zeros_like(queries), queries)
-    visit = move(leaving, trip)
+    visit = jnp.where(core == 0, move(leaving, trip, stay=False), queries)
     own, *guests, zero = pick_blocks(bank, ids, block_home, me, n_dp, n_fsdp)
+    stay = guests[0]
     guests = [
-        move(g, lambda f, k=k: k if f % 2 == 0 else k ^ half) for k, g in enumerate(guests)
+        move(g, lambda f, k=k: k if f % 2 == 0 else k ^ half, stay=False)
+        for k, g in enumerate(guests)
     ]
+    stays = core.astype(jnp.int32).reshape(1)
     sides = [list(range(half)), list(range(half, n_dp))]
     own = lax.all_to_all(
         own, "dp", split_axis=0, concat_axis=0, tiled=True, axis_index_groups=sides
@@ -552,8 +575,8 @@
     late = jnp.where(zero[0, 0] < 0, jnp.zeros_like(passages), passages)
 
     full_weight = lax.all_gather(weight, "fsdp", axis=0, tiled=True)
-    emb_q = jnp.dot(queries, full_weight, preferred_element_type=F32).astype(BF16)
-    emb_p = jnp.dot(passages, full_weight, preferred_element_type=F32).astype(BF16)
+    both = jnp.concatenate([queries, passages], axis=0)
+    emb = jnp.dot(both, full_weight, preferred_element_type=F32).astype(BF16)
     emb_v = jnp.dot(visit, full_weight, preferred_element_type=F32).astype(BF16)
 
     f_bits = [("fsdp", b) for b in bits_of(n_fsdp)]
@@ -583,22 +606,30 @@
         guest_held = [held(me ^ half ^ far, me ^ k ^ far).reshape(1) for k in range(half)]
     rows = CAP * block_rows
     s_own, own_stats, inner = part_scores(
-        emb_q, own, rows, own_held, scale, emb_p=emb_p, pack=True
+        emb, count, own, rows, own_held, scale, near=True, pack=True
     )
     their_stats = move(own_stats, trip)
     s_guest, stats = [], None
     for k, x in enumerate(guests):
         after = (inner,) if k == half // 2 else ()
         s, stats = part_scores(
-            emb_v, x, rows, guest_held[k], scale, before=stats, pack=k == half - 1, after=after
+            emb_v,
+            count,
+            x,
+            rows,
+            guest_held[k],
+            scale,
+            before=stats,
+            pack=k == half - 1,
+            after=after,
+            other=(stays, stay) if k == 0 else (),
         )
         s_guest.append(s)
 
     far_stats = move(stats, trip)
     tile = width // 4
-    stays = core.astype(jnp.int32).reshape(1)
     far, *backs = guest_rows(
-        stats, their_stats, s_guest, guests, stays, scale, tile, left_in
+        stats, their_stats, s_guest, guests, stay, stays, scale, tile, left_in
     )
     home = [move(r, trip) for r in backs]
     p_own, near, near_t, loss = own_grads(own_stats, far_stats, inner, s_own, scale)
@@ -609,8 +640,7 @@
             near,
             near_t,
             own,
-            emb_q,
-            emb_p,
+            emb,
             far,
             backs[2 * i : 2 * i + 2],
             loss,

time: 279 us -> 281 us (level)
  waiting for transfers between devices: 92.4 us -> 105 us
  starting transfers between devices: 60.2 us -> 53.3 us
  matrix products: 20.4 us -> 13.5 us
  Pallas kernels: 55.3 us -> 61.8 us
    ppermute x11, waiting for transfers between devices: 59.6 us -> 72.1 us  [move(): return lax.ppermute(x, ('dp', 'fsdp'), pairs)]
    ppermute x11, starting transfers between devices: 36.2 us -> 30.3 us  [move(): return lax.ppermute(x, ('dp', 'fsdp'), pairs)]
    pallas_call x6, Pallas kernels: 13.7 us -> 17.9 us  [weight_part(): pl.pallas_call(kernel, grid=(m,), in_specs=in_specs, out_specs=out_specs,...]
    dot_general x1, matrix products: 7.34 us -> 3.52 us  [body(): emb_v = jnp.dot(visit, full_weight, preferred_element_type=F32).astype(BF16)]
    dot_general x2 -> x1, matrix products: 13 us -> 10 us  [body(): emb = jnp.dot(both, full_weight, preferred_element_type=F32).astype(BF16)]
    unnamed x40 -> x26, local copies, waits for them, and re-layouts: 12.6 us -> 9.84 us
  transfers between devices with their start and end apart: 27 -> 27, of which waited for: 10 -> 11; matrix products, arithmetic and copies ran while one was open for 15% -> 12% of each run, Pallas kernels for 20% -> 22%
where the time goes in v4:
time: 281 us; the launch traced here: 280 us
  waiting for transfers between devices  105 us (37%)
  Pallas kernels  61.8 us (22%)
  starting transfers between devices  53.3 us (19%)
  local copies, waits for them, and re-layouts  18.4 us (7%)
  between operations  17.6 us (6%)
  matrix products  13.5 us (5%)
  other arithmetic  10.1 us (4%)
    ppermute x11, waiting for transfers between devices, move(): return lax.ppermute(x, ('dp', 'fsdp'), pairs)  72.1 us
    ppermute x11, starting transfers between devices, move(): return lax.ppermute(x, ('dp', 'fsdp'), pairs)  30.3 us
    ppermute x13, waiting for transfers between devices, swap(): lax.ppermute(x, axis, [(i, i ^ bit) for i in range(lax.axis_size(axis))])  26 us
    pallas_call x6, Pallas kernels, weight_part(): pl.pallas_call(kernel, grid=(m,), in_specs=in_specs, out_specs=out_specs,...  17.9 us
    pallas_call x5, Pallas kernels, part_scores(): pl.pallas_call(kernel, grid=(sets,), in_specs=in_specs, out_specs=out_spe...  14 us
    ppermute x13, starting transfers between devices, swap(): lax.ppermute(x, axis, [(i, i ^ bit) for i in range(lax.axis_size(axis))])  10.8 us
    pallas_call x2, Pallas kernels, last_product(): pl.pallas_call(kernel, grid=(kin // tile,), in_specs=in_specs + [ANY] * l...  10.1 us
    dot_general x1, matrix products, body(): emb = jnp.dot(both, full_weight, preferred_element_type=F32).astype(BF16)  10 us
  transfers between devices with their start and end apart: 27, of which 11 were waited for; matrix products, arithmetic and copies ran while one was open for 12% of the time, Pallas kernels for 22%

profile of v4, /device:TPU:0, one launch (start us, length us, event | category | flops | bytes accessed | tf_op | source)
XLA Modules:
  0.0 279.9 jit_solution(9557913763319451001)
XLA Ops:
  7.2 0.7 all-gather.2.cloned.1.call-update
  7.9 1.3 broadcast_in_dim.24
  9.1 7.3 %all-to-all-start = ((s32[8,1,16]{2,1,0:T(1,128)}), s32[8,1,16]{2,1,0:T(1,128)S(1)}, u32[]{:S(2)}, u32[]{:S(2)}) async-start(s32[8,1,16]{2,1,0:T(1,128)} %broadcast_in_dim.24), calls=%async_computation | async-start | bytes 8192 | tf_op jit(solution)/shard_map/all_to_all | solution.py:559
  16.4 6.4 %all-to-all-done = s32[8,1,16]{2,1,0:T(1,128)S(1)} async-done(((s32[8,1,16]{2,1,0:T(1,128)}), s32[8,1,16]{2,1,0:T(1,128)S(1)}, u32[]{:S(2)}, u32[]{:S(2)}) %all-to-all-start) | async-done | bytes 544 | tf_op jit(solution)/shard_map/all_to_all | solution.py:559
  22.8 2.8 copy-done.2
  25.6 0.7 copy-done.4
  26.3 3.9 %pick_blocks.1 = (bf16[1024,2048]{1,0:T(8,128)(2,1)S(1)}, bf16[256,2048]{1,0:T(8,128)(2,1)}, bf16[256,2048]{1,0:T(8,128)(2,1)}, bf16[256,2048]{1,0:T(8,128)(2,1)...) custom-call(s32[8,16]{1,0:T(8,128)S(1)} %bitcast.22, s32[256]{0:T(256)S(1)} %copy-done.4, s32[1]{0:T(128)} %bitcast.2.me_ref, ...), custom_call_target="tpu_custom_call" | custom-call | bytes 16777216 | tf_op jit(solution)/shard_map/pick_blocks/pallas_call | solution.py:99
  30.2 2.0 copy-done.3
  32.2 5.0 %all-to-all-start.1 = ((bf16[4,256,2048]{2,1,0:T(8,128)(2,1)}), bf16[4,256,2048]{2,1,0:T(8,128)(2,1)}, u32[]{:S(2)}, u32[]{:S(2)}) async-start(bf16[4,256,2048]{2,1,0:T(8,128)(2,1)} %bitcast.21), calls=%async_computation.1 | async-start | bytes 8388608 | tf_op jit(solution)/shard_map/all_to_all | solution.py:572
  37.2 0.9 copy.19
  38.1 0.5 slice.16
  39.2 1.3 broadcast_select_fusion
  40.5 2.5 collective-permute-start
  43.1 1.9 copy.16
  45.2 1.7 collective-permute-start.5
  46.8 2.0 collective-permute-start.4
  48.8 1.5 collective-permute-start.3
  50.3 0.5 slice.15
  51.6 65.7 %collective-permute-done = bf16[384,2048]{0,1:T(8,128)(2,1)} collective-permute-done((bf16[384,2048]{0,1:T(8,128)(2,1)}, bf16[384,2048]{0,1:T(8,128)(2,1)}, u32[]{:S(2)}, u32[]{:S(2)}) %collective-permute-start) | collective-permute-done | bytes 1572896 | tf_op jit(solution)/shard_map/ppermute | solution.py:41
  117.3 1.6 broadcast_select_fusion.1
  118.9 2.5 pad_maximum_fusion
  121.6 5.6 %gather_fusion = bf16[32,64,1152]{2,1,0:T(8,128)(2,1)} fusion(bf16[32,64,1152]{2,1,0:T(8,128)(2,1)} %bitcast.26, s32[1024]{0:T(1024)S(1)} %pad_clamp_fusion), kind=kCustom, calls=%fused_computation | custom fusion | bytes 9437312 | tf_op jit(solution)/shard_map/jit(_take)/gather | solution.py:596
  127.2 3.4 %slice_select_fusion = bf16[16,64,1152]{2,1,0:T(8,128)(2,1)} fusion(bf16[32,64,1152]{2,1,0:T(8,128)(2,1)} %gather_fusion, pred[16]{0:T(512)(128)(4,1)S(1)} %bitcast.27), kind=kLoop, calls=%fused_computation.8 | loop fusion | flops 1179648 | bytes 4718608 | tf_op jit(solution)/shard_map/jit(_take)/select_n | solution.py:596
  130.7 10.0 %convolution_convert_fusion.refs_0_.refs_2_.q_ref.p_ref = bf16[768,2048]{1,0:T(8,128)(2,1)S(1)} fusion(bf16[2048,2048]{1,0:T(8,128)(2,1)} %all-gather.2.cloned.1.call-done.w_ref, bf16[384,2048]{1,0:T(8,128)(2,1)} %param.8, bf16[384,2048]{1,0:T(8,128)(2,1)} %param.7), kind=kOutput, calls=%fused_computation.3 | convolution fusion | flops 6450315264 | bytes 14680064 | tf_op jit(solution)/shard_map/dot_general | solution.py:579
  140.7 6.2 %part_scores.5 = (f32[384,1024]{1,0:T(8,128)S(1)}, f32[8,384]{1,0:T(8,128)S(1)}, f32[384,384]{1,0:T(8,128)S(1)}) custom-call(bf16[768,2048]{1,0:T(8,128)(2,1)S(1)} %convolution_convert_fusion.refs_0_.refs_2_.q_ref.p_ref, bf16[1024,2048]{1,0:T(8,128)(2,1)} %bitcast.11.refs_1_.x_ref, bf16[768,2048]{1,0:T(8,128)(2,1)S(1)} %convolution_convert_fusion.refs_0_.refs_2_.q_ref.p_ref), custom_call_target="tpu_custom_call" | custom-call | flops 1610612736 | bytes 5767168 | tf_op jit(solution)/shard_map/part_scores/pallas_call | solution.py:209
  146.9 3.5 %convolution_convert_fusion.1.refs_0_ = bf16[384,2048]{1,0:T(8,128)(2,1)S(1)} fusion(bf16[384,2048]{0,1:T(8,128)(2,1)S(1)} %copy-done.6, bf16[2048,2048]{1,0:T(8,128)(2,1)S(1)} %copy-done), kind=kOutput, calls=%fused_computation.7 | convolution fusion | flops 3222011904 | bytes 11534336 | tf_op jit(solution)/shard_map/dot_general | solution.py:580
  150.5 5.5 %collective-permute-start.7 = (f32[8,384]{1,0:T(8,128)S(1)}, f32[8,384]{1,0:T(8,128)S(1)}, u32[]{:S(2)}, u32[]{:S(2)}) collective-permute-start(f32[8,384]{1,0:T(8,128)S(1)} %get-tuple-element.57.mine_ref), channel_id=1, source_target_pairs={{0,16},{1,1},{2,18},{3,3},{4,20},{5,5},{6,22},{7,7},{8,24},{9,9},{... | collective-permute-start | bytes 36872 | tf_op jit(solution)/shard_map/ppermute | solution.py:41
  156.0 2.2 part_scores.6
  158.2 1.9 part_scores.7
  160.1 1.9 part_scores.8
  161.9 3.8 %collective-permute-done.2.refs_1_.refs_7_ = bf16[256,2048]{1,0:T(8,128)(2,1)} collective-permute-done((bf16[256,2048]{1,0:T(8,128)(2,1)}, bf16[256,2048]{1,0:T(8,128)(2,1)}, u32[]{:S(2)}, u32[]{:S(2)}) %collective-permute-start.2) | collective-permute-done | bytes 1048608 | tf_op jit(solution)/shard_map/ppermute | solution.py:41
  165.8 2.0 part_scores.9
  167.7 2.2 collective-permute-start.6
  170.0 5.4 %guest_rows.1 = (f32[384,2048]{1,0:T(8,128)S(1)}, bf16[384,512]{1,0:T(8,128)(2,1)S(1)}, bf16[384,512]{1,0:T(8,128)(2,1)S(1)}, bf16[384,512]{1,0:T(8,128)(2,1)S(1)}, bf16[384,512]{1,0:T(8,128)(2,1)S(1)}) custom-call(s32[1]{0:T(128)} %bitcast.9.refs_2_.stays_ref, f32[8,384]{1,0:T(8,128)S(1)} %get-tuple-element.66.mine_ref, ...), custom_call_target="tpu_custom_call" | custom-call | flops 1610612736 | bytes 8912896 | tf_op jit(solution)/shard_map/guest_rows/pallas_call | solution.py:283
  175.4 4.5 %collective-permute-start.13 = (bf16[384,512]{1,0:T(8,128)(2,1)S(1)}, bf16[384,512]{1,0:T(8,128)(2,1)S(1)}, u32[]{:S(2)}, u32[]{:S(2)}) collective-permute-start(bf16[384,512]{1,0:T(8,128)(2,1)S(1)} %get-tuple-element.76.refs_0_), channel_id=1, source_target_pairs={{0,16},{1,1},{2,18},{3,3},{4,20},{5,5},{6,22},{7,7},{8,24},{9,9},{... | collective-permute-start | bytes 1179656 | tf_op jit(solution)/shard_map/ppermute | solution.py:41
  179.9 1.5 own_grads.1
  181.4 3.6 %grad_rows.2 = (bf16[1168,512]{1,0:T(8,128)(2,1)S(1)}, bf16[1168,512]{1,0:T(8,128)(2,1)S(1)}, f32[384,2048]{1,0:T(8,128)S(1)}) custom-call(s32[1]{0:T(128)} %bitcast.9.refs_2_.stays_ref, bf16[384,1024]{1,0:T(8,128)(2,1)S(1)} %get-tuple-element.68.own_ref, bf16[384,384]{1,0:T(8,128)(2,1)S(1)} %get-tuple-element.69.near_ref, ...), custom_call_target="tpu_custom_call" | custom-call | flops 1409286144 | bytes 9961472 | tf_op jit(solution)/shard_map/grad_rows/pallas_call | solution.py:363
  185.0 3.7 %grad_rows.3 = (bf16[1168,512]{1,0:T(8,128)(2,1)S(1)}, bf16[1168,512]{1,0:T(8,128)(2,1)S(1)}, f32[384,2048]{1,0:T(8,128)S(1)}) custom-call(s32[1]{0:T(128)} %bitcast.9.refs_2_.stays_ref, bf16[384,1024]{1,0:T(8,128)(2,1)S(1)} %get-tuple-element.68.own_ref, bf16[384,384]{1,0:T(8,128)(2,1)S(1)} %get-tuple-element.69.near_ref, ...), custom_call_target="tpu_custom_call", output_to_operand_aliasing={{2}: (11, {})} | custom-call | flops 1409286144 | bytes 9961472 | tf_op jit(solution)/shard_map/grad_rows/pallas_call | solution.py:363
  189.8 1.1 bitcast_select_fusion.left_ref
  190.9 3.4 %collective-permute-start.14 = (bf16[384,512]{1,0:T(8,128)(2,1)S(1)}, bf16[384,512]{1,0:T(8,128)(2,1)S(1)}, u32[]{:S(2)}, u32[]{:S(2)}) collective-permute-start(bf16[384,512]{1,0:T(8,128)(2,1)S(1)} %get-tuple-element.77.refs_1_), channel_id=1, source_target_pairs={{0,16},{1,1},{2,18},{3,3},{4,20},{5,5},{6,22},{7,7},{8,24},{9,9},{... | collective-permute-start | bytes 1179656 | tf_op jit(solution)/shard_map/ppermute | solution.py:41
  194.3 3.4 %weight_part.6.refs_2_ = f32[1024,1024]{1,0:T(8,128)S(1)} custom-call(bf16[2048,1152]{1,0:T(8,128)(2,1)S(1)} %bitcast_select_fusion.left_ref, bf16[1168,512]{1,0:T(8,128)(2,1)S(1)} %get-tuple-element.79.refs_0_.refs_3_, bf16[1168,512]{1,0:T(8,128)(2,1)S(1)} %get-tuple-element.80.refs_1_), custom_call_target="tpu_custom_call" | custom-call | flops 2415919104 | bytes 13107200 | tf_op jit(solution)/shard_map/weight_part/pallas_call | solution.py:471
  197.7 3.4 %weight_part.9.refs_2_ = f32[1024,1024]{1,0:T(8,128)S(1)} custom-call(bf16[2048,1152]{1,0:T(8,128)(2,1)S(1)} %bitcast_select_fusion.left_ref, bf16[1168,512]{1,0:T(8,128)(2,1)S(1)} %get-tuple-element.86.refs_0_.refs_2_, bf16[1168,512]{1,0:T(8,128)(2,1)S(1)} %get-tuple-element.87.refs_1_.refs_3_, bf16[384,512]{1,0:T(8,128)(2,1)S(1)} %collective-permute-done.13.refs_2_.refs_0_), custom_call_target="tpu_custom_call" | custom-call | flops 2415919104 | bytes 13107200 | tf_op jit(solution)/shard_map/weight_part/pallas_call | solution.py:471
  201.1 2.8 weight_part.8
  203.9 1.5 collective-permute-start.10
  205.7 2.8 weight_part.10.refs_4_
  208.5 0.6 collective-permute-start.18
  209.1 2.9 %collective-permute-start.19 = (bf16[384,512]{1,0:T(8,128)(2,1)S(1)}, bf16[384,512]{1,0:T(8,128)(2,1)S(1)}, u32[]{:S(2)}, u32[]{:S(2)}) collective-permute-start(bf16[384,512]{1,0:T(8,128)(2,1)S(1)} %get-tuple-element.83.refs_0_), channel_id=1, source_target_pairs={{0,16},{1,1},{2,18},{3,3},{4,20},{5,5},{6,22},{7,7},{8,24},{9,9},{... | collective-permute-start | bytes 1179656 | tf_op jit(solution)/shard_map/ppermute | solution.py:41
  212.1 4.0 %collective-permute-start.20 = (bf16[384,512]{1,0:T(8,128)(2,1)S(1)}, bf16[384,512]{1,0:T(8,128)(2,1)S(1)}, u32[]{:S(2)}, u32[]{:S(2)}) collective-permute-start(bf16[384,512]{1,0:T(8,128)(2,1)S(1)} %get-tuple-element.84.refs_1_), channel_id=1, source_target_pairs={{0,16},{1,1},{2,18},{3,3},{4,20},{5,5},{6,22},{7,7},{8,24},{9,9},{... | collective-permute-start | bytes 1179656 | tf_op jit(solution)/shard_map/ppermute | solution.py:41
  216.1 2.8 weight_part.11.refs_2_.keep_ref
  218.9 2.8 weight_part.7.keep_ref
  221.7 5.0 %last_product.2.refs_1_ = bf16[384,2048]{1,0:T(8,128)(2,1)} custom-call(bf16[2048,2048]{1,0:T(8,128)(2,1)S(1)} %copy-done, bf16[1168,512]{1,0:T(8,128)(2,1)S(1)} %get-tuple-element.79.refs_0_.refs_3_, bf16[1168,512]{1,0:T(8,128)(2,1)S(1)} %get-tuple-element.80.refs_1_, bf16[1168,512]{1,0:T(8,128)(2,1)S(1)} %get-tuple-element.86.refs_0_.refs_2_, ...), custom_call_target="tpu_custom_call" | custom-call | flops 3221225472 | bytes 14680064 | tf_op jit(solution)/shard_map/last_product/pallas_call | solution.py:411
  227.1 1.4 copy-done.1
  228.9 1.1 collective-permute-start.15
  229.9 2.2 collective-permute-done.20.refs_1_.refs_3_
  232.5 0.8 collective-permute-start.21
  233.3 8.8 %collective-permute-done.15.got_ref = bf16[272,1024]{1,0:T(8,128)(2,1)S(1)} collective-permute-done((bf16[272,1024]{1,0:T(8,128)(2,1)S(1)}, bf16[272,1024]{1,0:T(8,128)(2,1)S(1)}, u32[]{:S(2)}, u32[]{:S(2)}) %collective-permute-start.15) | collective-permute-done | bytes 557088 | tf_op jit(solution)/shard_map/ppermute | solution.py:30
  242.3 2.6 collective-permute-start.16
  245.1 11.1 %collective-permute-done.22.got_ref = bf16[128,1024]{1,0:T(8,128)(2,1)S(1)} collective-permute-done((bf16[128,1024]{1,0:T(8,128)(2,1)S(1)}, bf16[128,1024]{1,0:T(8,128)(2,1)S(1)}, u32[]{:S(2)}, u32[]{:S(2)}) %collective-permute-start.22) | collective-permute-done | bytes 262176 | tf_op jit(solution)/shard_map/ppermute | solution.py:30
  256.2 0.8 collective-permute-start.23
  257.2 2.2 collective-permute-start.17
  259.4 5.1 %last_product.3 = bf16[384,2048]{1,0:T(8,128)(2,1)} custom-call(bf16[2048,2048]{1,0:T(8,128)(2,1)S(1)} %copy-done, bf16[384,512]{1,0:T(8,128)(2,1)S(1)} %collective-permute-done.13.refs_2_.refs_0_, bf16[384,512]{1,0:T(8,128)(2,1)S(1)} %collective-permute-done.14.refs_3_.refs_1_, bf16[384,512]{1,0:T(8,128)(2,1)S(1)} %collective-permute-done.19.refs_0_.refs_2_, ...), custom_call_target="tpu_custom_call" | custom-call | flops 3221225472 | bytes 14680064 | tf_op jit(solution)/shard_map/last_product/pallas_call | solution.py:411
  264.5 3.0 %collective-permute-done.23.got1 = bf16[64,1024]{1,0:T(8,128)(2,1)S(1)} collective-permute-done((bf16[64,1024]{1,0:T(8,128)(2,1)S(1)}, bf16[64,1024]{1,0:T(8,128)(2,1)S(1)}, u32[]{:S(2)}, u32[]{:S(2)}) %collective-permute-start.23) | collective-permute-done | bytes 131104 | tf_op jit(solution)/shard_map/ppermute | solution.py:30
  267.5 2.5 collective-permute-done.17.got0
  269.9 0.8 last_stage.1
  (61 shorter events, 4.2 us)
Async XLA Ops:
  7.2 123.5 %all-gather.2.cloned.1.call-start = ((), (), s32[]{:S(2)}) async-start(), calls=%async_computation.2 | async-start | bytes 10485760 | tf_op jit(solution)/shard_map/all_gather | solution.py:577
  9.1 13.7 %all-to-all-start = ((s32[8,1,16]{2,1,0:T(1,128)}), s32[8,1,16]{2,1,0:T(1,128)S(1)}, u32[]{:S(2)}, u32[]{:S(2)}) async-start(s32[8,1,16]{2,1,0:T(1,128)} %broadcast_in_dim.24), calls=%async_computation | async-start | bytes 8192 | tf_op jit(solution)/shard_map/all_to_all | solution.py:559
  22.8 2.8 copy-start.2
  25.6 0.7 copy-start.4
  30.1 2.0 copy-start.3
  32.2 5.0 %copy-start.7 = (bf16[384,2048]{1,0:T(8,128)(2,1)S(1)}, bf16[384,2048]{1,0:T(8,128)(2,1)}, u32[]{:S(2)}) copy-start(bf16[384,2048]{1,0:T(8,128)(2,1)} %param.7) | copy-start | bytes 4718596
  32.2 108.5 %all-to-all-start.1 = ((bf16[4,256,2048]{2,1,0:T(8,128)(2,1)}), bf16[4,256,2048]{2,1,0:T(8,128)(2,1)}, u32[]{:S(2)}, u32[]{:S(2)}) async-start(bf16[4,256,2048]{2,1,0:T(8,128)(2,1)} %bitcast.21), calls=%async_computation.1 | async-start | bytes 8388608 | tf_op jit(solution)/shard_map/all_to_all | solution.py:572
  40.5 4.4 %copy-start.9 = (s32[32]{0:T(128)S(1)}, s32[32]{0:T(128)}, u32[]{:S(2)}) copy-start(s32[32]{0:T(128)} %constant.56) | copy-start | bytes 388
  40.5 4.6 %copy-start.8 = (s32[32,1]{0,1:T(1,128)S(1)}, s32[32,1]{0,1:T(1,128)}, u32[]{:S(2)}) copy-start(s32[32,1]{0,1:T(1,128)} %constant.59) | copy-start | bytes 388
  40.5 76.8 %collective-permute-start = (bf16[384,2048]{0,1:T(8,128)(2,1)}, bf16[384,2048]{0,1:T(8,128)(2,1)}, u32[]{:S(2)}, u32[]{:S(2)}) collective-permute-start(bf16[384,2048]{0,1:T(8,128)(2,1)} %broadcast_select_fusion), channel_id=1, source_target_pairs={{0,16},{2,18},{4,20},{6,22},{8,24},{10,26},{12,28},{14,30},{16,0},... | collective-permute-start | bytes 4718600 | tf_op jit(solution)/shard_map/ppermute | solution.py:41
  45.2 105.3 %collective-permute-start.5 = (bf16[256,2048]{1,0:T(8,128)(2,1)}, bf16[256,2048]{1,0:T(8,128)(2,1)}, u32[]{:S(2)}, u32[]{:S(2)}) collective-permute-start(bf16[256,2048]{1,0:T(8,128)(2,1)} %get-tuple-element.61.refs_3_.refs_8_), channel_id=1, source_target_pairs={{1,17},{3,19},{5,21},{7,23},{9,25},{11,27},{13,29},{15,31},{17,1},... | collective-permute-start | bytes 3145736 | tf_op jit(solution)/shard_map/ppermute | solution.py:41
  46.8 111.4 %collective-permute-start.4 = (bf16[256,2048]{1,0:T(8,128)(2,1)}, bf16[256,2048]{1,0:T(8,128)(2,1)}, u32[]{:S(2)}, u32[]{:S(2)}) collective-permute-start(bf16[256,2048]{1,0:T(8,128)(2,1)} %get-tuple-element.60), channel_id=1, source_target_pairs={{0,4},{1,21},{2,6},{3,23},{4,0},{5,17},{6,2},{7,19},{8,12},{9,29},... | collective-permute-start | bytes 3145736 | tf_op jit(solution)/shard_map/ppermute | solution.py:41
  48.8 111.3 %collective-permute-start.3 = (bf16[256,2048]{1,0:T(8,128)(2,1)}, bf16[256,2048]{1,0:T(8,128)(2,1)}, u32[]{:S(2)}, u32[]{:S(2)}) collective-permute-start(bf16[256,2048]{1,0:T(8,128)(2,1)} %get-tuple-element.59), channel_id=1, source_target_pairs={{0,8},{1,25},{2,10},{3,27},{4,12},{5,29},{6,14},{7,31},{8,0},{9,17... | collective-permute-start | bytes 3145736 | tf_op jit(solution)/shard_map/ppermute | solution.py:41
  50.3 115.5 %collective-permute-start.2 = (bf16[256,2048]{1,0:T(8,128)(2,1)}, bf16[256,2048]{1,0:T(8,128)(2,1)}, u32[]{:S(2)}, u32[]{:S(2)}) collective-permute-start(bf16[256,2048]{1,0:T(8,128)(2,1)} %get-tuple-element.58), channel_id=1, source_target_pairs={{0,12},{1,29},{2,14},{3,31},{4,8},{5,25},{6,10},{7,27},{8,4},{9,21... | collective-permute-start | bytes 3145736 | tf_op jit(solution)/shard_map/ppermute | solution.py:41
  118.9 2.7 copy-start.5
  130.7 39.3 %collective-permute-start.1 = (bf16[1024,1152]{1,0:T(8,128)(2,1)}, bf16[1024,1152]{1,0:T(8,128)(2,1)}, u32[]{:S(2)}, u32[]{:S(2)}) collective-permute-start(bf16[1024,1152]{1,0:T(8,128)(2,1)} %bitcast.8), channel_id=1, source_target_pairs={{0,1},{1,0},{2,3},{3,2},{4,5},{5,4},{6,7},{7,6},{8,9},{9,8},{10,11... | collective-permute-start | bytes 7077896 | tf_op jit(solution)/shard_map/ppermute | solution.py:30
  140.7 6.2 %copy-start = (bf16[2048,2048]{1,0:T(8,128)(2,1)S(1)}, bf16[2048,2048]{1,0:T(8,128)(2,1)}, u32[]{:S(2)}) copy-start(bf16[2048,2048]{1,0:T(8,128)(2,1)} %all-gather.2.cloned.1.call-done.w_ref) | copy-start | bytes 25165828
  140.7 6.2 %copy-start.6 = (bf16[384,2048]{0,1:T(8,128)(2,1)S(1)}, bf16[384,2048]{0,1:T(8,128)(2,1)}, u32[]{:S(2)}) copy-start(bf16[384,2048]{0,1:T(8,128)(2,1)} %copy-done.5) | copy-start | bytes 4718596
  150.5 19.5 %collective-permute-start.7 = (f32[8,384]{1,0:T(8,128)S(1)}, f32[8,384]{1,0:T(8,128)S(1)}, u32[]{:S(2)}, u32[]{:S(2)}) collective-permute-start(f32[8,384]{1,0:T(8,128)S(1)} %get-tuple-element.57.mine_ref), channel_id=1, source_target_pairs={{0,16},{1,1},{2,18},{3,3},{4,20},{5,5},{6,22},{7,7},{8,24},{9,9},{... | collective-permute-start | bytes 36872 | tf_op jit(solution)/shard_map/ppermute | solution.py:41
  167.7 12.2 %collective-permute-start.6 = (f32[8,384]{1,0:T(8,128)S(1)}, f32[8,384]{1,0:T(8,128)S(1)}, u32[]{:S(2)}, u32[]{:S(2)}) collective-permute-start(f32[8,384]{1,0:T(8,128)S(1)} %get-tuple-element.66.mine_ref), channel_id=1, source_target_pairs={{0,16},{1,1},{2,18},{3,3},{4,20},{5,5},{6,22},{7,7},{8,24},{9,9},{... | collective-permute-start | bytes 36872 | tf_op jit(solution)/shard_map/ppermute | solution.py:41
  175.4 15.5 %collective-permute-start.13 = (bf16[384,512]{1,0:T(8,128)(2,1)S(1)}, bf16[384,512]{1,0:T(8,128)(2,1)S(1)}, u32[]{:S(2)}, u32[]{:S(2)}) collective-permute-start(bf16[384,512]{1,0:T(8,128)(2,1)S(1)} %get-tuple-element.76.refs_0_), channel_id=1, source_target_pairs={{0,16},{1,1},{2,18},{3,3},{4,20},{5,5},{6,22},{7,7},{8,24},{9,9},{... | collective-permute-start | bytes 1179656 | tf_op jit(solution)/shard_map/ppermute | solution.py:41
  185.0 4.8 %slice-start = ((s8[4718592]{0:T(1024)(128)(4,1)}), s8[4194304]{0:T(1024)(128)(4,1)S(1)}, s32[]{:S(2)}) async-start(s8[4718592]{0:T(1024)(128)(4,1)} %bitcast.24), calls=%async_computation.3 | async-start | bytes 8388608
  185.0 4.8 %slice-start.1 = ((s8[4718592]{0:T(1024)(128)(4,1)}), s8[524288]{0:T(1024)(128)(4,1)S(1)}, s32[]{:S(2)}) async-start(s8[4718592]{0:T(1024)(128)(4,1)} %bitcast.24), calls=%async_computation.4 | async-start | bytes 1048576
  188.7 17.0 %collective-permute-start.11 = (bf16[1168,512]{1,0:T(8,128)(2,1)S(1)}, bf16[1168,512]{1,0:T(8,128)(2,1)S(1)}, u32[]{:S(2)}, u32[]{:S(2)}) collective-permute-start(bf16[1168,512]{1,0:T(8,128)(2,1)S(1)} %get-tuple-element.86.refs_0_.refs_2_), channel_id=1, source_target_pairs={{0,1},{1,0},{2,3},{3,2},{4,5},{5,4},{6,7},{7,6},{8,9},{9,8},{10,11... | collective-permute-start | bytes 3588104 | tf_op jit(solution)/shard_map/ppermute | solution.py:30
  188.8 16.9 %collective-permute-start.12 = (bf16[1168,512]{1,0:T(8,128)(2,1)S(1)}, bf16[1168,512]{1,0:T(8,128)(2,1)S(1)}, u32[]{:S(2)}, u32[]{:S(2)}) collective-permute-start(bf16[1168,512]{1,0:T(8,128)(2,1)S(1)} %get-tuple-element.87.refs_1_.refs_3_), channel_id=1, source_target_pairs={{0,1},{1,0},{2,3},{3,2},{4,5},{5,4},{6,7},{7,6},{8,9},{9,8},{10,11... | collective-permute-start | bytes 3588104 | tf_op jit(solution)/shard_map/ppermute | solution.py:30
  189.3 11.8 %collective-permute-start.8 = (bf16[1168,512]{1,0:T(8,128)(2,1)S(1)}, bf16[1168,512]{1,0:T(8,128)(2,1)S(1)}, u32[]{:S(2)}, u32[]{:S(2)}) collective-permute-start(bf16[1168,512]{1,0:T(8,128)(2,1)S(1)} %get-tuple-element.79.refs_0_.refs_3_), channel_id=1, source_target_pairs={{0,1},{1,0},{2,3},{3,2},{4,5},{5,4},{6,7},{7,6},{8,9},{9,8},{10,11... | collective-permute-start | bytes 3588104 | tf_op jit(solution)/shard_map/ppermute | solution.py:30
  189.4 11.7 %collective-permute-start.9 = (bf16[1168,512]{1,0:T(8,128)(2,1)S(1)}, bf16[1168,512]{1,0:T(8,128)(2,1)S(1)}, u32[]{:S(2)}, u32[]{:S(2)}) collective-permute-start(bf16[1168,512]{1,0:T(8,128)(2,1)S(1)} %get-tuple-element.80.refs_1_), channel_id=1, source_target_pairs={{0,1},{1,0},{2,3},{3,2},{4,5},{5,4},{6,7},{7,6},{8,9},{9,8},{10,11... | collective-permute-start | bytes 3588104 | tf_op jit(solution)/shard_map/ppermute | solution.py:30
  190.9 14.8 %collective-permute-start.14 = (bf16[384,512]{1,0:T(8,128)(2,1)S(1)}, bf16[384,512]{1,0:T(8,128)(2,1)S(1)}, u32[]{:S(2)}, u32[]{:S(2)}) collective-permute-start(bf16[384,512]{1,0:T(8,128)(2,1)S(1)} %get-tuple-element.77.refs_1_), channel_id=1, source_target_pairs={{0,16},{1,1},{2,18},{3,3},{4,20},{5,5},{6,22},{7,7},{8,24},{9,9},{... | collective-permute-start | bytes 1179656 | tf_op jit(solution)/shard_map/ppermute | solution.py:41
  203.9 23.2 %collective-permute-start.10 = (bf16[528,1024]{1,0:T(8,128)(2,1)S(1)}, bf16[528,1024]{1,0:T(8,128)(2,1)S(1)}, u32[]{:S(2)}, u32[]{:S(2)}) collective-permute-start(bf16[528,1024]{1,0:T(8,128)(2,1)S(1)} %get-tuple-element.81), channel_id=1, source_target_pairs={{0,2},{1,3},{2,0},{3,1},{4,6},{5,7},{6,4},{7,5},{8,10},{9,11},{10,... | collective-permute-start | bytes 3244040 | tf_op jit(solution)/shard_map/ppermute | solution.py:30
  208.5 23.9 %collective-permute-start.18 = (bf16[512,1024]{1,0:T(8,128)(2,1)S(1)}, bf16[512,1024]{1,0:T(8,128)(2,1)S(1)}, u32[]{:S(2)}, u32[]{:S(2)}) collective-permute-start(bf16[512,1024]{1,0:T(8,128)(2,1)S(1)} %weight_part.10.refs_4_), channel_id=1, source_target_pairs={{0,4},{4,0},{8,12},{12,8},{16,20},{20,16},{24,28},{28,24},{1,5},{5... | collective-permute-start | bytes 3145736 | tf_op jit(solution)/shard_map/ppermute | solution.py:30
  209.1 20.8 %collective-permute-start.19 = (bf16[384,512]{1,0:T(8,128)(2,1)S(1)}, bf16[384,512]{1,0:T(8,128)(2,1)S(1)}, u32[]{:S(2)}, u32[]{:S(2)}) collective-permute-start(bf16[384,512]{1,0:T(8,128)(2,1)S(1)} %get-tuple-element.83.refs_0_), channel_id=1, source_target_pairs={{0,16},{1,1},{2,18},{3,3},{4,20},{5,5},{6,22},{7,7},{8,24},{9,9},{... | collective-permute-start | bytes 1179656 | tf_op jit(solution)/shard_map/ppermute | solution.py:41
  212.1 20.1 %collective-permute-start.20 = (bf16[384,512]{1,0:T(8,128)(2,1)S(1)}, bf16[384,512]{1,0:T(8,128)(2,1)S(1)}, u32[]{:S(2)}, u32[]{:S(2)}) collective-permute-start(bf16[384,512]{1,0:T(8,128)(2,1)S(1)} %get-tuple-element.84.refs_1_), channel_id=1, source_target_pairs={{0,16},{1,1},{2,18},{3,3},{4,20},{5,5},{6,22},{7,7},{8,24},{9,9},{... | collective-permute-start | bytes 1179656 | tf_op jit(solution)/shard_map/ppermute | solution.py:41
  227.1 1.4 copy-start.1
  228.9 13.3 %collective-permute-start.15 = (bf16[272,1024]{1,0:T(8,128)(2,1)S(1)}, bf16[272,1024]{1,0:T(8,128)(2,1)S(1)}, u32[]{:S(2)}, u32[]{:S(2)}) collective-permute-start(bf16[272,1024]{1,0:T(8,128)(2,1)S(1)} %get-tuple-element.89), channel_id=1, source_target_pairs={{0,4},{4,0},{8,12},{12,8},{16,20},{20,16},{24,28},{28,24},{1,5},{5... | collective-permute-start | bytes 1671176 | tf_op jit(solution)/shard_map/ppermute | solution.py:30
  232.5 12.4 %collective-permute-start.21 = (bf16[256,1024]{1,0:T(8,128)(2,1)S(1)}, bf16[256,1024]{1,0:T(8,128)(2,1)S(1)}, u32[]{:S(2)}, u32[]{:S(2)}) collective-permute-start(bf16[256,1024]{1,0:T(8,128)(2,1)S(1)} %get-tuple-element.97), channel_id=1, source_target_pairs={{0,2},{1,3},{2,0},{3,1},{4,6},{5,7},{6,4},{7,5},{8,10},{9,11},{10,... | collective-permute-start | bytes 1572872 | tf_op jit(solution)/shard_map/ppermute | solution.py:30
  242.3 14.8 %collective-permute-start.16 = (bf16[144,1024]{1,0:T(8,128)(2,1)S(1)}, bf16[144,1024]{1,0:T(8,128)(2,1)S(1)}, u32[]{:S(2)}, u32[]{:S(2)}) collective-permute-start(bf16[144,1024]{1,0:T(8,128)(2,1)S(1)} %get-tuple-element.92), channel_id=1, source_target_pairs={{0,8},{4,12},{8,0},{12,4},{16,24},{20,28},{24,16},{28,20},{1,9},{5... | collective-permute-start | bytes 884744 | tf_op jit(solution)/shard_map/ppermute | solution.py:30
  245.0 11.2 %collective-permute-start.22 = (bf16[128,1024]{1,0:T(8,128)(2,1)S(1)}, bf16[128,1024]{1,0:T(8,128)(2,1)S(1)}, u32[]{:S(2)}, u32[]{:S(2)}) collective-permute-start(bf16[128,1024]{1,0:T(8,128)(2,1)S(1)} %get-tuple-element.99), channel_id=1, source_target_pairs={{0,8},{4,12},{8,0},{12,4},{16,24},{20,28},{24,16},{28,20},{1,9},{5... | collective-permute-start | bytes 786440 | tf_op jit(solution)/shard_map/ppermute | solution.py:30
  256.2 11.2 %collective-permute-start.23 = (bf16[64,1024]{1,0:T(8,128)(2,1)S(1)}, bf16[64,1024]{1,0:T(8,128)(2,1)S(1)}, u32[]{:S(2)}, u32[]{:S(2)}) collective-permute-start(bf16[64,1024]{1,0:T(8,128)(2,1)S(1)} %get-tuple-element.101.refs_6_), channel_id=1, source_target_pairs={{0,16},{4,20},{8,24},{12,28},{16,0},{20,4},{24,8},{28,12},{1,17},{... | collective-permute-start | bytes 393224 | tf_op jit(solution)/shard_map/ppermute | solution.py:30
  257.2 12.8 %collective-permute-start.17 = (bf16[80,1024]{1,0:T(8,128)(2,1)S(1)}, bf16[80,1024]{1,0:T(8,128)(2,1)S(1)}, u32[]{:S(2)}, u32[]{:S(2)}) collective-permute-start(bf16[80,1024]{1,0:T(8,128)(2,1)S(1)} %get-tuple-element.95.refs_5_), channel_id=1, source_target_pairs={{0,16},{4,20},{8,24},{12,28},{16,0},{20,4},{24,8},{28,12},{1,17},{... | collective-permute-start | bytes 491528 | tf_op jit(solution)/shard_map/ppermute | solution.py:30
Sparse Core Ops, SparseCore 0:
  9.6 60.9 all-gather.1

commit v5 on v2

--- a/solution.py
+++ b/solution.py
@@ -19,7 +19,7 @@
 F32 = jnp.float32
 BF16 = jnp.bfloat16
 
-VMEM_LIMIT = 24 * 1024 * 1024
+VMEM_LIMIT = 20 * 1024 * 1024
 
 
 def bits_of(size):

time: 279 us -> 279 us (level)
  no operation moved by 1% of the time
where the time goes in v5:
time: 279 us; the launch traced here: 277 us
  waiting for transfers between devices  92.4 us (33%)
  starting transfers between devices  60.1 us (22%)
  Pallas kernels  55.4 us (20%)
  local copies, waits for them, and re-layouts  20.5 us (7%)
  matrix products  20.4 us (7%)
  between operations  17.6 us (6%)
  other arithmetic  10.8 us (4%)
    ppermute x11, waiting for transfers between devices, move(): return lax.ppermute(x, ('dp', 'fsdp'), pairs)  59.6 us
    ppermute x11, starting transfers between devices, move(): return lax.ppermute(x, ('dp', 'fsdp'), pairs)  36.2 us
    ppermute x13, waiting for transfers between devices, swap(): lax.ppermute(x, axis, [(i, i ^ bit) for i in range(lax.axis_size(axis))])  25.7 us
    pallas_call x6, Pallas kernels, weight_part(): pl.pallas_call(kernel, grid=(m,), in_specs=in_specs, out_specs=out_specs,...  13.7 us
    unnamed x40, local copies, waits for them, and re-layouts  12.6 us
    pallas_call x5, Pallas kernels, part_scores(): pl.pallas_call(kernel, grid=(sets,), in_specs=in_specs, out_specs=out_spe...  12.1 us
    ppermute x13, starting transfers between devices, swap(): lax.ppermute(x, axis, [(i, i ^ bit) for i in range(lax.axis_size(axis))])  11.7 us
    pallas_call x2, Pallas kernels, last_product(): pl.pallas_call(kernel, grid=(kin // tile,), in_specs=in_specs + [ANY] * l...  10.1 us
  transfers between devices with their start and end apart: 27, of which 10 were waited for; matrix products, arithmetic and copies ran while one was open for 15% of the time, Pallas kernels for 20%

profile of v5, /device:TPU:0, one launch (start us, length us, event | category | flops | bytes accessed | tf_op | source)
XLA Modules:
  0.0 277.3 jit_solution(7110962464093319148)
XLA Ops:
  7.2 0.7 all-gather.2.cloned.1.call-update
  8.5 7.3 %all-to-all-start = ((s32[8,1,16]{2,1,0:T(1,128)}), s32[8,1,16]{2,1,0:T(1,128)S(1)}, u32[]{:S(2)}, u32[]{:S(2)}) async-start(s32[8,1,16]{2,1,0:T(1,128)} %broadcast_in_dim.24), calls=%async_computation | async-start | bytes 8192 | tf_op jit(solution)/shard_map/all_to_all | solution.py:539
  15.8 6.4 %all-to-all-done = s32[8,1,16]{2,1,0:T(1,128)S(1)} async-done(((s32[8,1,16]{2,1,0:T(1,128)}), s32[8,1,16]{2,1,0:T(1,128)S(1)}, u32[]{:S(2)}, u32[]{:S(2)}) %all-to-all-start) | async-done | bytes 544 | tf_op jit(solution)/shard_map/all_to_all | solution.py:539
  22.2 3.3 %copy-done.6 = bf16[8,128,2048]{2,1,0:T(8,128)(2,1)S(1)} copy-done((bf16[8,128,2048]{2,1,0:T(8,128)(2,1)S(1)}, bf16[8,128,2048]{2,1,0:T(8,128)(2,1)}, u32[]{:S(2)}) %copy-start.6) | copy-done | bytes 4194328
  25.5 3.7 %pick_blocks.1 = (bf16[1024,2048]{1,0:T(8,128)(2,1)S(1)}, bf16[256,2048]{1,0:T(8,128)(2,1)}, bf16[256,2048]{1,0:T(8,128)(2,1)}, bf16[256,2048]{1,0:T(8,128)(2,1)...) custom-call(s32[8,16]{1,0:T(8,128)S(1)} %bitcast.27, s32[256]{0:T(256)S(1)} %copy-done.8, s32[1]{0:T(128)} %bitcast.2.me_ref, ...), custom_call_target="tpu_custom_call" | custom-call | bytes 16777216 | tf_op jit(solution)/shard_map/pick_blocks/pallas_call | solution.py:96
  29.3 2.0 copy-done.7
  31.3 5.0 %all-to-all-start.1 = ((bf16[4,256,2048]{2,1,0:T(8,128)(2,1)}), bf16[4,256,2048]{2,1,0:T(8,128)(2,1)}, u32[]{:S(2)}, u32[]{:S(2)}) async-start(bf16[4,256,2048]{2,1,0:T(8,128)(2,1)} %bitcast.26), calls=%async_computation.1 | async-start | bytes 8388608 | tf_op jit(solution)/shard_map/all_to_all | solution.py:549
  36.3 0.9 copy.17
  38.4 1.3 broadcast_select_fusion
  39.7 2.1 collective-permute-start
  41.9 1.6 copy.15
  43.6 9.4 %collective-permute-start.5 = (bf16[256,2048]{1,0:T(8,128)(2,1)}, bf16[256,2048]{1,0:T(8,128)(2,1)}, u32[]{:S(2)}, u32[]{:S(2)}) collective-permute-start(bf16[256,2048]{1,0:T(8,128)(2,1)} %get-tuple-element.61), channel_id=1, source_target_pairs={{0,0},{1,17},{2,2},{3,19},{4,4},{5,21},{6,6},{7,23},{8,8},{9,25},{... | collective-permute-start | bytes 3145736 | tf_op jit(solution)/shard_map/ppermute | solution.py:38
  53.1 2.0 collective-permute-start.4
  55.1 1.4 collective-permute-start.3
  57.7 1.6 broadcast_select_fusion.1
  59.3 57.1 %collective-permute-done = bf16[384,2048]{0,1:T(8,128)(2,1)} collective-permute-done((bf16[384,2048]{0,1:T(8,128)(2,1)}, bf16[384,2048]{0,1:T(8,128)(2,1)}, u32[]{:S(2)}, u32[]{:S(2)}) %collective-permute-start) | collective-permute-done | bytes 1572896 | tf_op jit(solution)/shard_map/ppermute | solution.py:38
  116.4 3.5 %pad_maximum_fusion = bf16[1152,2048]{0,1:T(8,128)(2,1)} fusion(bf16[384,2048]{0,1:T(8,128)(2,1)} %collective-permute-done, bf16[384,2048]{0,1:T(8,128)(2,1)S(1)} %broadcast_select_fusion.1, bf16[384,2048]{0,1:T(8,128)(2,1)S(1)} %copy.17), kind=kLoop, calls=%fused_computation.1 | loop fusion | flops 14155776 | bytes 9437184 | tf_op jit(solution)/shard_map/concatenate | solution.py:570
  119.9 5.6 %gather_fusion = bf16[32,64,1152]{2,1,0:T(8,128)(2,1)} fusion(bf16[32,64,1152]{2,1,0:T(8,128)(2,1)} %bitcast.31, s32[1024]{0:T(1024)S(1)} %pad_clamp_fusion), kind=kCustom, calls=%fused_computation | custom fusion | bytes 9437312 | tf_op jit(solution)/shard_map/jit(_take)/gather | solution.py:573
  125.5 3.4 %slice_select_fusion = bf16[16,64,1152]{2,1,0:T(8,128)(2,1)} fusion(bf16[32,64,1152]{2,1,0:T(8,128)(2,1)} %gather_fusion, pred[16]{0:T(512)(128)(4,1)S(1)} %bitcast.32), kind=kLoop, calls=%fused_computation.6 | loop fusion | flops 1179648 | bytes 4718608 | tf_op jit(solution)/shard_map/jit(_take)/select_n | solution.py:573
  128.9 8.6 %convolution_convert_fusion.1.refs_2_.p_ref = bf16[384,2048]{1,0:T(8,128)(2,1)} fusion(bf16[384,2048]{1,0:T(8,128)(2,1)} %param.8, bf16[2048,2048]{1,0:T(8,128)(2,1)} %all-gather.2.cloned.1.call-done.w_ref), kind=kOutput, calls=%fused_computation.4 | convolution fusion | flops 3222011904 | bytes 11534336 | tf_op jit(solution)/shard_map/dot_general | solution.py:556
  137.5 4.5 %convolution_convert_fusion.2.refs_0_.q_ref = bf16[384,2048]{1,0:T(8,128)(2,1)} fusion(bf16[384,2048]{1,0:T(8,128)(2,1)S(1)} %copy-done.11, bf16[2048,2048]{1,0:T(8,128)(2,1)S(1)} %copy-done), kind=kOutput, calls=%fused_computation.5 | convolution fusion | flops 3222011904 | bytes 11534336 | tf_op jit(solution)/shard_map/dot_general | solution.py:555
  142.0 1.4 copy-done.1
  143.4 1.4 copy-done.3
  144.8 5.8 %part_scores.5 = (f32[384,1024]{1,0:T(8,128)S(1)}, f32[8,384]{1,0:T(8,128)S(1)}, f32[384,384]{1,0:T(8,128)S(1)}) custom-call(bf16[384,2048]{1,0:T(8,128)(2,1)S(1)} %copy-done.3, bf16[1024,2048]{1,0:T(8,128)(2,1)} %bitcast.11.refs_1_.x_ref, bf16[384,2048]{1,0:T(8,128)(2,1)S(1)} %copy-done.1), custom_call_target="tpu_custom_call" | custom-call | flops 1610612736 | bytes 5767168 | tf_op jit(solution)/shard_map/part_scores/pallas_call | solution.py:192
  150.6 7.3 %convolution_convert_fusion.refs_0_ = bf16[384,2048]{1,0:T(8,128)(2,1)S(1)} fusion(bf16[384,2048]{0,1:T(8,128)(2,1)} %collective-permute-done, bf16[2048,2048]{1,0:T(8,128)(2,1)} %all-gather.2.cloned.1.call-done.w_ref), kind=kOutput, calls=%fused_computation.3 | convolution fusion | flops 3222011904 | bytes 11534336 | tf_op jit(solution)/shard_map/dot_general | solution.py:557
  157.9 5.3 %collective-permute-start.7 = (f32[8,384]{1,0:T(8,128)S(1)}, f32[8,384]{1,0:T(8,128)S(1)}, u32[]{:S(2)}, u32[]{:S(2)}) collective-permute-start(f32[8,384]{1,0:T(8,128)S(1)} %get-tuple-element.57.mine_ref), channel_id=1, source_target_pairs={{0,16},{1,1},{2,18},{3,3},{4,20},{5,5},{6,22},{7,7},{8,24},{9,9},{... | collective-permute-start | bytes 36872 | tf_op jit(solution)/shard_map/ppermute | solution.py:38
  163.3 1.9 part_scores.6
  165.2 0.6 part_scores.7
  165.8 1.9 part_scores.8
  167.7 2.0 part_scores.9
  169.7 2.1 collective-permute-start.6
  171.9 5.1 %guest_rows.1 = (f32[384,2048]{1,0:T(8,128)S(1)}, bf16[384,512]{1,0:T(8,128)(2,1)S(1)}, bf16[384,512]{1,0:T(8,128)(2,1)S(1)}, bf16[384,512]{1,0:T(8,128)(2,1)S(1)}, bf16[384,512]{1,0:T(8,128)(2,1)S(1)}) custom-call(s32[1]{0:T(128)} %bitcast.9.stays_ref, f32[8,384]{1,0:T(8,128)S(1)} %get-tuple-element.66.mine_ref, ...), custom_call_target="tpu_custom_call" | custom-call | flops 1610612736 | bytes 8912896 | tf_op jit(solution)/shard_map/guest_rows/pallas_call | solution.py:263
  177.0 5.0 %collective-permute-start.13 = (bf16[384,512]{1,0:T(8,128)(2,1)S(1)}, bf16[384,512]{1,0:T(8,128)(2,1)S(1)}, u32[]{:S(2)}, u32[]{:S(2)}) collective-permute-start(bf16[384,512]{1,0:T(8,128)(2,1)S(1)} %get-tuple-element.76.refs_0_), channel_id=1, source_target_pairs={{0,16},{1,1},{2,18},{3,3},{4,20},{5,5},{6,22},{7,7},{8,24},{9,9},{... | collective-permute-start | bytes 1179656 | tf_op jit(solution)/shard_map/ppermute | solution.py:38
  182.0 1.5 own_grads.1
  183.5 3.6 %grad_rows.2 = (bf16[1168,512]{1,0:T(8,128)(2,1)S(1)}, bf16[1168,512]{1,0:T(8,128)(2,1)S(1)}, f32[384,2048]{1,0:T(8,128)S(1)}) custom-call(s32[1]{0:T(128)} %bitcast.9.stays_ref, bf16[384,1024]{1,0:T(8,128)(2,1)S(1)} %get-tuple-element.68.own_ref, bf16[384,384]{1,0:T(8,128)(2,1)S(1)} %get-tuple-element.69.near_ref, ...), custom_call_target="tpu_custom_call" | custom-call | flops 1409286144 | bytes 9961472 | tf_op jit(solution)/shard_map/grad_rows/pallas_call | solution.py:343
  187.1 3.7 %grad_rows.3 = (bf16[1168,512]{1,0:T(8,128)(2,1)S(1)}, bf16[1168,512]{1,0:T(8,128)(2,1)S(1)}, f32[384,2048]{1,0:T(8,128)S(1)}) custom-call(s32[1]{0:T(128)} %bitcast.9.stays_ref, bf16[384,1024]{1,0:T(8,128)(2,1)S(1)} %get-tuple-element.68.own_ref, bf16[384,384]{1,0:T(8,128)(2,1)S(1)} %get-tuple-element.69.near_ref, ...), custom_call_target="tpu_custom_call", output_to_operand_aliasing={{2}: (11, {})} | custom-call | flops 1409286144 | bytes 9961472 | tf_op jit(solution)/shard_map/grad_rows/pallas_call | solution.py:343
  191.9 1.1 bitcast_select_fusion.left_ref
  193.0 1.9 collective-permute-start.14
  194.9 3.4 %weight_part.6.refs_2_ = f32[1024,1024]{1,0:T(8,128)S(1)} custom-call(bf16[2048,1152]{1,0:T(8,128)(2,1)S(1)} %bitcast_select_fusion.left_ref, bf16[1168,512]{1,0:T(8,128)(2,1)S(1)} %get-tuple-element.79.refs_0_.refs_3_, bf16[1168,512]{1,0:T(8,128)(2,1)S(1)} %get-tuple-element.80.refs_1_), custom_call_target="tpu_custom_call" | custom-call | flops 2415919104 | bytes 13107200 | tf_op jit(solution)/shard_map/weight_part/pallas_call | solution.py:451
  198.3 3.4 %weight_part.9.refs_2_ = f32[1024,1024]{1,0:T(8,128)S(1)} custom-call(bf16[2048,1152]{1,0:T(8,128)(2,1)S(1)} %bitcast_select_fusion.left_ref, bf16[1168,512]{1,0:T(8,128)(2,1)S(1)} %get-tuple-element.86.refs_0_.refs_2_, bf16[1168,512]{1,0:T(8,128)(2,1)S(1)} %get-tuple-element.87.refs_1_.refs_3_, bf16[384,512]{1,0:T(8,128)(2,1)S(1)} %collective-permute-done.13.refs_2_.refs_0_), custom_call_target="tpu_custom_call" | custom-call | flops 2415919104 | bytes 13107200 | tf_op jit(solution)/shard_map/weight_part/pallas_call | solution.py:451
  201.8 1.7 weight_part.8
  203.5 1.3 collective-permute-start.10
  204.8 1.6 collective-permute-done.14.refs_3_.refs_1_
  206.4 1.7 weight_part.10.refs_4_
  208.2 1.5 collective-permute-start.18
  209.7 3.8 %collective-permute-start.19 = (bf16[384,512]{1,0:T(8,128)(2,1)S(1)}, bf16[384,512]{1,0:T(8,128)(2,1)S(1)}, u32[]{:S(2)}, u32[]{:S(2)}) collective-permute-start(bf16[384,512]{1,0:T(8,128)(2,1)S(1)} %get-tuple-element.83.refs_0_), channel_id=1, source_target_pairs={{0,16},{1,1},{2,18},{3,3},{4,20},{5,5},{6,22},{7,7},{8,24},{9,9},{... | collective-permute-start | bytes 1179656 | tf_op jit(solution)/shard_map/ppermute | solution.py:38
  213.5 2.9 %collective-permute-start.20 = (bf16[384,512]{1,0:T(8,128)(2,1)S(1)}, bf16[384,512]{1,0:T(8,128)(2,1)S(1)}, u32[]{:S(2)}, u32[]{:S(2)}) collective-permute-start(bf16[384,512]{1,0:T(8,128)(2,1)S(1)} %get-tuple-element.84.refs_1_), channel_id=1, source_target_pairs={{0,16},{1,1},{2,18},{3,3},{4,20},{5,5},{6,22},{7,7},{8,24},{9,9},{... | collective-permute-start | bytes 1179656 | tf_op jit(solution)/shard_map/ppermute | solution.py:38
  216.4 1.7 weight_part.11.refs_2_.keep_ref
  218.2 1.7 weight_part.7.keep_ref
  220.5 4.9 %last_product.2.refs_1_ = bf16[384,2048]{1,0:T(8,128)(2,1)} custom-call(bf16[2048,2048]{1,0:T(8,128)(2,1)S(1)} %bitcast.25, bf16[1168,512]{1,0:T(8,128)(2,1)S(1)} %get-tuple-element.79.refs_0_.refs_3_, bf16[1168,512]{1,0:T(8,128)(2,1)S(1)} %get-tuple-element.80.refs_1_, bf16[1168,512]{1,0:T(8,128)(2,1)S(1)} %get-tuple-element.86.refs_0_.refs_2_, ...), custom_call_target="tpu_custom_call" | custom-call | flops 3221225472 | bytes 14680064 | tf_op jit(solution)/shard_map/last_product/pallas_call | solution.py:391
  225.4 2.7 collective-permute-done.10.got_ref
  228.2 1.4 copy-done.5
  229.9 2.1 collective-permute-start.15
  232.0 0.9 collective-permute-done.20.refs_1_.refs_3_
  233.1 1.2 collective-permute-start.21
  234.3 8.4 %collective-permute-done.15.got_ref = bf16[272,1024]{1,0:T(8,128)(2,1)S(1)} collective-permute-done((bf16[272,1024]{1,0:T(8,128)(2,1)S(1)}, bf16[272,1024]{1,0:T(8,128)(2,1)S(1)}, u32[]{:S(2)}, u32[]{:S(2)}) %collective-permute-start.15) | collective-permute-done | bytes 557088 | tf_op jit(solution)/shard_map/ppermute | solution.py:30
  242.9 0.8 collective-permute-done.21.got_ref
  243.8 1.3 collective-permute-start.22
  245.1 9.6 %collective-permute-done.22.got_ref = bf16[128,1024]{1,0:T(8,128)(2,1)S(1)} collective-permute-done((bf16[128,1024]{1,0:T(8,128)(2,1)S(1)}, bf16[128,1024]{1,0:T(8,128)(2,1)S(1)}, u32[]{:S(2)}, u32[]{:S(2)}) %collective-permute-start.22) | collective-permute-done | bytes 262176 | tf_op jit(solution)/shard_map/ppermute | solution.py:30
  254.9 3.0 %collective-permute-start.17 = (bf16[80,1024]{1,0:T(8,128)(2,1)S(1)}, bf16[80,1024]{1,0:T(8,128)(2,1)S(1)}, u32[]{:S(2)}, u32[]{:S(2)}) collective-permute-start(bf16[80,1024]{1,0:T(8,128)(2,1)S(1)} %get-tuple-element.95.refs_5_), channel_id=1, source_target_pairs={{0,16},{4,20},{8,24},{12,28},{16,0},{20,4},{24,8},{28,12},{1,17},{... | collective-permute-start | bytes 491528 | tf_op jit(solution)/shard_map/ppermute | solution.py:30
  257.9 5.2 %last_product.3 = bf16[384,2048]{1,0:T(8,128)(2,1)} custom-call(bf16[2048,2048]{1,0:T(8,128)(2,1)S(1)} %bitcast.25, bf16[384,512]{1,0:T(8,128)(2,1)S(1)} %collective-permute-done.13.refs_2_.refs_0_, bf16[384,512]{1,0:T(8,128)(2,1)S(1)} %collective-permute-done.14.refs_3_.refs_1_, bf16[384,512]{1,0:T(8,128)(2,1)S(1)} %collective-permute-done.19.refs_0_.refs_2_, ...), custom_call_target="tpu_custom_call" | custom-call | flops 3221225472 | bytes 14680064 | tf_op jit(solution)/shard_map/last_product/pallas_call | solution.py:391
  263.1 2.2 collective-permute-done.23.got1
  265.3 1.9 collective-permute-done.17.got0
  267.3 0.8 last_stage.1
  (76 shorter events, 5.1 us)
Async XLA Ops:
  7.2 0.8 copy-start.12
  7.2 15.0 %copy-start.8 = (s32[256]{0:T(256)S(1)}, s32[256]{0:T(256)}, u32[]{:S(2)}) copy-start(s32[256]{0:T(256)} %home_ref.1) | copy-start | bytes 3076
  7.2 121.7 %all-gather.2.cloned.1.call-start = ((), (), s32[]{:S(2)}) async-start(), calls=%async_computation.2 | async-start | bytes 10485760 | tf_op jit(solution)/shard_map/all_gather | solution.py:554
  8.5 13.7 %all-to-all-start = ((s32[8,1,16]{2,1,0:T(1,128)}), s32[8,1,16]{2,1,0:T(1,128)S(1)}, u32[]{:S(2)}, u32[]{:S(2)}) async-start(s32[8,1,16]{2,1,0:T(1,128)} %broadcast_in_dim.24), calls=%async_computation | async-start | bytes 8192 | tf_op jit(solution)/shard_map/all_to_all | solution.py:539
  22.2 3.3 %copy-start.6 = (bf16[8,128,2048]{2,1,0:T(8,128)(2,1)S(1)}, bf16[8,128,2048]{2,1,0:T(8,128)(2,1)}, u32[]{:S(2)}) copy-start(bf16[8,128,2048]{2,1,0:T(8,128)(2,1)} %bank_ref.1) | copy-start | bytes 12582916
  29.3 2.0 copy-start.7
  31.3 5.0 %copy-start.10 = (bf16[384,2048]{1,0:T(8,128)(2,1)S(1)}, bf16[384,2048]{1,0:T(8,128)(2,1)}, u32[]{:S(2)}) copy-start(bf16[384,2048]{1,0:T(8,128)(2,1)} %param.7) | copy-start | bytes 4718596
  31.3 110.7 %all-to-all-start.1 = ((bf16[4,256,2048]{2,1,0:T(8,128)(2,1)}), bf16[4,256,2048]{2,1,0:T(8,128)(2,1)}, u32[]{:S(2)}, u32[]{:S(2)}) async-start(bf16[4,256,2048]{2,1,0:T(8,128)(2,1)} %bitcast.26), calls=%async_computation.1 | async-start | bytes 8388608 | tf_op jit(solution)/shard_map/all_to_all | solution.py:549
  37.2 4.6 %copy-start.9 = (bf16[384,2048]{1,0:T(8,128)(2,1)S(1)}, bf16[384,2048]{1,0:T(8,128)(2,1)}, u32[]{:S(2)}) copy-start(bf16[384,2048]{1,0:T(8,128)(2,1)} %param.8) | copy-start | bytes 4718596
  39.7 3.7 %copy-start.14 = (s32[32]{0:T(128)S(1)}, s32[32]{0:T(128)}, u32[]{:S(2)}) copy-start(s32[32]{0:T(128)} %constant.56) | copy-start | bytes 388
  39.7 3.9 %copy-start.13 = (s32[32,1]{0,1:T(1,128)S(1)}, s32[32,1]{0,1:T(1,128)}, u32[]{:S(2)}) copy-start(s32[32,1]{0,1:T(1,128)} %constant.59) | copy-start | bytes 388
  39.7 76.8 %collective-permute-start = (bf16[384,2048]{0,1:T(8,128)(2,1)}, bf16[384,2048]{0,1:T(8,128)(2,1)}, u32[]{:S(2)}, u32[]{:S(2)}) collective-permute-start(bf16[384,2048]{0,1:T(8,128)(2,1)} %broadcast_select_fusion), channel_id=1, source_target_pairs={{0,16},{1,1},{2,18},{3,3},{4,20},{5,5},{6,22},{7,7},{8,24},{9,9},{... | collective-permute-start | bytes 4718600 | tf_op jit(solution)/shard_map/ppermute | solution.py:38
  43.6 114.3 %collective-permute-start.5 = (bf16[256,2048]{1,0:T(8,128)(2,1)}, bf16[256,2048]{1,0:T(8,128)(2,1)}, u32[]{:S(2)}, u32[]{:S(2)}) collective-permute-start(bf16[256,2048]{1,0:T(8,128)(2,1)} %get-tuple-element.61), channel_id=1, source_target_pairs={{0,0},{1,17},{2,2},{3,19},{4,4},{5,21},{6,6},{7,23},{8,8},{9,25},{... | collective-permute-start | bytes 3145736 | tf_op jit(solution)/shard_map/ppermute | solution.py:38
  53.1 112.1 %collective-permute-start.4 = (bf16[256,2048]{1,0:T(8,128)(2,1)}, bf16[256,2048]{1,0:T(8,128)(2,1)S(1)}, u32[]{:S(2)}, u32[]{:S(2)}) collective-permute-start(bf16[256,2048]{1,0:T(8,128)(2,1)} %get-tuple-element.60), channel_id=1, source_target_pairs={{0,4},{1,21},{2,6},{3,23},{4,0},{5,17},{6,2},{7,19},{8,12},{9,29},... | collective-permute-start | bytes 3145736 | tf_op jit(solution)/shard_map/ppermute | solution.py:38
  55.1 110.8 %collective-permute-start.3 = (bf16[256,2048]{1,0:T(8,128)(2,1)}, bf16[256,2048]{1,0:T(8,128)(2,1)}, u32[]{:S(2)}, u32[]{:S(2)}) collective-permute-start(bf16[256,2048]{1,0:T(8,128)(2,1)} %get-tuple-element.59), channel_id=1, source_target_pairs={{0,8},{1,25},{2,10},{3,27},{4,12},{5,29},{6,14},{7,31},{8,0},{9,17... | collective-permute-start | bytes 3145736 | tf_op jit(solution)/shard_map/ppermute | solution.py:38
  56.5 111.2 %collective-permute-start.2 = (bf16[256,2048]{1,0:T(8,128)(2,1)}, bf16[256,2048]{1,0:T(8,128)(2,1)}, u32[]{:S(2)}, u32[]{:S(2)}) collective-permute-start(bf16[256,2048]{1,0:T(8,128)(2,1)} %get-tuple-element.58), channel_id=1, source_target_pairs={{0,12},{1,29},{2,14},{3,31},{4,8},{5,25},{6,10},{7,27},{8,4},{9,21... | collective-permute-start | bytes 3145736 | tf_op jit(solution)/shard_map/ppermute | solution.py:38
  128.9 42.9 %collective-permute-start.1 = (bf16[1024,1152]{1,0:T(8,128)(2,1)}, bf16[1024,1152]{1,0:T(8,128)(2,1)S(1)}, u32[]{:S(2)}, u32[]{:S(2)}) collective-permute-start(bf16[1024,1152]{1,0:T(8,128)(2,1)} %bitcast.8), channel_id=1, source_target_pairs={{0,1},{1,0},{2,3},{3,2},{4,5},{5,4},{6,7},{7,6},{8,9},{9,8},{10,11... | collective-permute-start | bytes 7077896 | tf_op jit(solution)/shard_map/ppermute | solution.py:30
  128.9 8.6 %copy-start = (bf16[2048,2048]{1,0:T(8,128)(2,1)S(1)}, bf16[2048,2048]{1,0:T(8,128)(2,1)}, u32[]{:S(2)}) copy-start(bf16[2048,2048]{1,0:T(8,128)(2,1)} %all-gather.2.cloned.1.call-done.w_ref) | copy-start | bytes 25165828
  128.9 8.6 %copy-start.11 = (bf16[384,2048]{1,0:T(8,128)(2,1)S(1)}, bf16[384,2048]{1,0:T(8,128)(2,1)}, u32[]{:S(2)}) copy-start(bf16[384,2048]{1,0:T(8,128)(2,1)} %param.7) | copy-start | bytes 4718596
  142.0 1.4 copy-start.1
  143.4 1.4 copy-start.3
  157.9 13.9 %collective-permute-start.7 = (f32[8,384]{1,0:T(8,128)S(1)}, f32[8,384]{1,0:T(8,128)S(1)}, u32[]{:S(2)}, u32[]{:S(2)}) collective-permute-start(f32[8,384]{1,0:T(8,128)S(1)} %get-tuple-element.57.mine_ref), channel_id=1, source_target_pairs={{0,16},{1,1},{2,18},{3,3},{4,20},{5,5},{6,22},{7,7},{8,24},{9,9},{... | collective-permute-start | bytes 36872 | tf_op jit(solution)/shard_map/ppermute | solution.py:38
  169.7 12.3 %collective-permute-start.6 = (f32[8,384]{1,0:T(8,128)S(1)}, f32[8,384]{1,0:T(8,128)S(1)}, u32[]{:S(2)}, u32[]{:S(2)}) collective-permute-start(f32[8,384]{1,0:T(8,128)S(1)} %get-tuple-element.66.mine_ref), channel_id=1, source_target_pairs={{0,16},{1,1},{2,18},{3,3},{4,20},{5,5},{6,22},{7,7},{8,24},{9,9},{... | collective-permute-start | bytes 36872 | tf_op jit(solution)/shard_map/ppermute | solution.py:38
  171.9 11.7 %copy-start.4 = (bf16[384,2048]{1,0:T(8,128)(2,1)S(1)}, bf16[384,2048]{1,0:T(8,128)(2,1)}, u32[]{:S(2)}) copy-start(bf16[384,2048]{1,0:T(8,128)(2,1)} %convolution_convert_fusion.2.refs_0_.q_ref) | copy-start | bytes 4718596
  177.0 6.5 %copy-start.2 = (bf16[384,2048]{1,0:T(8,128)(2,1)S(1)}, bf16[384,2048]{1,0:T(8,128)(2,1)}, u32[]{:S(2)}) copy-start(bf16[384,2048]{1,0:T(8,128)(2,1)} %convolution_convert_fusion.1.refs_2_.p_ref) | copy-start | bytes 4718596
  177.0 16.0 %collective-permute-start.13 = (bf16[384,512]{1,0:T(8,128)(2,1)S(1)}, bf16[384,512]{1,0:T(8,128)(2,1)S(1)}, u32[]{:S(2)}, u32[]{:S(2)}) collective-permute-start(bf16[384,512]{1,0:T(8,128)(2,1)S(1)} %get-tuple-element.76.refs_0_), channel_id=1, source_target_pairs={{0,16},{1,1},{2,18},{3,3},{4,20},{5,5},{6,22},{7,7},{8,24},{9,9},{... | collective-permute-start | bytes 1179656 | tf_op jit(solution)/shard_map/ppermute | solution.py:38
  187.1 4.8 %slice-start.2 = ((s8[4718592]{0:T(1024)(128)(4,1)}), s8[4194304]{0:T(1024)(128)(4,1)S(1)}, s32[]{:S(2)}) async-start(s8[4718592]{0:T(1024)(128)(4,1)} %bitcast.29), calls=%async_computation.5 | async-start | bytes 8388608
  187.1 4.8 %slice-start.3 = ((s8[4718592]{0:T(1024)(128)(4,1)}), s8[524288]{0:T(1024)(128)(4,1)S(1)}, s32[]{:S(2)}) async-start(s8[4718592]{0:T(1024)(128)(4,1)} %bitcast.29), calls=%async_computation.6 | async-start | bytes 1048576
  190.8 15.6 %collective-permute-start.11 = (bf16[1168,512]{1,0:T(8,128)(2,1)S(1)}, bf16[1168,512]{1,0:T(8,128)(2,1)S(1)}, u32[]{:S(2)}, u32[]{:S(2)}) collective-permute-start(bf16[1168,512]{1,0:T(8,128)(2,1)S(1)} %get-tuple-element.86.refs_0_.refs_2_), channel_id=1, source_target_pairs={{0,1},{1,0},{2,3},{3,2},{4,5},{5,4},{6,7},{7,6},{8,9},{9,8},{10,11... | collective-permute-start | bytes 3588104 | tf_op jit(solution)/shard_map/ppermute | solution.py:30
  190.9 15.5 %collective-permute-start.12 = (bf16[1168,512]{1,0:T(8,128)(2,1)S(1)}, bf16[1168,512]{1,0:T(8,128)(2,1)S(1)}, u32[]{:S(2)}, u32[]{:S(2)}) collective-permute-start(bf16[1168,512]{1,0:T(8,128)(2,1)S(1)} %get-tuple-element.87.refs_1_.refs_3_), channel_id=1, source_target_pairs={{0,1},{1,0},{2,3},{3,2},{4,5},{5,4},{6,7},{7,6},{8,9},{9,8},{10,11... | collective-permute-start | bytes 3588104 | tf_op jit(solution)/shard_map/ppermute | solution.py:30
  191.4 10.3 %collective-permute-start.8 = (bf16[1168,512]{1,0:T(8,128)(2,1)S(1)}, bf16[1168,512]{1,0:T(8,128)(2,1)S(1)}, u32[]{:S(2)}, u32[]{:S(2)}) collective-permute-start(bf16[1168,512]{1,0:T(8,128)(2,1)S(1)} %get-tuple-element.79.refs_0_.refs_3_), channel_id=1, source_target_pairs={{0,1},{1,0},{2,3},{3,2},{4,5},{5,4},{6,7},{7,6},{8,9},{9,8},{10,11... | collective-permute-start | bytes 3588104 | tf_op jit(solution)/shard_map/ppermute | solution.py:30
  191.5 10.3 %collective-permute-start.9 = (bf16[1168,512]{1,0:T(8,128)(2,1)S(1)}, bf16[1168,512]{1,0:T(8,128)(2,1)S(1)}, u32[]{:S(2)}, u32[]{:S(2)}) collective-permute-start(bf16[1168,512]{1,0:T(8,128)(2,1)S(1)} %get-tuple-element.80.refs_1_), channel_id=1, source_target_pairs={{0,1},{1,0},{2,3},{3,2},{4,5},{5,4},{6,7},{7,6},{8,9},{9,8},{10,11... | collective-permute-start | bytes 3588104 | tf_op jit(solution)/shard_map/ppermute | solution.py:30
  193.0 13.4 %collective-permute-start.14 = (bf16[384,512]{1,0:T(8,128)(2,1)S(1)}, bf16[384,512]{1,0:T(8,128)(2,1)S(1)}, u32[]{:S(2)}, u32[]{:S(2)}) collective-permute-start(bf16[384,512]{1,0:T(8,128)(2,1)S(1)} %get-tuple-element.77.refs_1_), channel_id=1, source_target_pairs={{0,16},{1,1},{2,18},{3,3},{4,20},{5,5},{6,22},{7,7},{8,24},{9,9},{... | collective-permute-start | bytes 1179656 | tf_op jit(solution)/shard_map/ppermute | solution.py:38
  203.5 24.7 %collective-permute-start.10 = (bf16[528,1024]{1,0:T(8,128)(2,1)S(1)}, bf16[528,1024]{1,0:T(8,128)(2,1)S(1)}, u32[]{:S(2)}, u32[]{:S(2)}) collective-permute-start(bf16[528,1024]{1,0:T(8,128)(2,1)S(1)} %get-tuple-element.81), channel_id=1, source_target_pairs={{0,2},{1,3},{2,0},{3,1},{4,6},{5,7},{6,4},{7,5},{8,10},{9,11},{10,... | collective-permute-start | bytes 3244040 | tf_op jit(solution)/shard_map/ppermute | solution.py:30
  208.2 24.7 %collective-permute-start.18 = (bf16[512,1024]{1,0:T(8,128)(2,1)S(1)}, bf16[512,1024]{1,0:T(8,128)(2,1)S(1)}, u32[]{:S(2)}, u32[]{:S(2)}) collective-permute-start(bf16[512,1024]{1,0:T(8,128)(2,1)S(1)} %weight_part.10.refs_4_), channel_id=1, source_target_pairs={{0,4},{4,0},{8,12},{12,8},{16,20},{20,16},{24,28},{28,24},{1,5},{5... | collective-permute-start | bytes 3145736 | tf_op jit(solution)/shard_map/ppermute | solution.py:30
  209.7 22.3 %collective-permute-start.19 = (bf16[384,512]{1,0:T(8,128)(2,1)S(1)}, bf16[384,512]{1,0:T(8,128)(2,1)S(1)}, u32[]{:S(2)}, u32[]{:S(2)}) collective-permute-start(bf16[384,512]{1,0:T(8,128)(2,1)S(1)} %get-tuple-element.83.refs_0_), channel_id=1, source_target_pairs={{0,16},{1,1},{2,18},{3,3},{4,20},{5,5},{6,22},{7,7},{8,24},{9,9},{... | collective-permute-start | bytes 1179656 | tf_op jit(solution)/shard_map/ppermute | solution.py:38
  213.5 19.4 %collective-permute-start.20 = (bf16[384,512]{1,0:T(8,128)(2,1)S(1)}, bf16[384,512]{1,0:T(8,128)(2,1)S(1)}, u32[]{:S(2)}, u32[]{:S(2)}) collective-permute-start(bf16[384,512]{1,0:T(8,128)(2,1)S(1)} %get-tuple-element.84.refs_1_), channel_id=1, source_target_pairs={{0,16},{1,1},{2,18},{3,3},{4,20},{5,5},{6,22},{7,7},{8,24},{9,9},{... | collective-permute-start | bytes 1179656 | tf_op jit(solution)/shard_map/ppermute | solution.py:38
  216.4 3.5 %slice-start = ((s8[8388608]{0:T(1024)(128)(4,1)}), s8[4194304]{0:T(1024)(128)(4,1)S(1)}, s32[]{:S(2)}) async-start(s8[8388608]{0:T(1024)(128)(4,1)} %bitcast.24), calls=%async_computation.3 | async-start | bytes 8388608
  218.2 2.3 slice-start.1
  228.2 1.4 copy-start.5
  229.9 12.8 %collective-permute-start.15 = (bf16[272,1024]{1,0:T(8,128)(2,1)S(1)}, bf16[272,1024]{1,0:T(8,128)(2,1)S(1)}, u32[]{:S(2)}, u32[]{:S(2)}) collective-permute-start(bf16[272,1024]{1,0:T(8,128)(2,1)S(1)} %get-tuple-element.89), channel_id=1, source_target_pairs={{0,4},{4,0},{8,12},{12,8},{16,20},{20,16},{24,28},{28,24},{1,5},{5... | collective-permute-start | bytes 1671176 | tf_op jit(solution)/shard_map/ppermute | solution.py:30
  233.1 10.6 %collective-permute-start.21 = (bf16[256,1024]{1,0:T(8,128)(2,1)S(1)}, bf16[256,1024]{1,0:T(8,128)(2,1)S(1)}, u32[]{:S(2)}, u32[]{:S(2)}) collective-permute-start(bf16[256,1024]{1,0:T(8,128)(2,1)S(1)} %get-tuple-element.97), channel_id=1, source_target_pairs={{0,2},{1,3},{2,0},{3,1},{4,6},{5,7},{6,4},{7,5},{8,10},{9,11},{10,... | collective-permute-start | bytes 1572872 | tf_op jit(solution)/shard_map/ppermute | solution.py:30
  242.9 12.0 %collective-permute-start.16 = (bf16[144,1024]{1,0:T(8,128)(2,1)S(1)}, bf16[144,1024]{1,0:T(8,128)(2,1)S(1)}, u32[]{:S(2)}, u32[]{:S(2)}) collective-permute-start(bf16[144,1024]{1,0:T(8,128)(2,1)S(1)} %get-tuple-element.92), channel_id=1, source_target_pairs={{0,8},{4,12},{8,0},{12,4},{16,24},{20,28},{24,16},{28,20},{1,9},{5... | collective-permute-start | bytes 884744 | tf_op jit(solution)/shard_map/ppermute | solution.py:30
  243.8 10.9 %collective-permute-start.22 = (bf16[128,1024]{1,0:T(8,128)(2,1)S(1)}, bf16[128,1024]{1,0:T(8,128)(2,1)S(1)}, u32[]{:S(2)}, u32[]{:S(2)}) collective-permute-start(bf16[128,1024]{1,0:T(8,128)(2,1)S(1)} %get-tuple-element.99), channel_id=1, source_target_pairs={{0,8},{4,12},{8,0},{12,4},{16,24},{20,28},{24,16},{28,20},{1,9},{5... | collective-permute-start | bytes 786440 | tf_op jit(solution)/shard_map/ppermute | solution.py:30
  254.8 10.6 %collective-permute-start.23 = (bf16[64,1024]{1,0:T(8,128)(2,1)S(1)}, bf16[64,1024]{1,0:T(8,128)(2,1)S(1)}, u32[]{:S(2)}, u32[]{:S(2)}) collective-permute-start(bf16[64,1024]{1,0:T(8,128)(2,1)S(1)} %get-tuple-element.101.refs_6_), channel_id=1, source_target_pairs={{0,16},{4,20},{8,24},{12,28},{16,0},{20,4},{24,8},{28,12},{1,17},{... | collective-permute-start | bytes 393224 | tf_op jit(solution)/shard_map/ppermute | solution.py:30
  254.9 12.3 %collective-permute-start.17 = (bf16[80,1024]{1,0:T(8,128)(2,1)S(1)}, bf16[80,1024]{1,0:T(8,128)(2,1)S(1)}, u32[]{:S(2)}, u32[]{:S(2)}) collective-permute-start(bf16[80,1024]{1,0:T(8,128)(2,1)S(1)} %get-tuple-element.95.refs_5_), channel_id=1, source_target_pairs={{0,16},{4,20},{8,24},{12,28},{16,0},{20,4},{24,8},{28,12},{1,17},{... | collective-permute-start | bytes 491528 | tf_op jit(solution)/shard_map/ppermute | solution.py:30
Sparse Core Ops, SparseCore 0:
  9.6 60.9 all-gather.1
